TPU v7x, 256 devices: a whole 4x4x8 slice. The times are simulated.
256 devices in a mesh: section: 8 (over x, core), fsdp: 32 (over y, z).
Axes of the slice: x: 4, y: 4, z: 8, core: 2. Of those that a mesh axis runs over, the one named last changes fastest.
Arguments:
- hidden: bfloat16 [512, 4608], P(('section', 'fsdp')), may hold values from -6 to 6
- unembed: bfloat16 [256000, 4608], P(('section', 'fsdp')), may hold values from -0.375 to 0.375
- targets: int32 [512], P(('section', 'fsdp')), may hold values from 0 to 255999
- valid_mask: int32 [512], P(('section', 'fsdp')), may hold values from 0 to 1, as said below
- loss_scale: float32 [], replicated, may hold values from 256 to 1024
Outputs:
- hidden_grad: float32 [512, 4608], P(('section', 'fsdp'))
- losses: float32 [4], replicated
Inputs may be any that keep to these rules, and one draw needn't show every extreme that they name: `valid_mask`: the first token of every microbatch is valid.
All inputs are finite; a program needn't handle non-finite values.
Results may differ from a plain program's by a relative error of at most 0.0042.
Values may be sent and summed in bfloat16 or wider, within the bound.
No kernel may reach another device: no remote copies, remote signals or barrier semaphores. Data moves between devices by JAX's collectives and lax.ppermute only.
A program may use at most 128 MiB of HBM per device.

v0:
```python
import jax
import jax.numpy as jnp
from jax import lax
from jax.sharding import PartitionSpec as P

MICRO = 4


SOFTCAP = 30.0


def in_one(arrays, axis):
    ends = [0]
    for a in arrays:
        ends.append(ends[-1] + a.size)
    so_far = lax.psum(jnp.concatenate([a.ravel() for a in arrays]), axis)
    return tuple((so_far[b:e].reshape(a.shape) for a, b, e in zip(arrays, ends, ends[1:])))


def cut_along(shard, dim, peers):
    lengths = shard.shape
    blocks = shard.reshape(*lengths[:dim], peers, lengths[dim] // peers, *lengths[dim + 1 :])
    return jnp.moveaxis(blocks, dim, 0)


def summed_on_arrival(shard, axis, dim):
    blocks = cut_along(shard, dim, lax.axis_size(axis))
    arrived = lax.all_to_all(blocks, axis, split_axis=0, concat_axis=0, tiled=True)
    return arrived.astype(jnp.float32).sum(axis=0)


def sum_at_owner(shard, axis, dim):
    peers = lax.axis_size(axis)
    blocks = lax.all_to_all(cut_along(shard, dim, peers), axis, 0, 0, tiled=True)
    return jnp.sum(blocks, axis=0)


def body(hidden, unembed, targets, valid_mask, loss_scale):
    own_rows = hidden.shape[0]
    vocab_rows = unembed.shape[0]
    width = hidden.shape[1]
    sections = lax.axis_size("section")
    groups = lax.axis_size("fsdp")
    tokens = own_rows * lax.axis_size(("section", "fsdp"))
    rows_section = tokens // sections
    tok_micro = tokens // MICRO
    labels, marks = (
        lax.all_gather(targets, ("section", "fsdp"), axis=0, tiled=True),
        lax.all_gather(valid_mask, ("section", "fsdp"), axis=0, tiled=True),
    )
    order = jnp.arange(tokens, dtype=jnp.int32) // tok_micro
    labels = jnp.roll(labels, -rows_section)
    marks = jnp.roll(marks, -rows_section)
    order = jnp.roll(order, -rows_section)
    logits = lax.dot_general(
        lax.all_gather(hidden, ("section", "fsdp"), axis=0, tiled=True),
        unembed,
        (((1,), (1,)), ((), ())),
        preferred_element_type=jnp.float32,
    )
    capped = SOFTCAP * jnp.tanh(logits / SOFTCAP)
    device_index = lax.axis_index(("section", "fsdp"))
    columns = device_index * vocab_rows + jnp.arange(vocab_rows, dtype=jnp.int32)
    hits = columns[None, :] == labels[:, None]
    total_part = jnp.sum(jnp.exp(capped - SOFTCAP), axis=1)
    picked_part = jnp.sum(jnp.where(hits, capped, jnp.zeros_like(capped)), axis=1)
    micro_ids = jnp.arange(MICRO, dtype=jnp.int32)
    member = (order[:, None] == micro_ids[None, :]).astype(jnp.float32)
    weights = marks.astype(jnp.float32)
    own_order = (device_index * own_rows + jnp.arange(own_rows, dtype=jnp.int32)) // tok_micro
    own_member = (own_order[:, None] == micro_ids[None, :]).astype(jnp.float32)
    own_counts = jnp.sum(valid_mask.astype(jnp.float32)[:, None] * own_member, axis=0)
    total, picked, counts = in_one((total_part, picked_part, own_counts), ("section", "fsdp"))
    lse = SOFTCAP + jnp.log(total)
    token_loss = weights * (lse - picked)
    losses = jnp.sum(token_loss[:, None] * member, axis=0) / counts
    coef = loss_scale * weights / jnp.sum(member * counts[None, :], axis=1)
    probs = jnp.exp(capped - lse[:, None])
    onehot = hits.astype(jnp.float32)
    grad = (coef[:, None] * (probs - onehot) * (1.0 - (capped / SOFTCAP) ** 2)).astype(jnp.bfloat16)
    partial_grad = jnp.dot(grad, unembed, preferred_element_type=jnp.float32)
    regrouped = (
        partial_grad.reshape(sections, groups, own_rows, width)
        .transpose(1, 0, 2, 3)
        .reshape(tokens, width)
    )
    by_group = summed_on_arrival(regrouped.astype(jnp.bfloat16), "fsdp", 0)
    own_grad = sum_at_owner(by_group, "section", 0)
    return (own_grad, losses)


def solution(mesh):
    return jax.shard_map(
        body,
        mesh=mesh,
        in_specs=(
            P(("section", "fsdp"), None),
            P(("section", "fsdp"), None),
            P(("section", "fsdp")),
            P(("section", "fsdp")),
            P(),
        ),
        out_specs=(P(("section", "fsdp"), None), P()),
        check_vma=False,
    )
```

profile of v0, /device:TPU:8, one launch (start us, length us, event | category | flops | bytes accessed | tf_op | source)
XLA Modules:
  0.0 378.4 jit_solution(7947519376520240688)
XLA Ops:
  7.2 0.0 all-gather.3.cloned.1.call-start
  7.2 0.7 all-gather.3.cloned.1.call-update
  7.9 0.1 slice.31
  8.0 0.7 convert_element_type.35
  8.7 0.8 dynamic-update-slice
  9.5 0.8 dynamic-update-slice.1
  10.3 79.0 %all-reduce.2 = (s32[512]{0:T(512)S(1)}, s32[512]{0:T(512)S(1)}) all-reduce(s32[512]{0:T(512)S(1)} %dynamic-update-slice.1, s32[512]{0:T(512)S(1)} %dynamic-update-slice), channel_id=1, replica_groups=mesh['section'=8,'fsdp'=32] {'section','fsdp'}, use_global_device_ids=true, to_apply=%add.1 | all-reduce | flops 1024 | bytes 8192
  89.4 0.1 slice.29
  89.4 0.1 slice.33
  90.2 0.1 pad_add_fusion
  90.3 0.1 pad_add_fusion.1
  90.3 0.1 fusion.19
  90.4 39.5 %all-gather.3.cloned.1.call-done = bf16[256,2,4608]{2,1,0:T(2,128)(2,1)} async-done(((bf16[1,2,4608]{2,1,0:T(2,128)(2,1)}), bf16[256,2,4608]{2,1,0:T(2,128)(2,1)}) %all-gather.3.cloned.1.call-update) | async-done | bytes 4718608 | tf_op jit(solution)/shard_map/all_gather | solution.py:56
  129.9 7.6 %reshape.67 = bf16[512,4608]{1,0:T(8,128)(2,1)} reshape(bf16[256,2,4608]{2,1,0:T(2,128)(2,1)} %all-gather.3.cloned.1.call-done) | data formatting | bytes 9437184
  137.5 9.4 %exponential_reduce_fusion = (f32[512]{0:T(512)S(1)}, f32[512]{0:T(512)S(1)}, f32[512,1000]{0,1:T(8,128)S(1)}) fusion(s32[512]{0:T(512)S(1)} %pad_add_fusion.1, s32[1000]{0:T(1024)S(1)} %iota_add_fusion, bf16[512,4608]{1,0:T(8,128)(2,1)} %reshape.67, bf16[1000,4608]{1,0:T(8,128)(2,1)} %param.6), kind=kOutput, calls=%fused_computation.9 | convolution fusion | flops 4722174976 | bytes 15992736 | tf_op jit(solution)/shard_map/dot_general | solution.py:55
  147.0 74.2 %psum.7 = f32[1028]{0:T(1024)S(1)} all-reduce(f32[1028]{0:T(1024)S(1)} %pad_maximum_fusion), channel_id=1, replica_groups=mesh['section'=8,'fsdp'=32] {'section','fsdp'}, use_global_device_ids=true, to_apply=%region_3.4 | all-reduce | flops 1028 | bytes 8224 | tf_op jit(solution)/shard_map/psum | solution.py:16
  221.2 0.1 fusion.16
  221.3 0.1 select_reduce_fusion
  221.4 0.1 multiply_divide_fusion
  221.5 10.9 %convolution_convert_fusion = bf16[512,4608]{1,0:T(8,128)(2,1)} fusion(bf16[1000,4608]{1,0:T(8,128)(2,1)} %param.6, f32[512,1000]{0,1:T(8,128)S(1)} %get-tuple-element.10, f32[512]{0:T(512)S(1)} %get-tuple-element.9, f32[512]{0:T(512)S(1)} %multiply_divide_fusion, s32[512]{0:T(512)S(1)} %pad_add_fusion.1, s32[1000]{0:T(1024)S(1)} %iota_add_fusion), kind=kOutput, calls=%fused_computation.1 | convolution fusion | flops 4726583296 | bytes 15992736 | tf_op jit(solution)/shard_map/dot_general | solution.py:81
  232.3 7.6 %convert_element_type.39 = bf16[8,32,2,4608]{3,2,1,0:T(2,128)(2,1)} reshape(bf16[512,4608]{1,0:T(8,128)(2,1)} %convolution_convert_fusion) | data formatting | bytes 9437184 | tf_op jit(solution)/shard_map/convert_element_type | solution.py:87
  239.9 3.1 copy.12
  243.1 2.6 copy.13
  245.7 112.4 %all_to_all.10 = bf16[32,16,4608]{2,1,0:T(8,128)(2,1)S(1)} all-to-all(bf16[32,16,4608]{2,1,0:T(8,128)(2,1)S(1)} %copy.13), channel_id=1, replica_groups=mesh['section'=8,'fsdp'=32] {'fsdp'}, dimensions={0} | all-to-all | bytes 9437184 | tf_op jit(solution)/shard_map/all_to_all | solution.py:28
  358.1 0.7 convert_reduce_fusion
  358.8 0.9 reshape.61
  359.6 3.4 all-to-all-start.1
  363.1 0.5 slice_divide_fusion
  363.6 7.3 %all-to-all-done.1 = f32[8,2,4608]{2,1,0:T(2,128)S(1)} async-done(((f32[8,2,4608]{2,1,0:T(2,128)}), f32[8,2,4608]{2,1,0:T(2,128)S(1)}, u32[]{:S(2)}, u32[]{:S(2)}) %all-to-all-start.1) | async-done | bytes 294944 | tf_op jit(solution)/shard_map/all_to_all | solution.py:34
  370.9 0.7 reduce_sum.68
  (10 shorter events, 0.0 us)
Async XLA Ops:
  7.2 122.8 %all-gather.3.cloned.1.call-start = ((), (), s32[]{:S(2)}) async-start(), calls=%async_computation.2 | async-start | bytes 4737024 | tf_op jit(solution)/shard_map/all_gather | solution.py:56
  359.6 11.2 %all-to-all-start.1 = ((f32[8,2,4608]{2,1,0:T(2,128)}), f32[8,2,4608]{2,1,0:T(2,128)S(1)}, u32[]{:S(2)}, u32[]{:S(2)}) async-start(f32[8,2,4608]{2,1,0:T(2,128)} %reshape.61), calls=%async_computation.1 | async-start | bytes 589824 | tf_op jit(solution)/shard_map/all_to_all | solution.py:34
Sparse Core Ops, SparseCore 0:
  11.7 118.2 all-gather.2
where the time goes:
time: 381 us; the launch traced here: 378 us
  blocking collectives  266 us (70%)
  waiting for transfers between devices  47.5 us (12%)
  local copies, waits for them, and re-layouts  23.7 us (6%)
  matrix products  20.3 us (5%)
  between operations  14.8 us (4%)
    all_to_all x1, blocking collectives, summed_on_arrival(): lax.all_to_all(blocks, axis, split_axis=0, concat_axis=0, tiled=True)  112 us
    unnamed x1, blocking collectives  79 us
    psum x1, blocking collectives, in_one(): so_far = lax.psum(jnp.concatenate([a.ravel() for a in arrays]), axis)  74.2 us
    all_gather x1, waiting for transfers between devices, body(): lax.all_gather(hidden, ('section', 'fsdp'), axis=0, tiled=True)  39.5 us
    convert_element_type x3, local copies, waits for them, and re-layouts, body(): by_group = summed_on_arrival(regrouped.astype(jnp.bfloat16), 'fsdp', 0)  13.3 us
    dot_general x1, matrix products, body(): partial_grad = jnp.dot(grad, unembed, preferred_element_type=jnp.float32)  10.9 us
    dot_general x1, matrix products, body(): lax.dot_general(lax.all_gather(hidden, ('section', 'fsdp'), axis=0, tiled...  9.44 us
    unnamed x5, local copies, waits for them, and re-layouts  9.27 us
  transfers between devices with their start and end apart: 2, of which 2 were waited for; matrix products, arithmetic and copies ran while one was open for 1% of the time, Pallas kernels for 0%

commit v1 on v0

v1 whole, which is shorter than its diff:
```python
import jax
import jax.numpy as jnp
from jax import lax
from jax.sharding import Mesh, PartitionSpec as P

MICRO = 4
SOFTCAP = 30.0
TAIL = 128
ALL = ("x", "core", "y", "z")


def swap(v):
    return lax.ppermute(v, "core", [(0, 1), (1, 0)])


def gather(v, axis):
    peers = lax.axis_size(axis)
    return lax.all_to_all(jnp.broadcast_to(v[None], (peers, *v.shape)), axis, 0, 0, tiled=True)


def body(hidden, unembed, targets, valid_mask, loss_scale):
    own_rows, width = hidden.shape
    vocab_rows = unembed.shape[0]
    nx, nc, ny, nz = (lax.axis_size(a) for a in ALL)
    core = lax.axis_index("core")
    plane = nx * ny * nz * own_rows
    f32 = jnp.float32

    unembed_sib = swap(unembed)

    digits = jnp.stack([targets % 256, (targets // 256) % 256, targets // 65536, valid_mask], axis=1)
    tail = jnp.pad(digits, ((0, 0), (0, TAIL - digits.shape[1]))).astype(jnp.bfloat16)
    mine = jnp.concatenate([hidden, tail], axis=1)
    by_z = gather(mine, "z").reshape(nz * own_rows, width + TAIL)
    rows = gather(by_z, ("x", "y")).reshape(plane, width + TAIL)
    tokens = rows[:, :width]

    own_tail = rows[:, width:]
    sib_tail = swap(own_tail)
    code_own = own_tail[:, :4].astype(jnp.int32)
    code_sib = sib_tail[:, :4].astype(jnp.int32)
    per_x = plane // nx
    code = jnp.where(core == 0, code_sib, jnp.roll(code_sib, -per_x, axis=0))
    labels = code[:, 0] + 256 * code[:, 1] + 65536 * code[:, 2]
    weights = code[:, 3].astype(f32)
    counts = jnp.sum((code_own[:, 3] + code_sib[:, 3]).reshape(nx, per_x), axis=1).astype(f32)
    counts_tok = jnp.repeat(jnp.where(core == 0, counts, jnp.roll(counts, -1)), per_x)

    def dot_t(u):
        return lax.dot_general(tokens, u, (((1,), (1,)), ((), ())), preferred_element_type=f32)

    device = lax.axis_index(ALL)
    device_sib = device + (1 - 2 * core) * ny * nz
    parts = []
    for u, d in ((unembed, device), (unembed_sib, device_sib)):
        capped = SOFTCAP * jnp.tanh(dot_t(u) / SOFTCAP)
        columns = d * vocab_rows + jnp.arange(vocab_rows, dtype=jnp.int32)
        hits = columns[None, :] == labels[:, None]
        parts.append((u, capped, hits))
    total = sum(jnp.sum(jnp.exp(c - SOFTCAP), axis=1) for _, c, _ in parts)
    picked = sum(jnp.sum(jnp.where(h, c, jnp.zeros_like(c)), axis=1) for _, c, h in parts)
    stats = jnp.stack([total, picked]).reshape(2 * plane // 128, 128)
    stats = jnp.sum(gather(stats, ("x", "y")).reshape(nx * ny, *stats.shape), axis=0)
    stats = jnp.sum(gather(stats, "z").reshape(nz, *stats.shape), axis=0)
    total, picked = stats.reshape(2, plane)

    lse = SOFTCAP + jnp.log(total)
    sums = jnp.sum((weights * (lse - picked)).reshape(nx, per_x), axis=1)
    sums = jnp.where(core == 0, sums, jnp.roll(sums, 1))
    losses = (sums + swap(sums)) / counts
    coef = loss_scale * weights / counts_tok

    partial = jnp.zeros((plane, width), f32)
    for u, capped, hits in parts:
        probs = jnp.exp(capped - lse[:, None])
        grad = coef[:, None] * (probs - hits.astype(f32)) * (1.0 - (capped / SOFTCAP) ** 2)
        partial = partial + jnp.dot(grad.astype(jnp.bfloat16), u, preferred_element_type=f32)

    cut = partial.astype(jnp.bfloat16).reshape(nx * ny, plane // (nx * ny), width)
    got = lax.all_to_all(cut, ("x", "y"), 0, 0, tiled=True)
    some = jnp.sum(got.astype(f32), axis=0)
    cut = some.astype(jnp.bfloat16).reshape(nz, own_rows, width)
    got = lax.all_to_all(cut, "z", 0, 0, tiled=True)
    return jnp.sum(got.astype(f32), axis=0), losses


def solution(mesh):
    sections, groups = mesh.devices.shape
    chips = Mesh(mesh.devices.reshape(sections // 2, 2, 4, groups // 4), ALL)
    return jax.shard_map(
        body,
        mesh=chips,
        in_specs=(P(ALL, None), P(ALL, None), P(ALL), P(ALL), P()),
        out_specs=(P(ALL, None), P()),
        check_vma=False,
    )
```

time: 381 us -> 167 us (0.44)
  blocking collectives: 266 us -> 18.4 us
  waiting for transfers between devices: 47.5 us -> 80.9 us
  starting transfers between devices: 3.46 us -> 24.8 us
  local copies, waits for them, and re-layouts: 23.7 us -> 5.24 us
  between operations: 14.8 us -> 1.45 us
  matrix products: 20.3 us -> 30.2 us
    all_to_all x1, blocking collectives: 112 us -> 18.4 us  [gather(): lax.all_to_all(jnp.broadcast_to(v[None], (peers, *v.shape)), axis, 0, 0,...]
    unnamed x1 -> x0, blocking collectives: 79 us -> none
    psum x1 -> x0, blocking collectives: 74.2 us -> none  [in_one(): so_far = lax.psum(jnp.concatenate([a.ravel() for a in arrays]), axis)]
    all_to_all x1 -> x5, waiting for transfers between devices: 7.29 us -> 79.8 us  [the longest x3 44.1 us: gather(): lax.all_to_all(jnp.broadcast_to(v[None], (peers, *v.shape)), axis, 0, 0,...]
    all_gather x1 -> x0, waiting for transfers between devices: 39.5 us -> none  [body(): lax.all_gather(hidden, ('section', 'fsdp'), axis=0, tiled=True)]
    all_to_all x1 -> x5, starting transfers between devices: 3.42 us -> 24.7 us  [the longest x3 16.3 us: gather(): lax.all_to_all(jnp.broadcast_to(v[None], (peers, *v.shape)), axis, 0, 0,...]
    convert_element_type x3 -> x1, local copies, waits for them, and re-layouts: 13.3 us -> 0.08 us  [body(): weights = code[:, 3].astype(f32)]
    dot_general x2 -> x4, matrix products: 20.3 us -> 30.2 us  [the longest x2 15.2 us: body(): jnp.dot(grad.astype(jnp.bfloat16), u, preferred_element_type=f32)]
  transfers between devices with their start and end apart: 2 -> 8, of which waited for: 2 -> 6; matrix products, arithmetic and copies ran while one was open for 1% -> 9% of each run, Pallas kernels for 0% -> 0%
where the time goes in v1:
time: 167 us; the launch traced here: 166 us
  waiting for transfers between devices  80.9 us (48%)
  matrix products  30.2 us (18%)
  starting transfers between devices  24.8 us (15%)
  blocking collectives  18.4 us (11%)
  local copies, waits for them, and re-layouts  5.24 us (3%)
  other arithmetic  4.92 us (3%)
    all_to_all x3, waiting for transfers between devices, gather(): lax.all_to_all(jnp.broadcast_to(v[None], (peers, *v.shape)), axis, 0, 0,...  44.1 us
    all_to_all x1, waiting for transfers between devices, body(): got = lax.all_to_all(cut, ('x', 'y'), 0, 0, tiled=True)  28.9 us
    all_to_all x1, blocking collectives, gather(): lax.all_to_all(jnp.broadcast_to(v[None], (peers, *v.shape)), axis, 0, 0,...  18.4 us
    all_to_all x3, starting transfers between devices, gather(): lax.all_to_all(jnp.broadcast_to(v[None], (peers, *v.shape)), axis, 0, 0,...  16.3 us
    dot_general x2, matrix products, body(): jnp.dot(grad.astype(jnp.bfloat16), u, preferred_element_type=f32)  15.2 us
    dot_general x2, matrix products, dot_t(): lax.dot_general(tokens, u, (((1,), (1,)), ((), ())), preferred_element_ty...  15 us
    all_to_all x1, waiting for transfers between devices, body(): got = lax.all_to_all(cut, 'z', 0, 0, tiled=True)  6.78 us
    all_to_all x1, starting transfers between devices, body(): got = lax.all_to_all(cut, ('x', 'y'), 0, 0, tiled=True)  4.98 us
  transfers between devices with their start and end apart: 8, of which 6 were waited for; matrix products, arithmetic and copies ran while one was open for 9% of the time, Pallas kernels for 0%

profile of v1, /device:TPU:8, one launch (start us, length us, event | category | flops | bytes accessed | tf_op | source)
XLA Modules:
  0.0 166.0 jit_solution(4000197391727560708)
XLA Ops:
  0.6 0.1 collective-permute-start.1
  0.7 0.7 fusion.50
  1.4 0.1 copy.58
  1.6 0.7 fusion.48
  2.3 0.1 broadcast_in_dim.14
  2.4 18.4 %all_to_all.30 = bf16[8,2,4736]{2,1,0:T(2,128)(2,1)S(1)} all-to-all(bf16[8,2,4736]{2,1,0:T(2,128)(2,1)S(1)} %broadcast_in_dim.14), channel_id=1, replica_groups=mesh['x'=4,'core'=2,'y'=4,'z'=8] {'z'}, dimensions={0} | all-to-all | bytes 303104 | tf_op jit(solution)/shard_map/all_to_all | solution.py:18
  20.8 0.1 broadcast_in_dim.15
  20.9 1.6 broadcast_in_dim.16
  22.5 7.4 %all-to-all-start.1 = ((bf16[16,16,4736]{2,1,0:T(8,128)(2,1)}), bf16[16,16,4736]{2,1,0:T(8,128)(2,1)S(1)}, u32[]{:S(2)}, u32[]{:S(2)}) async-start(bf16[16,16,4736]{2,1,0:T(8,128)(2,1)} %broadcast_in_dim.16), calls=%async_computation.1 | async-start | bytes 4849664 | tf_op jit(solution)/shard_map/all_to_all | solution.py:18
  30.5 30.9 %all-to-all-done.1 = bf16[16,16,4736]{2,1,0:T(8,128)(2,1)S(1)} async-done(((bf16[16,16,4736]{2,1,0:T(8,128)(2,1)}), bf16[16,16,4736]{2,1,0:T(8,128)(2,1)S(1)}, u32[]{:S(2)}, u32[]{:S(2)}) %all-to-all-start.1) | async-done | bytes 2424864 | tf_op jit(solution)/shard_map/all_to_all | solution.py:18
  61.4 0.0 collective-permute-start
  61.4 7.2 %fusion.14 = f32[256,1000]{0,1:T(8,128)} fusion(bf16[1000,4608]{1,0:T(8,128)(2,1)} %param.6, bf16[256,4736]{1,0:T(8,128)(2,1)S(1)} %bitcast.21), kind=kOutput, calls=%fused_computation.9 | convolution fusion | flops 2359552000 | bytes 12599296 | tf_op jit(solution)/shard_map/dot_general | solution.py:50
  68.6 0.0 collective-permute-done
  68.7 0.2 fusion.45
  68.9 0.1 add.121
  69.0 0.1 reduce_sum.93
  69.1 0.1 slice.67
  69.2 0.1 copy.54
  69.3 0.1 copy.55
  69.3 0.1 pad_add_fusion
  69.4 0.2 copy.47
  69.6 0.2 fusion.43
  69.8 0.0 collective-permute-done.1
  69.8 7.8 %exponential_reduce_fusion = (f32[256]{0:T(256)S(1)}, f32[256]{0:T(256)S(1)}, f32[256]{0:T(256)S(1)}, f32[256]{0:T(256)S(1)}, f32[256,1000]{0,1:T(8,128)}) fusion(s32[256]{0:T(256)S(1)} %fusion.43, s32[1000]{0:T(1024)S(1)} %get-tuple-element.17, s32[1000]{0:T(1024)S(1)} %get-tuple-element.18, f32[256,1000]{0,1:T(8,128)} %fusion.14, ...), kind=kOutput, calls=%fused_computation.24 | convolution fusion | flops 2362622976 | bytes 13636608 | tf_op jit(solution)/shard_map/dot_general | solution.py:50
  77.7 0.6 broadcast_in_dim.19
  78.3 5.4 %all-to-all-start.2 = ((f32[16,4,128]{2,1,0:T(4,128)}), f32[16,4,128]{2,1,0:T(4,128)S(1)}, u32[]{:S(2)}, u32[]{:S(2)}) async-start(f32[16,4,128]{2,1,0:T(4,128)} %broadcast_in_dim.19), calls=%async_computation.2 | async-start | bytes 65536 | tf_op jit(solution)/shard_map/all_to_all | solution.py:18
  83.7 0.1 broadcast_select_fusion.2
  83.8 0.1 broadcast_in_dim.17
  83.9 0.1 reshape.92
  84.0 5.9 %all-to-all-done.2 = f32[16,4,128]{2,1,0:T(4,128)S(1)} async-done(((f32[16,4,128]{2,1,0:T(4,128)}), f32[16,4,128]{2,1,0:T(4,128)S(1)}, u32[]{:S(2)}, u32[]{:S(2)}) %all-to-all-start.2) | async-done | bytes 32800 | tf_op jit(solution)/shard_map/all_to_all | solution.py:18
  90.0 0.6 broadcast_in_dim.20
  90.6 3.5 %all-to-all-start.3 = ((f32[8,4,128]{2,1,0:T(4,128)}), f32[8,4,128]{2,1,0:T(4,128)S(1)}, u32[]{:S(2)}, u32[]{:S(2)}) async-start(f32[8,4,128]{2,1,0:T(4,128)} %broadcast_in_dim.20), calls=%async_computation.3 | async-start | bytes 32768 | tf_op jit(solution)/shard_map/all_to_all | solution.py:18
  94.1 0.2 fusion.47
  94.3 7.3 %all-to-all-done.3 = f32[8,4,128]{2,1,0:T(4,128)S(1)} async-done(((f32[8,4,128]{2,1,0:T(4,128)}), f32[8,4,128]{2,1,0:T(4,128)S(1)}, u32[]{:S(2)}, u32[]{:S(2)}) %all-to-all-start.3) | async-done | bytes 16416 | tf_op jit(solution)/shard_map/all_to_all | solution.py:18
  101.7 0.0 copy-start
  101.7 7.1 %fusion.28 = f32[256,4608]{1,0:T(8,128)S(1)} fusion(bf16[1000,4608]{1,0:T(8,128)(2,1)} %param.6, f32[256,1000]{0,1:T(8,128)} %fusion.14, f32[256]{0:T(256)S(1)} %get-tuple-element.9, s32[256]{0:T(256)S(1)} %fusion.43, f32[256]{0:T(256)S(1)} %get-tuple-element.7, s32[1000]{0:T(1024)S(1)} %get-tuple-element.18), kind=kOutput, calls=%fused_computation.26 | convolution fusion | flops 2361856000 | bytes 14965664 | tf_op jit(solution)/shard_map/dot_general | solution.py:77
  108.7 0.0 copy-done
  108.7 8.2 %fusion = bf16[256,4608]{1,0:T(8,128)(2,1)} fusion(f32[256,4608]{1,0:T(8,128)S(1)} %fusion.28, bf16[1000,4608]{1,0:T(8,128)(2,1)} %collective-permute-done.1, f32[256,1000]{0,1:T(8,128)S(1)} %copy-done, f32[256]{0:T(256)S(1)} %get-tuple-element.9, s32[256]{0:T(256)S(1)} %fusion.43, f32[256]{0:T(256)S(1)} %get-tuple-element.7, s32[1000]{0:T(1024)S(1)} %get-tuple-element.17), kind=kOutput, calls=%fused_computation.1 | convolution fusion | flops 2364215296 | bytes 17324960 | tf_op jit(solution)/shard_map/dot_general | solution.py:77
  116.9 5.0 %all-to-all-start.4 = ((bf16[16,16,4608]{2,1,0:T(8,128)(2,1)}), bf16[16,16,4608]{2,1,0:T(8,128)(2,1)S(1)}, u32[]{:S(2)}, u32[]{:S(2)}) async-start(bf16[16,16,4608]{2,1,0:T(8,128)(2,1)} %bitcast.8), calls=%async_computation.4 | async-start | bytes 4718592 | tf_op jit(solution)/shard_map/all_to_all | solution.py:80
  121.9 0.1 convert_element_type.49
  122.0 0.1 sub.66
  122.1 0.1 multiply_reduce_fusion
  122.2 0.6 slice.73
  122.8 28.9 %all-to-all-done.4 = bf16[16,16,4608]{2,1,0:T(8,128)(2,1)S(1)} async-done(((bf16[16,16,4608]{2,1,0:T(8,128)(2,1)}), bf16[16,16,4608]{2,1,0:T(8,128)(2,1)S(1)}, u32[]{:S(2)}, u32[]{:S(2)}) %all-to-all-start.4) | async-done | bytes 2359328 | tf_op jit(solution)/shard_map/all_to_all | solution.py:80
  151.7 0.3 reduce_sum.100
  152.0 0.7 reshape.91
  152.7 3.4 %all-to-all-start.5 = ((bf16[8,2,4608]{2,1,0:T(2,128)(2,1)}), bf16[8,2,4608]{2,1,0:T(2,128)(2,1)S(1)}, u32[]{:S(2)}, u32[]{:S(2)}) async-start(bf16[8,2,4608]{2,1,0:T(2,128)(2,1)} %reshape.91), calls=%async_computation.5 | async-start | bytes 294912 | tf_op jit(solution)/shard_map/all_to_all | solution.py:83
  156.1 0.7 broadcast_select_fusion.1
  156.8 0.0 collective-permute-start.2
  156.9 1.1 collective-permute-done.2
  158.0 0.5 add_divide_fusion
  158.5 6.8 %all-to-all-done.5 = bf16[8,2,4608]{2,1,0:T(2,128)(2,1)S(1)} async-done(((bf16[8,2,4608]{2,1,0:T(2,128)(2,1)}), bf16[8,2,4608]{2,1,0:T(2,128)(2,1)S(1)}, u32[]{:S(2)}, u32[]{:S(2)}) %all-to-all-start.5) | async-done | bytes 147488 | tf_op jit(solution)/shard_map/all_to_all | solution.py:83
  165.3 0.7 convert_reduce_fusion
  (15 shorter events, 0.2 us)
Async XLA Ops:
  0.6 69.2 %collective-permute-start.1 = (bf16[1000,4608]{1,0:T(8,128)(2,1)}, bf16[1000,4608]{1,0:T(8,128)(2,1)}, u32[]{:S(2)}, u32[]{:S(2)}) collective-permute-start(bf16[1000,4608]{1,0:T(8,128)(2,1)} %param.6), channel_id=1, source_target_pairs={{0,32},{32,0},{1,33},{33,1},{2,34},{34,2},{3,35},{35,3},{4,36},{36... | collective-permute-start | bytes 27648008 | tf_op jit(solution)/shard_map/ppermute | solution.py:13
  22.5 39.0 %all-to-all-start.1 = ((bf16[16,16,4736]{2,1,0:T(8,128)(2,1)}), bf16[16,16,4736]{2,1,0:T(8,128)(2,1)S(1)}, u32[]{:S(2)}, u32[]{:S(2)}) async-start(bf16[16,16,4736]{2,1,0:T(8,128)(2,1)} %broadcast_in_dim.16), calls=%async_computation.1 | async-start | bytes 4849664 | tf_op jit(solution)/shard_map/all_to_all | solution.py:18
  61.4 7.2 %collective-permute-start = (bf16[256,128]{1,0:T(8,128)(2,1)S(1)}, bf16[256,128]{1,0:T(8,128)(2,1)S(1)}, u32[]{:S(2)}, u32[]{:S(2)}) collective-permute-start(bf16[256,128]{1,0:T(8,128)(2,1)S(1)} %slice.75), channel_id=1, source_target_pairs={{0,32},{32,0},{1,33},{33,1},{2,34},{34,2},{3,35},{35,3},{4,36},{36... | collective-permute-start | bytes 196616 | tf_op jit(solution)/shard_map/ppermute | solution.py:13
  78.3 11.7 %all-to-all-start.2 = ((f32[16,4,128]{2,1,0:T(4,128)}), f32[16,4,128]{2,1,0:T(4,128)S(1)}, u32[]{:S(2)}, u32[]{:S(2)}) async-start(f32[16,4,128]{2,1,0:T(4,128)} %broadcast_in_dim.19), calls=%async_computation.2 | async-start | bytes 65536 | tf_op jit(solution)/shard_map/all_to_all | solution.py:18
  90.6 11.0 %all-to-all-start.3 = ((f32[8,4,128]{2,1,0:T(4,128)}), f32[8,4,128]{2,1,0:T(4,128)S(1)}, u32[]{:S(2)}, u32[]{:S(2)}) async-start(f32[8,4,128]{2,1,0:T(4,128)} %broadcast_in_dim.20), calls=%async_computation.3 | async-start | bytes 32768 | tf_op jit(solution)/shard_map/all_to_all | solution.py:18
  101.7 7.1 %copy-start = (f32[256,1000]{0,1:T(8,128)S(1)}, f32[256,1000]{0,1:T(8,128)}, u32[]{:S(2)}) copy-start(f32[256,1000]{0,1:T(8,128)} %get-tuple-element.15) | copy-start | bytes 3072004
  116.9 34.8 %all-to-all-start.4 = ((bf16[16,16,4608]{2,1,0:T(8,128)(2,1)}), bf16[16,16,4608]{2,1,0:T(8,128)(2,1)S(1)}, u32[]{:S(2)}, u32[]{:S(2)}) async-start(bf16[16,16,4608]{2,1,0:T(8,128)(2,1)} %bitcast.8), calls=%async_computation.4 | async-start | bytes 4718592 | tf_op jit(solution)/shard_map/all_to_all | solution.py:80
  152.7 12.6 %all-to-all-start.5 = ((bf16[8,2,4608]{2,1,0:T(2,128)(2,1)}), bf16[8,2,4608]{2,1,0:T(2,128)(2,1)S(1)}, u32[]{:S(2)}, u32[]{:S(2)}) async-start(bf16[8,2,4608]{2,1,0:T(2,128)(2,1)} %reshape.91), calls=%async_computation.5 | async-start | bytes 294912 | tf_op jit(solution)/shard_map/all_to_all | solution.py:83
  156.8 1.1 collective-permute-start.2

commit v2 on v1

v2 whole, which is shorter than its diff:
```python
import functools

import jax
import jax.numpy as jnp
from jax import lax
from jax.experimental import pallas as pl
from jax.experimental.pallas import tpu as pltpu
from jax.sharding import Mesh, PartitionSpec as P

SOFTCAP = 30.0
TAIL = 128
ALL = ("x", "core", "y", "z")
VMEM_BYTES = 52 * 1024 * 1024


def shifted(v, axis, by):
    n = lax.axis_size(axis)
    return lax.ppermute(v, axis, [(i, (i + by) % n) for i in range(n)])


def gather(v, axis):
    peers = lax.axis_size(axis)
    return lax.all_to_all(jnp.broadcast_to(v[None], (peers, *v.shape)), axis, 0, 0, tiled=True)


def column_chunk(width):
    return next(c for c in (1152, 128) if width % (2 * c) == 0)


def logits_kernel(n, chunk, where_ref, labels_ref, *refs):
    late = refs[:n]
    early = refs[n : 2 * n]
    own_ref, sib_ref, stats_ref, own_out, sib_out, tok, acc = refs[2 * n :]
    step = pl.program_id(0)
    half = late[0].shape[1]
    rows = late[0].shape[0] // n
    steps = 2 * half // chunk
    vocab = own_ref.shape[0]

    @pl.when(step == 0)
    def _():
        for e in range(n):
            for d in range(n):
                at = pl.multiple_of(where_ref[e * n + d] * rows, rows)
                tok[pl.ds(at, rows), half:] = late[e][d * rows : (d + 1) * rows, :]
                tok[pl.ds(at, rows), :half] = early[d][e * rows : (e + 1) * rows, :]

    def add(u_ref, k):
        columns = tok[:, pl.ds(pl.multiple_of(k * chunk, 128), chunk)]
        part = lax.dot_general(u_ref[...], columns, (((1,), (1,)), ((), ())), preferred_element_type=jnp.float32)

        @pl.when(k == 0)
        def _():
            acc[...] = part

        @pl.when(k > 0)
        def _():
            acc[...] += part

    def finish(base, out, first):
        capped = SOFTCAP * jnp.tanh(acc[...] / SOFTCAP)
        ids = base + lax.broadcasted_iota(jnp.int32, capped.shape, 0)
        hits = ids == labels_ref[...]
        exps = jnp.exp(capped - SOFTCAP)
        total = jnp.sum(exps, axis=0, keepdims=True)
        picked = jnp.sum(jnp.where(hits, capped, 0.0), axis=0, keepdims=True)
        new = jnp.concatenate([total, picked, jnp.zeros((6, total.shape[1]), jnp.float32)], axis=0)
        stats_ref[...] = new if first else stats_ref[...] + new
        terms = exps * (1.0 - (capped / SOFTCAP) ** 2)
        out[...] = terms.T

    @pl.when(step < steps)
    def _():
        add(own_ref, step)

    @pl.when(step == steps - 1)
    def _():
        finish(where_ref[n * n], own_out, True)

    @pl.when(step >= steps)
    def _():
        add(sib_ref, step - steps)

    @pl.when(step == 2 * steps - 1)
    def _():
        finish(where_ref[n * n + 1], sib_out, False)


def logits_and_terms(where, labels, late, early, own, sib):
    n = len(late)
    vocab, width = own.shape
    plane = n * late[0].shape[0]
    chunk = column_chunk(width)
    steps = width // chunk
    whole = lambda a: pl.BlockSpec(a.shape, lambda i: (0, 0))
    terms = jax.ShapeDtypeStruct((plane, vocab), jnp.float32)
    stats = jax.ShapeDtypeStruct((8, plane), jnp.float32)
    return pl.pallas_call(
        functools.partial(logits_kernel, n, chunk),
        grid=(2 * steps,),
        out_shape=(stats, terms, terms),
        in_specs=[pl.BlockSpec(memory_space=pltpu.SMEM), whole(labels)]
        + [whole(a) for a in (*late, *early)]
        + [
            pl.BlockSpec((vocab, chunk), lambda i: (0, jnp.minimum(i, steps - 1))),
            pl.BlockSpec((vocab, chunk), lambda i: (0, jnp.maximum(i - steps, 0))),
        ],
        out_specs=(whole(stats), whole(terms), whole(terms)),
        scratch_shapes=[pltpu.VMEM((plane, width), jnp.bfloat16), pltpu.VMEM((vocab, plane), jnp.float32)],
        compiler_params=pltpu.CompilerParams(vmem_limit_bytes=VMEM_BYTES),
        cost_estimate=pl.CostEstimate(
            flops=4 * plane * vocab * width, bytes_accessed=4 * vocab * width + 4 * plane * width, transcendentals=0
        ),
    )(where, labels, *late, *early, own, sib)


def gradient_kernel(n, where_ref, rows_ref, own_t, sib_t, own_ref, sib_ref, *refs):
    outs = refs[:n]
    own_p, sib_p, columns = refs[n:]
    plane, vocab = own_t.shape
    rows = plane // (n * n)

    @pl.when(pl.program_id(0) == 0)
    def _():
        columns[...] = rows_ref[...].T
        for i in range(n * n):
            at = pl.ds(pl.multiple_of(where_ref[i] * rows, rows), rows)
            to = slice(i * rows, (i + 1) * rows)
            known = columns[at, :]
            fix, scale, labels = known[:, 0:1], known[:, 1:2], known[:, 2:3].astype(jnp.int32)
            for terms, out, base in ((own_t, own_p, where_ref[n * n]), (sib_t, sib_p, where_ref[n * n + 1])):
                ids = base + lax.broadcasted_iota(jnp.int32, (rows, vocab), 1)
                out[to, :] = jnp.where(ids == labels, fix, scale * terms[at, :]).astype(jnp.bfloat16)

    part = jnp.dot(own_p[...], own_ref[...], preferred_element_type=jnp.float32)
    part = part + jnp.dot(sib_p[...], sib_ref[...], preferred_element_type=jnp.float32)
    part = part.astype(jnp.bfloat16)
    for i in range(n):
        outs[i][...] = part[i * n * rows : (i + 1) * n * rows, :]


def gradient_half(n, where, rows, own_t, sib_t, own, sib, second):
    plane, vocab = own_t.shape
    half = own.shape[1] // 2
    chunk = 768 if half % 768 == 0 else 128
    steps = half // chunk
    skip = steps if second else 0
    whole = lambda a: pl.BlockSpec(a.shape, lambda i: (0, 0))
    block = pl.BlockSpec((vocab, chunk), lambda i: (0, i + skip))
    piece = jax.ShapeDtypeStruct((plane // n, half), jnp.bfloat16)
    return pl.pallas_call(
        functools.partial(gradient_kernel, n),
        grid=(steps,),
        out_shape=(piece,) * n,
        in_specs=[pl.BlockSpec(memory_space=pltpu.SMEM), whole(rows), whole(own_t), whole(sib_t), block, block],
        out_specs=(pl.BlockSpec((plane // n, chunk), lambda i: (0, i)),) * n,
        scratch_shapes=[
            pltpu.VMEM((plane, vocab), jnp.bfloat16),
            pltpu.VMEM((plane, vocab), jnp.bfloat16),
            pltpu.VMEM((plane, 8), jnp.float32),
        ],
        compiler_params=pltpu.CompilerParams(vmem_limit_bytes=VMEM_BYTES),
        cost_estimate=pl.CostEstimate(
            flops=4 * plane * vocab * half, bytes_accessed=4 * vocab * half + 2 * plane * half, transcendentals=0
        ),
    )(where, rows, own_t, sib_t, own, sib)


def summed(pieces):
    return sum(p.astype(jnp.float32) for p in pieces).astype(jnp.bfloat16)


def body(hidden, unembed, targets, valid_mask, loss_scale):
    own_rows, width = hidden.shape
    vocab = unembed.shape[0]
    nx, _, ny, nz = (lax.axis_size(a) for a in ALL)
    n = nx
    ix, core, iy, iz = (lax.axis_index(a) for a in ALL)
    plane = nx * ny * nz * own_rows
    per_x = plane // nx
    half = width // 2
    f32, i32 = jnp.float32, jnp.int32

    unembed_sib = lax.ppermute(unembed, "core", [(0, 1), (1, 0)])

    digits = jnp.stack([targets % 256, (targets // 256) % 256, targets // 65536, valid_mask], axis=1)
    tail = jnp.pad(digits, ((0, 0), (0, TAIL - digits.shape[1]))).astype(jnp.bfloat16)
    by_z = gather(jnp.concatenate([hidden, tail], axis=1), "z").reshape(nz * own_rows, width + TAIL)

    tail_own = by_z[:, width:]
    tail_sib = lax.ppermute(tail_own, "core", [(0, 1), (1, 0)])
    first, second = by_z[:, :half], by_z[:, half:width]
    along_x = jnp.concatenate([first] + [shifted(first, "x", e) for e in range(1, n)])
    along_y = jnp.concatenate([second] + [shifted(second, "y", d) for d in range(1, n)])
    early = [along_x] + [shifted(along_x, "y", d) for d in range(1, n)]
    late = [along_y] + [shifted(along_y, "x", e) for e in range(1, n)]

    codes = gather(jnp.stack([tail_own[:, :4], tail_sib[:, :4]]).astype(f32).reshape(1, -1), ("x", "y"))
    codes = codes.reshape(nx * ny, 2, nz * own_rows, 4).astype(i32).transpose(1, 3, 0, 2).reshape(2, 4, plane)
    code = jnp.where(core == 0, codes[1], jnp.roll(codes[1], -per_x, axis=1))
    labels = code[0] + 256 * code[1] + 65536 * code[2]
    weights = code[3].astype(f32)
    counts = jnp.sum((codes[0, 3] + codes[1, 3]).reshape(nx, per_x), axis=1).astype(f32)
    counts_tok = jnp.repeat(jnp.where(core == 0, counts, jnp.roll(counts, -1)), per_x)

    device = lax.axis_index(ALL)
    bases = vocab * jnp.stack([device, device + (1 - 2 * core) * ny * nz])
    near_x, near_y = (ix - jnp.arange(nx)) % nx, (iy - jnp.arange(ny)) % ny
    places = near_x[:, None] * ny + near_y[None, :]
    where_xy = jnp.concatenate([places.ravel(), bases]).astype(i32)
    where_yx = jnp.concatenate([places.T.ravel(), bases]).astype(i32)

    stats, own_t, sib_t = logits_and_terms(where_xy, labels[None], late, early, unembed, unembed_sib)
    stats = gather(stats[:2].reshape(2 * plane // 128, 128), ("x", "y", "z"))
    stats = jnp.sum(stats.reshape(nx * ny * nz, 2 * plane // 128, 128), axis=0)
    total, picked = stats.reshape(2, plane)
    coef = loss_scale * weights / counts_tok
    lse = SOFTCAP + jnp.log(total)
    fix = coef * (jnp.exp(picked - lse) - 1.0) * (1.0 - (picked / SOFTCAP) ** 2)
    rows = jnp.stack([fix, coef / total, labels.astype(f32)] + [jnp.zeros_like(fix)] * 5)

    to_x = gradient_half(n, where_xy, rows, own_t, sib_t, unembed, unembed_sib, True)
    to_y = gradient_half(n, where_yx, rows, own_t, sib_t, unembed, unembed_sib, False)
    got_x = [to_x[0]] + [shifted(to_x[e], "x", -e) for e in range(1, n)]
    got_y = [to_y[0]] + [shifted(to_y[d], "y", -d) for d in range(1, n)]

    sums = jnp.sum((weights * (lse - picked)).reshape(nx, per_x), axis=1)
    sums = jnp.where(core == 0, sums, jnp.roll(sums, 1))
    losses = (sums + lax.ppermute(sums, "core", [(0, 1), (1, 0)])) / counts

    part_x, part_y = summed(got_x), summed(got_y)
    cut = lambda v, i: v[i * nz * own_rows : (i + 1) * nz * own_rows]
    got_y = [cut(part_x, 0)] + [shifted(cut(part_x, d), "y", -d) for d in range(1, n)]
    got_x = [cut(part_y, 0)] + [shifted(cut(part_y, e), "x", -e) for e in range(1, n)]
    part = jnp.concatenate([summed(got_x), summed(got_y)], axis=1).reshape(nz, own_rows, width)
    got = lax.all_to_all(part, "z", 0, 0, tiled=True)
    return jnp.sum(got.astype(f32), axis=0), losses


def solution(mesh):
    sections, groups = mesh.devices.shape
    chips = Mesh(mesh.devices.reshape(sections // 2, 2, 4, groups // 4), ALL)
    return jax.shard_map(
        body,
        mesh=chips,
        in_specs=(P(ALL, None), P(ALL, None), P(ALL), P(ALL), P()),
        out_specs=(P(ALL, None), P()),
        check_vma=False,
    )
```

time: 167 us -> 163 us (0.976)
  starting transfers between devices: 24.8 us -> 66.3 us
  matrix products: 30.2 us -> 0 us
  waiting for transfers between devices: 80.9 us -> 51.7 us
  Pallas kernels: 0 us -> 29.2 us
  blocking collectives: 18.4 us -> 0 us
    ppermute x3 -> x27, starting transfers between devices: 0.13 us -> 42.2 us  [the longest x24 41.9 us: shifted(): return lax.ppermute(v, axis, [(i, (i + by) % n) for i in range(n)])]
    dot_general x4 -> x0, matrix products: 30.2 us -> none  [the longest x2 15.2 us: body(): jnp.dot(grad.astype(jnp.bfloat16), u, preferred_element_type=f32)]
    pallas_call x0 -> x3, Pallas kernels: none -> 29.2 us  [the longest x1 15.2 us: logits_and_terms(): pl.pallas_call(functools.partial(logits_kernel, n, chunk), grid=(2 * step...]
    all_to_all x2 -> x1, waiting for transfers between devices: 35.7 us -> 6.78 us  [body(): got = lax.all_to_all(part, 'z', 0, 0, tiled=True)]
    all_to_all x3, waiting for transfers between devices: 44.1 us -> 24.2 us  [gather(): lax.all_to_all(jnp.broadcast_to(v[None], (peers, *v.shape)), axis, 0, 0,...]
    ppermute x3 -> x27, waiting for transfers between devices: 1.11 us -> 20.7 us  [the longest x24 19.6 us: shifted(): return lax.ppermute(v, axis, [(i, (i + by) % n) for i in range(n)])]
    all_to_all x1 -> x0, blocking collectives: 18.4 us -> none  [gather(): lax.all_to_all(jnp.broadcast_to(v[None], (peers, *v.shape)), axis, 0, 0,...]
    all_to_all x2 -> x1, starting transfers between devices: 8.35 us -> 3.38 us  [body(): got = lax.all_to_all(part, 'z', 0, 0, tiled=True)]
  transfers between devices with their start and end apart: 8 -> 31, of which waited for: 6 -> 13; matrix products, arithmetic and copies ran while one was open for 9% -> 6% of each run, Pallas kernels for 0% -> 4%
where the time goes in v2:
time: 163 us; the launch traced here: 162 us
  starting transfers between devices  66.3 us (41%)
  waiting for transfers between devices  51.7 us (32%)
  Pallas kernels  29.2 us (18%)
  local copies, waits for them, and re-layouts  6.58 us (4%)
  other arithmetic  6.29 us (4%)
    ppermute x24, starting transfers between devices, shifted(): return lax.ppermute(v, axis, [(i, (i + by) % n) for i in range(n)])  41.9 us
    all_to_all x3, waiting for transfers between devices, gather(): lax.all_to_all(jnp.broadcast_to(v[None], (peers, *v.shape)), axis, 0, 0,...  24.2 us
    all_to_all x3, starting transfers between devices, gather(): lax.all_to_all(jnp.broadcast_to(v[None], (peers, *v.shape)), axis, 0, 0,...  20.8 us
    ppermute x24, waiting for transfers between devices, shifted(): return lax.ppermute(v, axis, [(i, (i + by) % n) for i in range(n)])  19.6 us
    pallas_call x1, Pallas kernels, logits_and_terms(): pl.pallas_call(functools.partial(logits_kernel, n, chunk), grid=(2 * step...  15.2 us
    pallas_call x2, Pallas kernels, gradient_half(): pl.pallas_call(functools.partial(gradient_kernel, n), grid=(steps,), out_...  14 us
    all_to_all x1, waiting for transfers between devices, body(): got = lax.all_to_all(part, 'z', 0, 0, tiled=True)  6.78 us
    all_to_all x1, starting transfers between devices, body(): got = lax.all_to_all(part, 'z', 0, 0, tiled=True)  3.38 us
  transfers between devices with their start and end apart: 31, of which 13 were waited for; matrix products, arithmetic and copies ran while one was open for 6% of the time, Pallas kernels for 4%

profile of v2, /device:TPU:8, one launch (start us, length us, event | category | flops | bytes accessed | tf_op | source)
XLA Modules:
  0.0 161.7 jit_solution(13953679083906671457)
XLA Ops:
  0.7 0.7 fusion.8
  1.6 0.7 fusion
  2.3 0.7 broadcast_in_dim.10
  3.0 8.5 %all-to-all-start = ((bf16[8,2,4736]{2,1,0:T(2,128)(2,1)}), bf16[8,2,4736]{2,1,0:T(2,128)(2,1)S(1)}, u32[]{:S(2)}, u32[]{:S(2)}) async-start(bf16[8,2,4736]{2,1,0:T(2,128)(2,1)} %broadcast_in_dim.10), calls=%async_computation | async-start | bytes 303104 | tf_op jit(solution)/shard_map/all_to_all | solution.py:23
  11.8 9.8 %all-to-all-done = bf16[8,2,4736]{2,1,0:T(2,128)(2,1)S(1)} async-done(((bf16[8,2,4736]{2,1,0:T(2,128)(2,1)}), bf16[8,2,4736]{2,1,0:T(2,128)(2,1)S(1)}, u32[]{:S(2)}, u32[]{:S(2)}) %all-to-all-start) | async-done | bytes 151584 | tf_op jit(solution)/shard_map/all_to_all | solution.py:23
  21.9 0.5 collective-permute-start.3
  22.4 2.6 %collective-permute-start.2 = (bf16[16,2304]{1,0:T(8,128)(2,1)S(1)}, bf16[16,2304]{1,0:T(8,128)(2,1)S(1)}, u32[]{:S(2)}, u32[]{:S(2)}) collective-permute-start(bf16[16,2304]{1,0:T(8,128)(2,1)S(1)} %get-tuple-element.33), channel_id=1, source_target_pairs={{0,16},{8,24},{16,0},{24,8},{1,17},{9,25},{17,1},{25,9},{2,18},{10... | collective-permute-start | bytes 221192 | tf_op jit(solution)/shard_map/ppermute | solution.py:18
  25.0 1.9 %collective-permute-start.1 = (bf16[16,2304]{1,0:T(8,128)(2,1)S(1)}, bf16[16,2304]{1,0:T(8,128)(2,1)S(1)}, u32[]{:S(2)}, u32[]{:S(2)}) collective-permute-start(bf16[16,2304]{1,0:T(8,128)(2,1)S(1)} %get-tuple-element.33), channel_id=1, source_target_pairs={{0,8},{8,16},{16,24},{24,0},{1,9},{9,17},{17,25},{25,1},{2,10},{10... | collective-permute-start | bytes 221192 | tf_op jit(solution)/shard_map/ppermute | solution.py:18
  27.2 0.1 reshape.163
  27.3 0.6 broadcast_in_dim.11
  27.9 6.2 %all-to-all-start.1 = ((f32[16,1,128]{2,1,0:T(1,128)}), f32[16,1,128]{2,1,0:T(1,128)S(1)}, u32[]{:S(2)}, u32[]{:S(2)}) async-start(f32[16,1,128]{2,1,0:T(1,128)} %broadcast_in_dim.11), calls=%async_computation.1 | async-start | bytes 16384 | tf_op jit(solution)/shard_map/all_to_all | solution.py:23
  34.1 2.7 %collective-permute-start.9 = (bf16[16,2304]{1,0:T(8,128)(2,1)S(1)}, bf16[16,2304]{1,0:T(8,128)(2,1)S(1)}, u32[]{:S(2)}, u32[]{:S(2)}) collective-permute-start(bf16[16,2304]{1,0:T(8,128)(2,1)S(1)} %get-tuple-element.32), channel_id=1, source_target_pairs={{0,192},{64,0},{128,64},{192,128},{1,193},{65,1},{129,65},{193,129... | collective-permute-start | bytes 221192 | tf_op jit(solution)/shard_map/ppermute | solution.py:18
  36.8 3.3 %all-to-all-done.1 = f32[16,1,128]{2,1,0:T(1,128)S(1)} async-done(((f32[16,1,128]{2,1,0:T(1,128)}), f32[16,1,128]{2,1,0:T(1,128)S(1)}, u32[]{:S(2)}, u32[]{:S(2)}) %all-to-all-start.1) | async-done | bytes 8224 | tf_op jit(solution)/shard_map/all_to_all | solution.py:23
  40.5 1.2 collective-permute-start.8
  41.8 0.8 collective-permute-start.7
  42.6 1.5 collective-permute-start.4
  44.2 2.4 %collective-permute-start.5 = (bf16[64,2304]{1,0:T(8,128)(2,1)S(1)}, bf16[64,2304]{1,0:T(8,128)(2,1)S(1)}, u32[]{:S(2)}, u32[]{:S(2)}) collective-permute-start(bf16[64,2304]{1,0:T(8,128)(2,1)S(1)} %pad_maximum_fusion.refs_0_), channel_id=1, source_target_pairs={{0,128},{64,192},{128,0},{192,64},{1,129},{65,193},{129,1},{193,65... | collective-permute-start | bytes 884744 | tf_op jit(solution)/shard_map/ppermute | solution.py:18
  46.6 0.6 collective-permute-done.8
  47.2 0.8 collective-permute-start.6
  48.0 0.5 collective-permute-done.7
  48.5 0.7 collective-permute-start.10
  49.2 5.3 %collective-permute-done.4.refs_1_ = bf16[64,2304]{1,0:T(8,128)(2,1)S(1)} collective-permute-done((bf16[64,2304]{1,0:T(8,128)(2,1)S(1)}, bf16[64,2304]{1,0:T(8,128)(2,1)S(1)}, u32[]{:S(2)}, u32[]{:S(2)}) %collective-permute-start.4) | collective-permute-done | bytes 294944 | tf_op jit(solution)/shard_map/ppermute | solution.py:18
  54.5 1.5 collective-permute-start.11
  55.9 3.1 %collective-permute-done.5.refs_2_ = bf16[64,2304]{1,0:T(8,128)(2,1)S(1)} collective-permute-done((bf16[64,2304]{1,0:T(8,128)(2,1)S(1)}, bf16[64,2304]{1,0:T(8,128)(2,1)S(1)}, u32[]{:S(2)}, u32[]{:S(2)}) %collective-permute-start.5) | collective-permute-done | bytes 294944 | tf_op jit(solution)/shard_map/ppermute | solution.py:18
  59.0 1.5 collective-permute-start.12
  60.6 5.2 %collective-permute-done.11.refs_6_ = bf16[64,2304]{1,0:T(8,128)(2,1)S(1)} collective-permute-done((bf16[64,2304]{1,0:T(8,128)(2,1)S(1)}, bf16[64,2304]{1,0:T(8,128)(2,1)S(1)}, u32[]{:S(2)}, u32[]{:S(2)}) %collective-permute-start.11) | collective-permute-done | bytes 294944 | tf_op jit(solution)/shard_map/ppermute | solution.py:18
  65.8 3.0 %collective-permute-done.12.refs_7_ = bf16[64,2304]{1,0:T(8,128)(2,1)S(1)} collective-permute-done((bf16[64,2304]{1,0:T(8,128)(2,1)S(1)}, bf16[64,2304]{1,0:T(8,128)(2,1)S(1)}, u32[]{:S(2)}, u32[]{:S(2)}) %collective-permute-start.12) | collective-permute-done | bytes 294944 | tf_op jit(solution)/shard_map/ppermute | solution.py:18
  68.8 0.7 copy-done.1
  69.5 15.2 %shard_map.68 = (f32[8,256]{1,0:T(8,128)S(1)}, f32[256,1000]{1,0:T(8,128)}, f32[256,1000]{1,0:T(8,128)}) custom-call(s32[18]{0:T(128)S(1)} %get-tuple-element.43.where_ref, s32[1,256]{1,0:T(1,128)S(1)} %get-tuple-element.25.labels_ref, bf16[64,2304]{1,0:T(8,128)(2,1)S(1)} %pad_maximum_fusion.refs_0_, bf16[64,2304]{1,0:T(8,128)(2,1)S(1)} %collective-permute-done.4.refs_1_, ...), custom_call_target="tpu_custom_call" | custom-call | flops 4718592000 | bytes 23150592 | tf_op jit(solution)/shard_map/pallas_call | solution.py:98
  84.7 0.7 broadcast_in_dim.28
  85.5 6.2 %all-to-all-start.2 = ((f32[128,4,128]{2,1,0:T(4,128)}), f32[128,4,128]{2,1,0:T(4,128)S(1)}, u32[]{:S(2)}, u32[]{:S(2)}) async-start(f32[128,4,128]{2,1,0:T(4,128)} %broadcast_in_dim.28), calls=%async_computation.2 | async-start | bytes 524288 | tf_op jit(solution)/shard_map/all_to_all | solution.py:23
  92.6 0.1 reduce_sum.36
  92.8 0.1 broadcast_select_fusion.1
  93.1 11.0 %all-to-all-done.2 = f32[128,4,128]{2,1,0:T(4,128)S(1)} async-done(((f32[128,4,128]{2,1,0:T(4,128)}), f32[128,4,128]{2,1,0:T(4,128)S(1)}, u32[]{:S(2)}, u32[]{:S(2)}) %all-to-all-start.2) | async-done | bytes 262176 | tf_op jit(solution)/shard_map/all_to_all | solution.py:23
  104.1 0.1 reduce_sum.37
  104.2 0.6 add_subtract_fusion
  104.9 7.0 %shard_map.70 = (bf16[64,2304]{1,0:T(8,128)(2,1)S(1)}, bf16[64,2304]{1,0:T(8,128)(2,1)S(1)}, bf16[64,2304]{1,0:T(8,128)(2,1)S(1)}, bf16[64,2304]{1,0:T(8,128)(2,1)S(1)}) custom-call(s32[18]{0:T(128)S(1)} %get-tuple-element.43.where_ref, f32[8,256]{1,0:T(8,128)S(1)} %stack.59.rows_ref, f32[256,1000]{1,0:T(8,128)} %get-tuple-element.14.own_t, ...), custom_call_target="tpu_custom_call" | custom-call | flops 2359296000 | bytes 10395648 | tf_op jit(solution)/shard_map/pallas_call | solution.py:151
  111.9 0.6 collective-permute-start.22
  112.5 1.7 %collective-permute-start.21 = (bf16[64,2304]{1,0:T(8,128)(2,1)S(1)}, bf16[64,2304]{1,0:T(8,128)(2,1)S(1)}, u32[]{:S(2)}, u32[]{:S(2)}) collective-permute-start(bf16[64,2304]{1,0:T(8,128)(2,1)S(1)} %get-tuple-element.22), channel_id=1, source_target_pairs={{0,128},{64,192},{128,0},{192,64},{1,129},{65,193},{129,1},{193,65... | collective-permute-start | bytes 884744 | tf_op jit(solution)/shard_map/ppermute | solution.py:18
  114.2 2.0 %collective-permute-start.20 = (bf16[64,2304]{1,0:T(8,128)(2,1)S(1)}, bf16[64,2304]{1,0:T(8,128)(2,1)}, u32[]{:S(2)}, u32[]{:S(2)}) collective-permute-start(bf16[64,2304]{1,0:T(8,128)(2,1)S(1)} %get-tuple-element.21), channel_id=1, source_target_pairs={{0,192},{64,0},{128,64},{192,128},{1,193},{65,1},{129,65},{193,129... | collective-permute-start | bytes 884744 | tf_op jit(solution)/shard_map/ppermute | solution.py:18
  116.2 7.0 %shard_map.69 = (bf16[64,2304]{1,0:T(8,128)(2,1)S(1)}, bf16[64,2304]{1,0:T(8,128)(2,1)S(1)}, bf16[64,2304]{1,0:T(8,128)(2,1)S(1)}, bf16[64,2304]{1,0:T(8,128)(2,1)S(1)}) custom-call(s32[18]{0:T(128)S(1)} %get-tuple-element.42.where_ref, f32[8,256]{1,0:T(8,128)S(1)} %stack.59.rows_ref, f32[256,1000]{1,0:T(8,128)} %get-tuple-element.14.own_t, ...), custom_call_target="tpu_custom_call" | custom-call | flops 2359296000 | bytes 10395648 | tf_op jit(solution)/shard_map/pallas_call | solution.py:151
  123.2 0.6 collective-permute-start.16
  123.8 2.9 %collective-permute-start.15 = (bf16[64,2304]{1,0:T(8,128)(2,1)S(1)}, bf16[64,2304]{1,0:T(8,128)(2,1)S(1)}, u32[]{:S(2)}, u32[]{:S(2)}) collective-permute-start(bf16[64,2304]{1,0:T(8,128)(2,1)S(1)} %get-tuple-element.18), channel_id=1, source_target_pairs={{0,16},{8,24},{16,0},{24,8},{1,17},{9,25},{17,1},{25,9},{2,18},{10... | collective-permute-start | bytes 884744 | tf_op jit(solution)/shard_map/ppermute | solution.py:18
  126.7 0.8 sub.75
  127.5 0.1 multiply_reduce_fusion
  127.6 0.6 slice.117
  128.2 0.5 collective-permute-start.14
  128.7 1.1 add_convert_fusion
  129.9 1.8 %collective-permute-start.25 = (bf16[16,2304]{1,0:T(8,128)(2,1)S(1)}, bf16[16,2304]{1,0:T(8,128)(2,1)S(1)}, u32[]{:S(2)}, u32[]{:S(2)}) collective-permute-start(bf16[16,2304]{1,0:T(8,128)(2,1)S(1)} %get-tuple-element.30), channel_id=1, source_target_pairs={{0,8},{8,16},{16,24},{24,0},{1,9},{9,17},{17,25},{25,1},{2,10},{10... | collective-permute-start | bytes 221192 | tf_op jit(solution)/shard_map/ppermute | solution.py:18
  131.7 1.9 %collective-permute-start.24 = (bf16[16,2304]{1,0:T(8,128)(2,1)S(1)}, bf16[16,2304]{1,0:T(8,128)(2,1)S(1)}, u32[]{:S(2)}, u32[]{:S(2)}) collective-permute-start(bf16[16,2304]{1,0:T(8,128)(2,1)S(1)} %get-tuple-element.31), channel_id=1, source_target_pairs={{0,16},{8,24},{16,0},{24,8},{1,17},{9,25},{17,1},{25,9},{2,18},{10... | collective-permute-start | bytes 221192 | tf_op jit(solution)/shard_map/ppermute | solution.py:18
  133.5 5.7 %collective-permute-start.23 = (bf16[16,2304]{1,0:T(8,128)(2,1)S(1)}, bf16[16,2304]{1,0:T(8,128)(2,1)S(1)}, u32[]{:S(2)}, u32[]{:S(2)}) collective-permute-start(bf16[16,2304]{1,0:T(8,128)(2,1)S(1)} %get-tuple-element.29), channel_id=1, source_target_pairs={{0,24},{8,0},{16,8},{24,16},{1,25},{9,1},{17,9},{25,17},{2,26},{10... | collective-permute-start | bytes 221192 | tf_op jit(solution)/shard_map/ppermute | solution.py:18
  139.3 0.1 add_convert_fusion.1
  139.5 1.7 %collective-permute-start.19 = (bf16[16,2304]{1,0:T(8,128)(2,1)S(1)}, bf16[16,2304]{1,0:T(8,128)(2,1)S(1)}, u32[]{:S(2)}, u32[]{:S(2)}) collective-permute-start(bf16[16,2304]{1,0:T(8,128)(2,1)S(1)} %get-tuple-element.27), channel_id=1, source_target_pairs={{0,64},{64,128},{128,192},{192,0},{1,65},{65,129},{129,193},{193,1... | collective-permute-start | bytes 221192 | tf_op jit(solution)/shard_map/ppermute | solution.py:18
  141.2 1.9 %collective-permute-start.18 = (bf16[16,2304]{1,0:T(8,128)(2,1)S(1)}, bf16[16,2304]{1,0:T(8,128)(2,1)S(1)}, u32[]{:S(2)}, u32[]{:S(2)}) collective-permute-start(bf16[16,2304]{1,0:T(8,128)(2,1)S(1)} %get-tuple-element.28), channel_id=1, source_target_pairs={{0,128},{64,192},{128,0},{192,64},{1,129},{65,193},{129,1},{193,65... | collective-permute-start | bytes 221192 | tf_op jit(solution)/shard_map/ppermute | solution.py:18
  143.1 2.5 %collective-permute-start.17 = (bf16[16,2304]{1,0:T(8,128)(2,1)S(1)}, bf16[16,2304]{1,0:T(8,128)(2,1)S(1)}, u32[]{:S(2)}, u32[]{:S(2)}) collective-permute-start(bf16[16,2304]{1,0:T(8,128)(2,1)S(1)} %get-tuple-element.26), channel_id=1, source_target_pairs={{0,192},{64,0},{128,64},{192,128},{1,193},{65,1},{129,65},{193,129... | collective-permute-start | bytes 221192 | tf_op jit(solution)/shard_map/ppermute | solution.py:18
  145.7 1.4 collective-permute-done.18
  147.0 0.5 collective-permute-done.17
  147.7 0.7 reshape.162
  148.4 3.4 %all-to-all-start.3 = ((bf16[8,2,4608]{2,1,0:T(2,128)(2,1)}), bf16[8,2,4608]{2,1,0:T(2,128)(2,1)S(1)}, u32[]{:S(2)}, u32[]{:S(2)}) async-start(bf16[8,2,4608]{2,1,0:T(2,128)(2,1)} %reshape.162), calls=%async_computation.3 | async-start | bytes 294912 | tf_op jit(solution)/shard_map/all_to_all | solution.py:236
  151.8 0.7 broadcast_select_fusion
  152.5 1.1 collective-permute-done.26
  153.6 0.5 add_divide_fusion
  154.1 6.8 %all-to-all-done.3 = bf16[8,2,4608]{2,1,0:T(2,128)(2,1)S(1)} async-done(((bf16[8,2,4608]{2,1,0:T(2,128)(2,1)}), bf16[8,2,4608]{2,1,0:T(2,128)(2,1)S(1)}, u32[]{:S(2)}, u32[]{:S(2)}) %all-to-all-start.3) | async-done | bytes 147488 | tf_op jit(solution)/shard_map/all_to_all | solution.py:236
  160.9 0.7 convert_reduce_fusion
  (71 shorter events, 2.5 us)
Async XLA Ops:
  0.6 68.2 %collective-permute-start.13 = (bf16[1000,4608]{1,0:T(8,128)(2,1)}, bf16[1000,4608]{1,0:T(8,128)(2,1)}, u32[]{:S(2)}, u32[]{:S(2)}) collective-permute-start(bf16[1000,4608]{1,0:T(8,128)(2,1)} %own_ref.3), channel_id=1, source_target_pairs={{0,32},{32,0},{1,33},{33,1},{2,34},{34,2},{3,35},{35,3},{4,36},{36... | collective-permute-start | bytes 27648008 | tf_op jit(solution)/shard_map/ppermute | solution.py:184
  3.0 18.6 %all-to-all-start = ((bf16[8,2,4736]{2,1,0:T(2,128)(2,1)}), bf16[8,2,4736]{2,1,0:T(2,128)(2,1)S(1)}, u32[]{:S(2)}, u32[]{:S(2)}) async-start(bf16[8,2,4736]{2,1,0:T(2,128)(2,1)} %broadcast_in_dim.10), calls=%async_computation | async-start | bytes 303104 | tf_op jit(solution)/shard_map/all_to_all | solution.py:23
  21.7 5.2 %collective-permute-start = (bf16[16,128]{1,0:T(8,128)(2,1)S(1)}, bf16[16,128]{1,0:T(8,128)(2,1)S(1)}, u32[]{:S(2)}, u32[]{:S(2)}) collective-permute-start(bf16[16,128]{1,0:T(8,128)(2,1)S(1)} %slice.120), channel_id=1, source_target_pairs={{0,32},{32,0},{1,33},{33,1},{2,34},{34,2},{3,35},{35,3},{4,36},{36... | collective-permute-start | bytes 12296 | tf_op jit(solution)/shard_map/ppermute | solution.py:191
  21.9 18.7 %collective-permute-start.3 = (bf16[16,2304]{1,0:T(8,128)(2,1)S(1)}, bf16[16,2304]{1,0:T(8,128)(2,1)S(1)}, u32[]{:S(2)}, u32[]{:S(2)}) collective-permute-start(bf16[16,2304]{1,0:T(8,128)(2,1)S(1)} %get-tuple-element.33), channel_id=1, source_target_pairs={{0,24},{8,0},{16,8},{24,16},{1,25},{9,1},{17,9},{25,17},{2,26},{10... | collective-permute-start | bytes 221192 | tf_op jit(solution)/shard_map/ppermute | solution.py:18
  22.4 19.4 %collective-permute-start.2 = (bf16[16,2304]{1,0:T(8,128)(2,1)S(1)}, bf16[16,2304]{1,0:T(8,128)(2,1)S(1)}, u32[]{:S(2)}, u32[]{:S(2)}) collective-permute-start(bf16[16,2304]{1,0:T(8,128)(2,1)S(1)} %get-tuple-element.33), channel_id=1, source_target_pairs={{0,16},{8,24},{16,0},{24,8},{1,17},{9,25},{17,1},{25,9},{2,18},{10... | collective-permute-start | bytes 221192 | tf_op jit(solution)/shard_map/ppermute | solution.py:18
  25.0 17.6 %collective-permute-start.1 = (bf16[16,2304]{1,0:T(8,128)(2,1)S(1)}, bf16[16,2304]{1,0:T(8,128)(2,1)S(1)}, u32[]{:S(2)}, u32[]{:S(2)}) collective-permute-start(bf16[16,2304]{1,0:T(8,128)(2,1)S(1)} %get-tuple-element.33), channel_id=1, source_target_pairs={{0,8},{8,16},{16,24},{24,0},{1,9},{9,17},{17,25},{25,1},{2,10},{10... | collective-permute-start | bytes 221192 | tf_op jit(solution)/shard_map/ppermute | solution.py:18
  27.9 12.3 %all-to-all-start.1 = ((f32[16,1,128]{2,1,0:T(1,128)}), f32[16,1,128]{2,1,0:T(1,128)S(1)}, u32[]{:S(2)}, u32[]{:S(2)}) async-start(f32[16,1,128]{2,1,0:T(1,128)} %broadcast_in_dim.11), calls=%async_computation.1 | async-start | bytes 16384 | tf_op jit(solution)/shard_map/all_to_all | solution.py:23
  34.1 10.1 %collective-permute-start.9 = (bf16[16,2304]{1,0:T(8,128)(2,1)S(1)}, bf16[16,2304]{1,0:T(8,128)(2,1)S(1)}, u32[]{:S(2)}, u32[]{:S(2)}) collective-permute-start(bf16[16,2304]{1,0:T(8,128)(2,1)S(1)} %get-tuple-element.32), channel_id=1, source_target_pairs={{0,192},{64,0},{128,64},{192,128},{1,193},{65,1},{129,65},{193,129... | collective-permute-start | bytes 221192 | tf_op jit(solution)/shard_map/ppermute | solution.py:18
  40.5 6.7 %collective-permute-start.8 = (bf16[16,2304]{1,0:T(8,128)(2,1)S(1)}, bf16[16,2304]{1,0:T(8,128)(2,1)S(1)}, u32[]{:S(2)}, u32[]{:S(2)}) collective-permute-start(bf16[16,2304]{1,0:T(8,128)(2,1)S(1)} %get-tuple-element.32), channel_id=1, source_target_pairs={{0,128},{64,192},{128,0},{192,64},{1,129},{65,193},{129,1},{193,65... | collective-permute-start | bytes 221192 | tf_op jit(solution)/shard_map/ppermute | solution.py:18
  41.8 6.8 %collective-permute-start.7 = (bf16[16,2304]{1,0:T(8,128)(2,1)S(1)}, bf16[16,2304]{1,0:T(8,128)(2,1)S(1)}, u32[]{:S(2)}, u32[]{:S(2)}) collective-permute-start(bf16[16,2304]{1,0:T(8,128)(2,1)S(1)} %get-tuple-element.32), channel_id=1, source_target_pairs={{0,64},{64,128},{128,192},{192,0},{1,65},{65,129},{129,193},{193,1... | collective-permute-start | bytes 221192 | tf_op jit(solution)/shard_map/ppermute | solution.py:18
  42.6 11.8 %collective-permute-start.4 = (bf16[64,2304]{1,0:T(8,128)(2,1)S(1)}, bf16[64,2304]{1,0:T(8,128)(2,1)S(1)}, u32[]{:S(2)}, u32[]{:S(2)}) collective-permute-start(bf16[64,2304]{1,0:T(8,128)(2,1)S(1)} %pad_maximum_fusion.refs_0_), channel_id=1, source_target_pairs={{0,64},{64,128},{128,192},{192,0},{1,65},{65,129},{129,193},{193,1... | collective-permute-start | bytes 884744 | tf_op jit(solution)/shard_map/ppermute | solution.py:18
  44.2 14.8 %collective-permute-start.5 = (bf16[64,2304]{1,0:T(8,128)(2,1)S(1)}, bf16[64,2304]{1,0:T(8,128)(2,1)S(1)}, u32[]{:S(2)}, u32[]{:S(2)}) collective-permute-start(bf16[64,2304]{1,0:T(8,128)(2,1)S(1)} %pad_maximum_fusion.refs_0_), channel_id=1, source_target_pairs={{0,128},{64,192},{128,0},{192,64},{1,129},{65,193},{129,1},{193,65... | collective-permute-start | bytes 884744 | tf_op jit(solution)/shard_map/ppermute | solution.py:18
  47.2 13.4 %collective-permute-start.6 = (bf16[64,2304]{1,0:T(8,128)(2,1)S(1)}, bf16[64,2304]{1,0:T(8,128)(2,1)S(1)}, u32[]{:S(2)}, u32[]{:S(2)}) collective-permute-start(bf16[64,2304]{1,0:T(8,128)(2,1)S(1)} %pad_maximum_fusion.refs_0_), channel_id=1, source_target_pairs={{0,192},{64,0},{128,64},{192,128},{1,193},{65,1},{129,65},{193,129... | collective-permute-start | bytes 884744 | tf_op jit(solution)/shard_map/ppermute | solution.py:18
  48.5 12.0 %collective-permute-start.10 = (bf16[64,2304]{1,0:T(8,128)(2,1)S(1)}, bf16[64,2304]{1,0:T(8,128)(2,1)S(1)}, u32[]{:S(2)}, u32[]{:S(2)}) collective-permute-start(bf16[64,2304]{1,0:T(8,128)(2,1)S(1)} %pad_maximum_fusion.1.refs_4_), channel_id=1, source_target_pairs={{0,8},{8,16},{16,24},{24,0},{1,9},{9,17},{17,25},{25,1},{2,10},{10... | collective-permute-start | bytes 884744 | tf_op jit(solution)/shard_map/ppermute | solution.py:18
  54.5 11.3 %collective-permute-start.11 = (bf16[64,2304]{1,0:T(8,128)(2,1)S(1)}, bf16[64,2304]{1,0:T(8,128)(2,1)S(1)}, u32[]{:S(2)}, u32[]{:S(2)}) collective-permute-start(bf16[64,2304]{1,0:T(8,128)(2,1)S(1)} %pad_maximum_fusion.1.refs_4_), channel_id=1, source_target_pairs={{0,16},{8,24},{16,0},{24,8},{1,17},{9,25},{17,1},{25,9},{2,18},{10... | collective-permute-start | bytes 884744 | tf_op jit(solution)/shard_map/ppermute | solution.py:18
  59.0 9.8 %collective-permute-start.12 = (bf16[64,2304]{1,0:T(8,128)(2,1)S(1)}, bf16[64,2304]{1,0:T(8,128)(2,1)S(1)}, u32[]{:S(2)}, u32[]{:S(2)}) collective-permute-start(bf16[64,2304]{1,0:T(8,128)(2,1)S(1)} %pad_maximum_fusion.1.refs_4_), channel_id=1, source_target_pairs={{0,24},{8,0},{16,8},{24,16},{1,25},{9,1},{17,9},{25,17},{2,26},{10... | collective-permute-start | bytes 884744 | tf_op jit(solution)/shard_map/ppermute | solution.py:18
  65.8 3.0 %copy-start = (bf16[64,2304]{1,0:T(8,128)(2,1)}, bf16[64,2304]{1,0:T(8,128)(2,1)S(1)}, u32[]{:S(2)}) copy-start(bf16[64,2304]{1,0:T(8,128)(2,1)S(1)} %collective-permute-done.11.refs_6_) | copy-start | bytes 884740
  68.8 0.7 copy-start.1
  85.5 18.6 %all-to-all-start.2 = ((f32[128,4,128]{2,1,0:T(4,128)}), f32[128,4,128]{2,1,0:T(4,128)S(1)}, u32[]{:S(2)}, u32[]{:S(2)}) async-start(f32[128,4,128]{2,1,0:T(4,128)} %broadcast_in_dim.28), calls=%async_computation.2 | async-start | bytes 524288 | tf_op jit(solution)/shard_map/all_to_all | solution.py:23
  111.9 16.3 %collective-permute-start.22 = (bf16[64,2304]{1,0:T(8,128)(2,1)S(1)}, bf16[64,2304]{1,0:T(8,128)(2,1)S(1)}, u32[]{:S(2)}, u32[]{:S(2)}) collective-permute-start(bf16[64,2304]{1,0:T(8,128)(2,1)S(1)} %get-tuple-element.23), channel_id=1, source_target_pairs={{0,64},{64,128},{128,192},{192,0},{1,65},{65,129},{129,193},{193,1... | collective-permute-start | bytes 884744 | tf_op jit(solution)/shard_map/ppermute | solution.py:18
  112.5 16.2 %collective-permute-start.21 = (bf16[64,2304]{1,0:T(8,128)(2,1)S(1)}, bf16[64,2304]{1,0:T(8,128)(2,1)S(1)}, u32[]{:S(2)}, u32[]{:S(2)}) collective-permute-start(bf16[64,2304]{1,0:T(8,128)(2,1)S(1)} %get-tuple-element.22), channel_id=1, source_target_pairs={{0,128},{64,192},{128,0},{192,64},{1,129},{65,193},{129,1},{193,65... | collective-permute-start | bytes 884744 | tf_op jit(solution)/shard_map/ppermute | solution.py:18
  114.2 14.6 %collective-permute-start.20 = (bf16[64,2304]{1,0:T(8,128)(2,1)S(1)}, bf16[64,2304]{1,0:T(8,128)(2,1)}, u32[]{:S(2)}, u32[]{:S(2)}) collective-permute-start(bf16[64,2304]{1,0:T(8,128)(2,1)S(1)} %get-tuple-element.21), channel_id=1, source_target_pairs={{0,192},{64,0},{128,64},{192,128},{1,193},{65,1},{129,65},{193,129... | collective-permute-start | bytes 884744 | tf_op jit(solution)/shard_map/ppermute | solution.py:18
  123.2 10.3 %collective-permute-start.16 = (bf16[64,2304]{1,0:T(8,128)(2,1)S(1)}, bf16[64,2304]{1,0:T(8,128)(2,1)S(1)}, u32[]{:S(2)}, u32[]{:S(2)}) collective-permute-start(bf16[64,2304]{1,0:T(8,128)(2,1)S(1)} %get-tuple-element.19), channel_id=1, source_target_pairs={{0,8},{8,16},{16,24},{24,0},{1,9},{9,17},{17,25},{25,1},{2,10},{10... | collective-permute-start | bytes 884744 | tf_op jit(solution)/shard_map/ppermute | solution.py:18
  123.8 15.5 %collective-permute-start.15 = (bf16[64,2304]{1,0:T(8,128)(2,1)S(1)}, bf16[64,2304]{1,0:T(8,128)(2,1)S(1)}, u32[]{:S(2)}, u32[]{:S(2)}) collective-permute-start(bf16[64,2304]{1,0:T(8,128)(2,1)S(1)} %get-tuple-element.18), channel_id=1, source_target_pairs={{0,16},{8,24},{16,0},{24,8},{1,17},{9,25},{17,1},{25,9},{2,18},{10... | collective-permute-start | bytes 884744 | tf_op jit(solution)/shard_map/ppermute | solution.py:18
  128.2 11.1 %collective-permute-start.14 = (bf16[64,2304]{1,0:T(8,128)(2,1)S(1)}, bf16[64,2304]{1,0:T(8,128)(2,1)S(1)}, u32[]{:S(2)}, u32[]{:S(2)}) collective-permute-start(bf16[64,2304]{1,0:T(8,128)(2,1)S(1)} %get-tuple-element.17), channel_id=1, source_target_pairs={{0,24},{8,0},{16,8},{24,16},{1,25},{9,1},{17,9},{25,17},{2,26},{10... | collective-permute-start | bytes 884744 | tf_op jit(solution)/shard_map/ppermute | solution.py:18
  129.9 13.2 %collective-permute-start.25 = (bf16[16,2304]{1,0:T(8,128)(2,1)S(1)}, bf16[16,2304]{1,0:T(8,128)(2,1)S(1)}, u32[]{:S(2)}, u32[]{:S(2)}) collective-permute-start(bf16[16,2304]{1,0:T(8,128)(2,1)S(1)} %get-tuple-element.30), channel_id=1, source_target_pairs={{0,8},{8,16},{16,24},{24,0},{1,9},{9,17},{17,25},{25,1},{2,10},{10... | collective-permute-start | bytes 221192 | tf_op jit(solution)/shard_map/ppermute | solution.py:18
  131.7 13.9 %collective-permute-start.24 = (bf16[16,2304]{1,0:T(8,128)(2,1)S(1)}, bf16[16,2304]{1,0:T(8,128)(2,1)S(1)}, u32[]{:S(2)}, u32[]{:S(2)}) collective-permute-start(bf16[16,2304]{1,0:T(8,128)(2,1)S(1)} %get-tuple-element.31), channel_id=1, source_target_pairs={{0,16},{8,24},{16,0},{24,8},{1,17},{9,25},{17,1},{25,9},{2,18},{10... | collective-permute-start | bytes 221192 | tf_op jit(solution)/shard_map/ppermute | solution.py:18
  133.5 12.1 %collective-permute-start.23 = (bf16[16,2304]{1,0:T(8,128)(2,1)S(1)}, bf16[16,2304]{1,0:T(8,128)(2,1)S(1)}, u32[]{:S(2)}, u32[]{:S(2)}) collective-permute-start(bf16[16,2304]{1,0:T(8,128)(2,1)S(1)} %get-tuple-element.29), channel_id=1, source_target_pairs={{0,24},{8,0},{16,8},{24,16},{1,25},{9,1},{17,9},{25,17},{2,26},{10... | collective-permute-start | bytes 221192 | tf_op jit(solution)/shard_map/ppermute | solution.py:18
  139.5 6.2 %collective-permute-start.19 = (bf16[16,2304]{1,0:T(8,128)(2,1)S(1)}, bf16[16,2304]{1,0:T(8,128)(2,1)S(1)}, u32[]{:S(2)}, u32[]{:S(2)}) collective-permute-start(bf16[16,2304]{1,0:T(8,128)(2,1)S(1)} %get-tuple-element.27), channel_id=1, source_target_pairs={{0,64},{64,128},{128,192},{192,0},{1,65},{65,129},{129,193},{193,1... | collective-permute-start | bytes 221192 | tf_op jit(solution)/shard_map/ppermute | solution.py:18
  141.2 5.9 %collective-permute-start.18 = (bf16[16,2304]{1,0:T(8,128)(2,1)S(1)}, bf16[16,2304]{1,0:T(8,128)(2,1)S(1)}, u32[]{:S(2)}, u32[]{:S(2)}) collective-permute-start(bf16[16,2304]{1,0:T(8,128)(2,1)S(1)} %get-tuple-element.28), channel_id=1, source_target_pairs={{0,128},{64,192},{128,0},{192,64},{1,129},{65,193},{129,1},{193,65... | collective-permute-start | bytes 221192 | tf_op jit(solution)/shard_map/ppermute | solution.py:18
  143.1 4.5 %collective-permute-start.17 = (bf16[16,2304]{1,0:T(8,128)(2,1)S(1)}, bf16[16,2304]{1,0:T(8,128)(2,1)S(1)}, u32[]{:S(2)}, u32[]{:S(2)}) collective-permute-start(bf16[16,2304]{1,0:T(8,128)(2,1)S(1)} %get-tuple-element.26), channel_id=1, source_target_pairs={{0,192},{64,0},{128,64},{192,128},{1,193},{65,1},{129,65},{193,129... | collective-permute-start | bytes 221192 | tf_op jit(solution)/shard_map/ppermute | solution.py:18
  148.4 12.6 %all-to-all-start.3 = ((bf16[8,2,4608]{2,1,0:T(2,128)(2,1)}), bf16[8,2,4608]{2,1,0:T(2,128)(2,1)S(1)}, u32[]{:S(2)}, u32[]{:S(2)}) async-start(bf16[8,2,4608]{2,1,0:T(2,128)(2,1)} %reshape.162), calls=%async_computation.3 | async-start | bytes 294912 | tf_op jit(solution)/shard_map/all_to_all | solution.py:236
  152.5 1.1 collective-permute-start.26

commit v3 on v2

v3 whole, which is shorter than its diff:
```python
import functools

import jax
import jax.numpy as jnp
from jax import lax
from jax.experimental import pallas as pl
from jax.experimental.pallas import tpu as pltpu
from jax.sharding import Mesh, PartitionSpec as P

SOFTCAP = 30.0
TAIL = 128
ALL = ("x", "core", "y", "z")
VMEM_BYTES = 52 * 1024 * 1024


def shifted(v, axis, by):
    n = lax.axis_size(axis)
    return lax.ppermute(v, axis, [(i, (i + by) % n) for i in range(n)])


def gather(v, axis):
    peers = lax.axis_size(axis)
    return lax.all_to_all(jnp.broadcast_to(v[None], (peers, *v.shape)), axis, 0, 0, tiled=True)


def column_chunks(width, most):
    chunk = next(c for c in (most, 128) if width % c == 0)
    return [(at, chunk) for at in range(0, width, chunk)]


def fetches(sources, buffers, sems, chunks, offset=0):
    return [
        [
            pltpu.make_async_copy(src.at[:, pl.ds(offset + at, size)], dst.at[:, pl.ds(at, size)], sems.at[j, k])
            for k, (at, size) in enumerate(chunks)
        ]
        for j, (src, dst) in enumerate(zip(sources, buffers))
    ]


def logits_kernel(n, where_ref, *refs):
    late = refs[:n]
    early = refs[n : 2 * n]
    own_ref, sib_ref, sums_ref, own_out, sib_out, own_u, sib_u, tok, acc, sems = refs[2 * n :]
    half = early[0].shape[1]
    rows = late[0].shape[0] // n
    chunks = column_chunks(2 * half, 1536)
    copies = fetches((own_ref, sib_ref), (own_u, sib_u), sems, chunks)
    for part in copies:
        for copy in part:
            copy.start()

    for e in range(n):
        for d in range(n):
            at = pl.multiple_of(where_ref[e * n + d] * rows, rows)
            tok[pl.ds(at, rows), half:] = late[e][d * rows : (d + 1) * rows, :half]
            tok[pl.ds(at, rows), :half] = early[d][e * rows : (e + 1) * rows, :]

    sums = 0.0
    for j, (u, out) in enumerate(((own_u, own_out), (sib_u, sib_out))):
        for k, (at, size) in enumerate(chunks):
            copies[j][k].wait()
            part = lax.dot_general(
                tok[:, at : at + size],
                u[:, at : at + size],
                (((1,), (1,)), ((), ())),
                preferred_element_type=jnp.float32,
            )
            if k:
                part = acc[...] + part
            acc[...] = part
        capped = SOFTCAP * jnp.tanh(acc[...] / SOFTCAP)
        out[...] = capped
        sums = sums + jnp.sum(jnp.exp(capped - SOFTCAP), axis=1, keepdims=True)
    sums_ref[...] = jnp.broadcast_to(sums, sums_ref.shape)


def capped_logits(where, late, early, own, sib):
    n = len(late)
    vocab, width = own.shape
    plane = n * late[0].shape[0]
    vmem, anywhere = pl.BlockSpec(memory_space=pltpu.VMEM), pl.BlockSpec(memory_space=pl.ANY)
    capped = jax.ShapeDtypeStruct((plane, vocab), jnp.float32)
    sums = jax.ShapeDtypeStruct((plane, TAIL), jnp.float32)
    return pl.pallas_call(
        functools.partial(logits_kernel, n),
        out_shape=(sums, capped, capped),
        in_specs=[pl.BlockSpec(memory_space=pltpu.SMEM)] + [vmem] * (2 * n) + [anywhere] * 2,
        out_specs=(vmem,) * 3,
        scratch_shapes=[
            pltpu.VMEM((vocab, width), jnp.bfloat16),
            pltpu.VMEM((vocab, width), jnp.bfloat16),
            pltpu.VMEM((plane, width), jnp.bfloat16),
            pltpu.VMEM((plane, vocab), jnp.float32),
            pltpu.SemaphoreType.DMA((2, len(column_chunks(width, 1536)))),
        ],
        compiler_params=pltpu.CompilerParams(vmem_limit_bytes=VMEM_BYTES),
        cost_estimate=pl.CostEstimate(
            flops=4 * plane * vocab * width, bytes_accessed=4 * vocab * width + 4 * plane * width, transcendentals=0
        ),
    )(where, *late, *early, own, sib)


def labels_kernel(n, where_ref, *refs):
    late = refs[:n]
    tail_ref, sums_ref, own_c, sib_c, rows_ref, own_tail, sib_tail = refs[n:]
    plane, vocab = own_c.shape
    half = late[0].shape[1] - TAIL
    rows = plane // (n * n)
    for e in range(n):
        for d in range(n):
            i = e * n + d
            at = pl.ds(pl.multiple_of(where_ref[i] * rows, rows), rows)
            own_tail[at, :] = late[e][d * rows : (d + 1) * rows, half:].astype(jnp.float32)
            at = pl.ds(pl.multiple_of(where_ref[n * n + 2 + i] * rows, rows), rows)
            sib_tail[at, :] = tail_ref[i * rows : (i + 1) * rows, :].astype(jnp.float32)
    labels = sib_tail[:, 0:1] + 256.0 * sib_tail[:, 1:2] + 65536.0 * sib_tail[:, 2:3]
    picked = 0.0
    for j, capped in enumerate((own_c, sib_c)):
        ids = where_ref[n * n + j] + lax.broadcasted_iota(jnp.int32, (plane, vocab), 1)
        hits = ids == labels.astype(jnp.int32)
        picked = picked + jnp.sum(jnp.where(hits, capped[...], 0.0), axis=1, keepdims=True)
    lane = lax.broadcasted_iota(jnp.int32, (plane, 8), 1)
    columns = jnp.zeros((plane, 8), jnp.float32)
    for i, column in enumerate((sums_ref[:, 0:1], picked, labels, sib_tail[:, 3:4], own_tail[:, 3:4])):
        columns = jnp.where(lane == i, column, columns)
    rows_ref[...] = columns.T


def labels_and_sums(where, late, tail, sums, own_c, sib_c):
    n = len(late)
    plane = own_c.shape[0]
    vmem = pl.BlockSpec(memory_space=pltpu.VMEM)
    return pl.pallas_call(
        functools.partial(labels_kernel, n),
        out_shape=jax.ShapeDtypeStruct((8, plane), jnp.float32),
        in_specs=[pl.BlockSpec(memory_space=pltpu.SMEM)] + [vmem] * (n + 4),
        out_specs=vmem,
        scratch_shapes=[pltpu.VMEM((plane, TAIL), jnp.float32)] * 2,
        compiler_params=pltpu.CompilerParams(vmem_limit_bytes=16 * 1024 * 1024),
    )(where, *late, tail, sums, own_c, sib_c)


def gradient_kernel(n, where_ref, rows_ref, own_c, sib_c, own_ref, sib_ref, *refs):
    outs = refs[:n]
    own_p, sib_p, columns = refs[n:]
    plane, vocab = own_c.shape
    rows = plane // (n * n)

    @pl.when(pl.program_id(0) == 0)
    def _():
        columns[...] = rows_ref[...].T
        for i in range(n * n):
            at = pl.ds(pl.multiple_of(where_ref[i] * rows, rows), rows)
            to = slice(i * rows, (i + 1) * rows)
            known = columns[at, :]
            lse, coef, labels = known[:, 0:1], known[:, 1:2], known[:, 2:3].astype(jnp.int32)
            for c_ref, out, base in ((own_c, own_p, where_ref[n * n]), (sib_c, sib_p, where_ref[n * n + 1])):
                capped = c_ref[at, :]
                ids = base + lax.broadcasted_iota(jnp.int32, (rows, vocab), 1)
                grad = jnp.exp(capped - lse) - jnp.where(ids == labels, 1.0, 0.0)
                out[to, :] = (coef * grad * (1.0 - (capped / SOFTCAP) ** 2)).astype(jnp.bfloat16)

    part = jnp.dot(own_p[...], own_ref[...], preferred_element_type=jnp.float32)
    part = part + jnp.dot(sib_p[...], sib_ref[...], preferred_element_type=jnp.float32)
    part = part.astype(jnp.bfloat16)
    for i in range(n):
        outs[i][...] = part[i * n * rows : (i + 1) * n * rows, :]


def gradient_half(n, where, rows, own_c, sib_c, own, sib, second):
    plane, vocab = own_c.shape
    half = own.shape[1] // 2
    chunk = 1152 if half % 1152 == 0 else 128
    steps = half // chunk
    skip = steps if second else 0
    whole = lambda a: pl.BlockSpec(a.shape, lambda i: (0, 0))
    block = pl.BlockSpec((vocab, chunk), lambda i: (0, i + skip))
    piece = jax.ShapeDtypeStruct((plane // n, half), jnp.bfloat16)
    return pl.pallas_call(
        functools.partial(gradient_kernel, n),
        grid=(steps,),
        out_shape=(piece,) * n,
        in_specs=[pl.BlockSpec(memory_space=pltpu.SMEM), whole(rows), whole(own_c), whole(sib_c), block, block],
        out_specs=(pl.BlockSpec((plane // n, chunk), lambda i: (0, i)),) * n,
        scratch_shapes=[
            pltpu.VMEM((plane, vocab), jnp.bfloat16),
            pltpu.VMEM((plane, vocab), jnp.bfloat16),
            pltpu.VMEM((plane, 8), jnp.float32),
        ],
        compiler_params=pltpu.CompilerParams(vmem_limit_bytes=VMEM_BYTES),
        cost_estimate=pl.CostEstimate(
            flops=4 * plane * vocab * half, bytes_accessed=4 * vocab * half + 2 * plane * half, transcendentals=0
        ),
    )(where, rows, own_c, sib_c, own, sib)


def summed(pieces):
    return sum(p.astype(jnp.float32) for p in pieces).astype(jnp.bfloat16)


def body(hidden, unembed, targets, valid_mask, loss_scale):
    own_rows, width = hidden.shape
    vocab = unembed.shape[0]
    nx, _, ny, nz = (lax.axis_size(a) for a in ALL)
    n = nx
    ix, core, iy, iz = (lax.axis_index(a) for a in ALL)
    plane = nx * ny * nz * own_rows
    per_x = plane // nx
    half = width // 2
    f32, i32 = jnp.float32, jnp.int32

    unembed_sib = lax.ppermute(unembed, "core", [(0, 1), (1, 0)])

    digits = jnp.stack([targets % 256, (targets // 256) % 256, targets // 65536, valid_mask], axis=1)
    tail = jnp.pad(digits, ((0, 0), (0, TAIL - digits.shape[1]))).astype(jnp.bfloat16)
    by_z = gather(jnp.concatenate([hidden, tail], axis=1), "z").reshape(nz * own_rows, width + TAIL)

    by_z, unembed_sib = lax.optimization_barrier((by_z, unembed_sib))

    first, second = by_z[:, :half], by_z[:, half:]
    along_x = jnp.concatenate([first] + [shifted(first, "x", e) for e in range(1, n)])
    along_y = jnp.concatenate([second] + [shifted(second, "y", d) for d in range(1, n)])
    along_x, along_y = lax.optimization_barrier((along_x, along_y))
    late = [along_y] + [shifted(along_y, "x", e) for e in range(1, n)]
    early = [along_x] + [shifted(along_x, "y", d) for d in range(1, n)]
    tail_sib = lax.ppermute(jnp.concatenate([v[:, half:] for v in late]), "core", [(0, 1), (1, 0)])

    device = lax.axis_index(ALL)
    bases = vocab * jnp.stack([device, device + (1 - 2 * core) * ny * nz])
    near_x, near_y = (ix - jnp.arange(nx)) % nx, (iy - jnp.arange(ny)) % ny
    places = near_x[:, None] * ny + near_y[None, :]
    label_places = ((near_x - core) % nx)[:, None] * ny + near_y[None, :]
    where_xy = jnp.concatenate([places.ravel(), bases, label_places.ravel()]).astype(i32)
    where_yx = jnp.concatenate([places.T.ravel(), bases]).astype(i32)

    sums, own_c, sib_c = capped_logits(where_xy, late, early, unembed, unembed_sib)
    known = labels_and_sums(where_xy, late, tail_sib, sums, own_c, sib_c)
    stats = gather(known[:2].reshape(2 * plane // 128, 128), ("x", "y", "z"))
    labels, weights = known[2], known[3]
    by_x = lambda v: jnp.sum(v.reshape(nx, per_x), axis=1)
    of_tokens = by_x(weights)
    counts = by_x(known[4]) + jnp.where(core == 0, of_tokens, jnp.roll(of_tokens, 1))
    counts_tok = jnp.repeat(jnp.where(core == 0, counts, jnp.roll(counts, -1)), per_x)
    coef = loss_scale * weights / counts_tok
    stats = jnp.sum(stats.reshape(nx * ny * nz, 2 * plane // 128, 128), axis=0)
    total, picked = stats.reshape(2, plane)
    lse = SOFTCAP + jnp.log(total)
    rows = jnp.stack([lse, coef, labels] + [jnp.zeros_like(lse)] * 5)

    to_x = gradient_half(n, where_xy, rows, own_c, sib_c, unembed, unembed_sib, True)
    to_y = gradient_half(n, where_yx, rows, own_c, sib_c, unembed, unembed_sib, False)
    got_x = [to_x[0]] + [shifted(to_x[e], "x", -e) for e in range(1, n)]
    got_y = [to_y[0]] + [shifted(to_y[d], "y", -d) for d in range(1, n)]

    sums = jnp.sum((weights * (lse - picked)).reshape(nx, per_x), axis=1)
    sums = jnp.where(core == 0, sums, jnp.roll(sums, 1))
    losses = (sums + lax.ppermute(sums, "core", [(0, 1), (1, 0)])) / counts

    part_x, part_y = summed(got_x), summed(got_y)
    cut = lambda v, i: v[i * nz * own_rows : (i + 1) * nz * own_rows]
    got_y = [cut(part_x, 0)] + [shifted(cut(part_x, d), "y", -d) for d in range(1, n)]
    got_x = [cut(part_y, 0)] + [shifted(cut(part_y, e), "x", -e) for e in range(1, n)]
    part = jnp.concatenate([summed(got_x), summed(got_y)], axis=1).reshape(nz, own_rows, width)
    got = lax.all_to_all(part, "z", 0, 0, tiled=True)
    return jnp.sum(got.astype(f32), axis=0), losses


def solution(mesh):
    sections, groups = mesh.devices.shape
    chips = Mesh(mesh.devices.reshape(sections // 2, 2, 4, groups // 4), ALL)
    return jax.shard_map(
        body,
        mesh=chips,
        in_specs=(P(ALL, None), P(ALL, None), P(ALL), P(ALL), P()),
        out_specs=(P(ALL, None), P()),
        check_vma=False,
    )
```

time: 163 us -> 158 us (0.969)
  blocking collectives: 0 us -> 11.6 us
  starting transfers between devices: 66.3 us -> 56.7 us
  waiting for transfers between devices: 51.7 us -> 46.9 us
  Pallas kernels: 29.2 us -> 26.1 us
    all_to_all x0 -> x1, blocking collectives: none -> 11.6 us  [body(): got = lax.all_to_all(part, 'z', 0, 0, tiled=True)]
    all_to_all x1 -> x0, waiting for transfers between devices: 6.78 us -> none  [body(): got = lax.all_to_all(part, 'z', 0, 0, tiled=True)]
    ppermute x24, waiting for transfers between devices: 19.6 us -> 25.3 us  [shifted(): return lax.ppermute(v, axis, [(i, (i + by) % n) for i in range(n)])]
    ppermute x24, starting transfers between devices: 41.9 us -> 38.1 us  [shifted(): return lax.ppermute(v, axis, [(i, (i + by) % n) for i in range(n)])]
    unnamed x5 -> x13, local copies, waits for them, and re-layouts: 0.8 us -> 4.49 us
    pallas_call x1 -> x2, Pallas kernels: 15.2 us -> 11.6 us  [the longest x1 10.4 us: capped_logits(): pl.pallas_call(functools.partial(logits_kernel, n), out_shape=(sums, capp...]
    all_to_all x1 -> x0, starting transfers between devices: 3.38 us -> none  [body(): got = lax.all_to_all(part, 'z', 0, 0, tiled=True)]
    all_to_all x3 -> x2, waiting for transfers between devices: 24.2 us -> 21 us  [gather(): lax.all_to_all(jnp.broadcast_to(v[None], (peers, *v.shape)), axis, 0, 0,...]
  transfers between devices with their start and end apart: 31 -> 29, of which waited for: 13 -> 15; matrix products, arithmetic and copies ran while one was open for 6% -> 3% of each run, Pallas kernels for 4% -> 11%
where the time goes in v3:
time: 158 us; the launch traced here: 156 us
  starting transfers between devices  56.7 us (36%)
  waiting for transfers between devices  46.9 us (30%)
  Pallas kernels  26.1 us (17%)
  blocking collectives  11.6 us (7%)
  local copies, waits for them, and re-layouts  8.13 us (5%)
  other arithmetic  5.47 us (3%)
    ppermute x24, starting transfers between devices, shifted(): return lax.ppermute(v, axis, [(i, (i + by) % n) for i in range(n)])  38.1 us
    ppermute x24, waiting for transfers between devices, shifted(): return lax.ppermute(v, axis, [(i, (i + by) % n) for i in range(n)])  25.3 us
    all_to_all x2, waiting for transfers between devices, gather(): lax.all_to_all(jnp.broadcast_to(v[None], (peers, *v.shape)), axis, 0, 0,...  21 us
    all_to_all x2, starting transfers between devices, gather(): lax.all_to_all(jnp.broadcast_to(v[None], (peers, *v.shape)), axis, 0, 0,...  18.2 us
    pallas_call x2, Pallas kernels, gradient_half(): pl.pallas_call(functools.partial(gradient_kernel, n), grid=(steps,), out_...  14.5 us
    all_to_all x1, blocking collectives, body(): got = lax.all_to_all(part, 'z', 0, 0, tiled=True)  11.6 us
    pallas_call x1, Pallas kernels, capped_logits(): pl.pallas_call(functools.partial(logits_kernel, n), out_shape=(sums, capp...  10.4 us
    unnamed x13, local copies, waits for them, and re-layouts  4.49 us
  transfers between devices with their start and end apart: 29, of which 15 were waited for; matrix products, arithmetic and copies ran while one was open for 3% of the time, Pallas kernels for 11%

profile of v3, /device:TPU:8, one launch (start us, length us, event | category | flops | bytes accessed | tf_op | source)
XLA Modules:
  0.0 156.5 jit_solution(772318741147145493)
XLA Ops:
  0.7 0.7 fusion.4
  1.4 0.1 copy.14
  1.6 0.7 fusion
  2.3 0.7 broadcast_in_dim.8
  3.0 8.5 %all-to-all-start = ((bf16[8,2,4736]{2,1,0:T(2,128)(2,1)}), bf16[8,2,4736]{2,1,0:T(2,128)(2,1)S(1)}, u32[]{:S(2)}, u32[]{:S(2)}) async-start(bf16[8,2,4736]{2,1,0:T(2,128)(2,1)} %broadcast_in_dim.8), calls=%async_computation | async-start | bytes 303104 | tf_op jit(solution)/shard_map/all_to_all | solution.py:23
  11.5 10.2 %all-to-all-done = bf16[8,2,4736]{2,1,0:T(2,128)(2,1)S(1)} async-done(((bf16[8,2,4736]{2,1,0:T(2,128)(2,1)}), bf16[8,2,4736]{2,1,0:T(2,128)(2,1)S(1)}, u32[]{:S(2)}, u32[]{:S(2)}) %all-to-all-start) | async-done | bytes 151584 | tf_op jit(solution)/shard_map/all_to_all | solution.py:23
  21.8 1.6 %collective-permute-start.1 = (bf16[16,2304]{1,0:T(8,128)(2,1)S(1)}, bf16[16,2304]{1,0:T(8,128)(2,1)S(1)}, u32[]{:S(2)}, u32[]{:S(2)}) collective-permute-start(bf16[16,2304]{1,0:T(8,128)(2,1)S(1)} %slice.78), channel_id=1, source_target_pairs={{0,64},{64,128},{128,192},{192,0},{1,65},{65,129},{129,193},{193,1... | collective-permute-start | bytes 221192 | tf_op jit(solution)/shard_map/ppermute | solution.py:18
  23.3 2.7 %collective-permute-start.2 = (bf16[16,2304]{1,0:T(8,128)(2,1)S(1)}, bf16[16,2304]{1,0:T(8,128)(2,1)S(1)}, u32[]{:S(2)}, u32[]{:S(2)}) collective-permute-start(bf16[16,2304]{1,0:T(8,128)(2,1)S(1)} %slice.78), channel_id=1, source_target_pairs={{0,128},{64,192},{128,0},{192,64},{1,129},{65,193},{129,1},{193,65... | collective-permute-start | bytes 221192 | tf_op jit(solution)/shard_map/ppermute | solution.py:18
  26.1 1.4 collective-permute-start.3
  27.5 1.7 %collective-permute-start.4 = (bf16[16,2432]{1,0:T(8,128)(2,1)S(1)}, bf16[16,2432]{1,0:T(8,128)(2,1)S(1)}, u32[]{:S(2)}, u32[]{:S(2)}) collective-permute-start(bf16[16,2432]{1,0:T(8,128)(2,1)S(1)} %slice.79), channel_id=1, source_target_pairs={{0,8},{8,16},{16,24},{24,0},{1,9},{9,17},{17,25},{25,1},{2,10},{10... | collective-permute-start | bytes 233480 | tf_op jit(solution)/shard_map/ppermute | solution.py:18
  29.2 0.9 collective-permute-start.5
  30.1 2.4 %collective-permute-start.6 = (bf16[16,2432]{1,0:T(8,128)(2,1)S(1)}, bf16[16,2432]{1,0:T(8,128)(2,1)S(1)}, u32[]{:S(2)}, u32[]{:S(2)}) collective-permute-start(bf16[16,2432]{1,0:T(8,128)(2,1)S(1)} %slice.79), channel_id=1, source_target_pairs={{0,24},{8,0},{16,8},{24,16},{1,25},{9,1},{17,9},{25,17},{2,26},{10... | collective-permute-start | bytes 233480 | tf_op jit(solution)/shard_map/ppermute | solution.py:18
  32.7 2.5 %collective-permute-done.5 = bf16[16,2432]{1,0:T(8,128)(2,1)S(1)} collective-permute-done((bf16[16,2432]{1,0:T(8,128)(2,1)S(1)}, bf16[16,2432]{1,0:T(8,128)(2,1)S(1)}, u32[]{:S(2)}, u32[]{:S(2)}) %collective-permute-start.5) | collective-permute-done | bytes 77856 | tf_op jit(solution)/shard_map/ppermute | solution.py:18
  35.2 0.2 collective-permute-done.6
  35.4 0.7 collective-permute-start.7
  36.1 0.9 collective-permute-start.8
  36.9 1.9 %collective-permute-start.9 = (bf16[64,2432]{1,0:T(8,128)(2,1)S(1)}, bf16[64,2432]{1,0:T(8,128)(2,1)S(1)}, u32[]{:S(2)}, u32[]{:S(2)}) collective-permute-start(bf16[64,2432]{1,0:T(8,128)(2,1)S(1)} %pad_maximum_fusion.refs_0_), channel_id=1, source_target_pairs={{0,192},{64,0},{128,64},{192,128},{1,193},{65,1},{129,65},{193,129... | collective-permute-start | bytes 933896 | tf_op jit(solution)/shard_map/ppermute | solution.py:18
  39.1 1.1 collective-permute-start.11
  40.2 2.5 %collective-permute-start.12 = (bf16[64,2304]{1,0:T(8,128)(2,1)S(1)}, bf16[64,2304]{1,0:T(8,128)(2,1)S(1)}, u32[]{:S(2)}, u32[]{:S(2)}) collective-permute-start(bf16[64,2304]{1,0:T(8,128)(2,1)S(1)} %pad_maximum_fusion.1.refs_4_), channel_id=1, source_target_pairs={{0,16},{8,24},{16,0},{24,8},{1,17},{9,25},{17,1},{25,9},{2,18},{10... | collective-permute-start | bytes 884744 | tf_op jit(solution)/shard_map/ppermute | solution.py:18
  42.8 6.8 %collective-permute-done.7.refs_1_ = bf16[64,2432]{1,0:T(8,128)(2,1)S(1)} collective-permute-done((bf16[64,2432]{1,0:T(8,128)(2,1)S(1)}, bf16[64,2432]{1,0:T(8,128)(2,1)S(1)}, u32[]{:S(2)}, u32[]{:S(2)}) %collective-permute-start.7) | collective-permute-done | bytes 311328 | tf_op jit(solution)/shard_map/ppermute | solution.py:18
  49.5 1.4 collective-permute-start.13
  51.2 0.3 collective-permute-start.10
  51.6 4.7 %collective-permute-done.13.refs_7_ = bf16[64,2304]{1,0:T(8,128)(2,1)S(1)} collective-permute-done((bf16[64,2304]{1,0:T(8,128)(2,1)S(1)}, bf16[64,2304]{1,0:T(8,128)(2,1)S(1)}, u32[]{:S(2)}, u32[]{:S(2)}) %collective-permute-start.13) | collective-permute-done | bytes 294944 | tf_op jit(solution)/shard_map/ppermute | solution.py:18
  56.3 10.4 %shard_map.68 = (f32[256,128]{1,0:T(8,128)S(1)}, f32[256,1000]{1,0:T(8,128)}, f32[256,1000]{1,0:T(8,128)}) custom-call(s32[34]{0:T(128)S(1)} %pad_add_fusion.1.where_ref, bf16[64,2432]{1,0:T(8,128)(2,1)S(1)} %pad_maximum_fusion.refs_0_, bf16[64,2432]{1,0:T(8,128)(2,1)S(1)} %collective-permute-done.7.refs_1_, bf16[64,2432]{1,0:T(8,128)(2,1)} %copy-done.2, ...), custom_call_target="tpu_custom_call" | custom-call | flops 4718592000 | bytes 23150592 | tf_op jit(solution)/shard_map/pallas_call | solution.py:85
  66.7 1.2 copy-done
  67.9 1.2 copy-done.1
  69.2 1.0 copy-done.3
  70.1 1.0 copy-done.5
  71.1 1.2 shard_map.69
  72.3 0.7 broadcast_in_dim.10
  73.1 9.7 %all-to-all-start.1 = ((f32[128,4,128]{2,1,0:T(4,128)}), f32[128,4,128]{2,1,0:T(4,128)S(1)}, u32[]{:S(2)}, u32[]{:S(2)}) async-start(f32[128,4,128]{2,1,0:T(4,128)} %broadcast_in_dim.10), calls=%async_computation.1 | async-start | bytes 524288 | tf_op jit(solution)/shard_map/all_to_all | solution.py:23
  83.8 0.1 reduce_sum.46
  83.9 10.9 %all-to-all-done.1 = f32[128,4,128]{2,1,0:T(4,128)S(1)} async-done(((f32[128,4,128]{2,1,0:T(4,128)}), f32[128,4,128]{2,1,0:T(4,128)S(1)}, u32[]{:S(2)}, u32[]{:S(2)}) %all-to-all-start.1) | async-done | bytes 262176 | tf_op jit(solution)/shard_map/all_to_all | solution.py:23
  94.8 0.1 reduce_sum.45
  95.0 0.1 multiply_reduce_fusion
  95.2 0.6 slice.100
  95.7 0.7 broadcast_select_fusion
  96.5 0.6 slice.87
  97.1 0.5 collective-permute-done.26
  97.6 1.2 add_divide_fusion
  98.9 0.1 broadcast_select_fusion.1
  99.2 7.3 %shard_map.70 = (bf16[64,2304]{1,0:T(8,128)(2,1)S(1)}, bf16[64,2304]{1,0:T(8,128)(2,1)S(1)}, bf16[64,2304]{1,0:T(8,128)(2,1)S(1)}, bf16[64,2304]{1,0:T(8,128)(2,1)S(1)}) custom-call(s32[18]{0:T(128)S(1)} %pad_add_fusion.where_ref, f32[8,256]{1,0:T(8,128)S(1)} %stack.46.rows_ref, f32[256,1000]{1,0:T(8,128)} %get-tuple-element.22.refs_6_.own_c, ...), custom_call_target="tpu_custom_call" | custom-call | flops 2359296000 | bytes 10395648 | tf_op jit(solution)/shard_map/pallas_call | solution.py:180
  106.5 2.3 %collective-permute-start.14 = (bf16[64,2304]{1,0:T(8,128)(2,1)S(1)}, bf16[64,2304]{1,0:T(8,128)(2,1)S(1)}, u32[]{:S(2)}, u32[]{:S(2)}) collective-permute-start(bf16[64,2304]{1,0:T(8,128)(2,1)S(1)} %get-tuple-element.25), channel_id=1, source_target_pairs={{0,24},{8,0},{16,8},{24,16},{1,25},{9,1},{17,9},{25,17},{2,26},{10... | collective-permute-start | bytes 884744 | tf_op jit(solution)/shard_map/ppermute | solution.py:18
  108.8 0.4 collective-permute-start.15
  109.2 1.6 %collective-permute-start.16 = (bf16[64,2304]{1,0:T(8,128)(2,1)S(1)}, bf16[64,2304]{1,0:T(8,128)(2,1)S(1)}, u32[]{:S(2)}, u32[]{:S(2)}) collective-permute-start(bf16[64,2304]{1,0:T(8,128)(2,1)S(1)} %get-tuple-element.27), channel_id=1, source_target_pairs={{0,8},{8,16},{16,24},{24,0},{1,9},{9,17},{17,25},{25,1},{2,10},{10... | collective-permute-start | bytes 884744 | tf_op jit(solution)/shard_map/ppermute | solution.py:18
  110.8 7.2 %shard_map.71 = (bf16[64,2304]{1,0:T(8,128)(2,1)S(1)}, bf16[64,2304]{1,0:T(8,128)(2,1)S(1)}, bf16[64,2304]{1,0:T(8,128)(2,1)S(1)}, bf16[64,2304]{1,0:T(8,128)(2,1)S(1)}) custom-call(s32[34]{0:T(128)S(1)} %pad_add_fusion.1.where_ref, f32[8,256]{1,0:T(8,128)S(1)} %stack.46.rows_ref, f32[256,1000]{1,0:T(8,128)} %get-tuple-element.22.refs_6_.own_c, ...), custom_call_target="tpu_custom_call" | custom-call | flops 2359296000 | bytes 10395648 | tf_op jit(solution)/shard_map/pallas_call | solution.py:180
  118.1 1.2 collective-permute-start.20
  119.3 1.7 %collective-permute-start.21 = (bf16[64,2304]{1,0:T(8,128)(2,1)S(1)}, bf16[64,2304]{1,0:T(8,128)(2,1)S(1)}, u32[]{:S(2)}, u32[]{:S(2)}) collective-permute-start(bf16[64,2304]{1,0:T(8,128)(2,1)S(1)} %get-tuple-element.30), channel_id=1, source_target_pairs={{0,128},{64,192},{128,0},{192,64},{1,129},{65,193},{129,1},{193,65... | collective-permute-start | bytes 884744 | tf_op jit(solution)/shard_map/ppermute | solution.py:18
  121.0 1.6 %collective-permute-done.15 = bf16[64,2304]{1,0:T(8,128)(2,1)S(1)} collective-permute-done((bf16[64,2304]{1,0:T(8,128)(2,1)S(1)}, bf16[64,2304]{1,0:T(8,128)(2,1)S(1)}, u32[]{:S(2)}, u32[]{:S(2)}) %collective-permute-start.15) | collective-permute-done | bytes 294944 | tf_op jit(solution)/shard_map/ppermute | solution.py:18
  122.6 1.2 collective-permute-done.16
  123.9 0.1 add_convert_fusion.1
  124.0 1.0 collective-permute-start.17
  125.0 1.9 %collective-permute-start.18 = (bf16[16,2304]{1,0:T(8,128)(2,1)S(1)}, bf16[16,2304]{1,0:T(8,128)(2,1)S(1)}, u32[]{:S(2)}, u32[]{:S(2)}) collective-permute-start(bf16[16,2304]{1,0:T(8,128)(2,1)S(1)} %get-tuple-element.40), channel_id=1, source_target_pairs={{0,128},{64,192},{128,0},{192,64},{1,129},{65,193},{129,1},{193,65... | collective-permute-start | bytes 221192 | tf_op jit(solution)/shard_map/ppermute | solution.py:18
  126.9 3.9 %collective-permute-done.20 = bf16[64,2304]{1,0:T(8,128)(2,1)S(1)} collective-permute-done((bf16[64,2304]{1,0:T(8,128)(2,1)S(1)}, bf16[64,2304]{1,0:T(8,128)(2,1)S(1)}, u32[]{:S(2)}, u32[]{:S(2)}) %collective-permute-start.20) | collective-permute-done | bytes 294944 | tf_op jit(solution)/shard_map/ppermute | solution.py:18
  130.9 4.3 %collective-permute-start.19 = (bf16[16,2304]{1,0:T(8,128)(2,1)S(1)}, bf16[16,2304]{1,0:T(8,128)(2,1)S(1)}, u32[]{:S(2)}, u32[]{:S(2)}) collective-permute-start(bf16[16,2304]{1,0:T(8,128)(2,1)S(1)} %get-tuple-element.39), channel_id=1, source_target_pairs={{0,64},{64,128},{128,192},{192,0},{1,65},{65,129},{129,193},{193,1... | collective-permute-start | bytes 221192 | tf_op jit(solution)/shard_map/ppermute | solution.py:18
  135.1 0.9 collective-permute-done.22
  136.0 0.1 add_convert_fusion
  136.2 0.2 collective-permute-start.23
  136.4 3.2 %collective-permute-start.24 = (bf16[16,2304]{1,0:T(8,128)(2,1)S(1)}, bf16[16,2304]{1,0:T(8,128)(2,1)S(1)}, u32[]{:S(2)}, u32[]{:S(2)}) collective-permute-start(bf16[16,2304]{1,0:T(8,128)(2,1)S(1)} %get-tuple-element.43), channel_id=1, source_target_pairs={{0,16},{8,24},{16,0},{24,8},{1,17},{9,25},{17,1},{25,9},{2,18},{10... | collective-permute-start | bytes 221192 | tf_op jit(solution)/shard_map/ppermute | solution.py:18
  139.6 1.0 collective-permute-start.25
  140.6 2.6 %collective-permute-done.24 = bf16[16,2304]{1,0:T(8,128)(2,1)S(1)} collective-permute-done((bf16[16,2304]{1,0:T(8,128)(2,1)S(1)}, bf16[16,2304]{1,0:T(8,128)(2,1)S(1)}, u32[]{:S(2)}, u32[]{:S(2)}) %collective-permute-start.24) | collective-permute-done | bytes 73760 | tf_op jit(solution)/shard_map/ppermute | solution.py:18
  143.3 0.7 collective-permute-done.25
  144.1 11.6 %all_to_all.15 = bf16[8,2,4608]{2,1,0:T(2,128)(2,1)S(1)} all-to-all(bf16[8,2,4608]{2,1,0:T(2,128)(2,1)S(1)} %reshape.115), channel_id=1, replica_groups=mesh['x'=4,'core'=2,'y'=4,'z'=8] {'z'}, dimensions={0} | all-to-all | bytes 294912 | tf_op jit(solution)/shard_map/all_to_all | solution.py:265
  155.7 0.7 convert_reduce_fusion
  (67 shorter events, 1.9 us)
Async XLA Ops:
  0.6 21.1 %collective-permute-start = (bf16[1000,4608]{1,0:T(8,128)(2,1)}, bf16[1000,4608]{1,0:T(8,128)(2,1)}, u32[]{:S(2)}, u32[]{:S(2)}) collective-permute-start(bf16[1000,4608]{1,0:T(8,128)(2,1)} %own_ref.3), channel_id=1, source_target_pairs={{0,32},{32,0},{1,33},{33,1},{2,34},{34,2},{3,35},{35,3},{4,36},{36... | collective-permute-start | bytes 27648008 | tf_op jit(solution)/shard_map/ppermute | solution.py:213
  3.0 18.6 %all-to-all-start = ((bf16[8,2,4736]{2,1,0:T(2,128)(2,1)}), bf16[8,2,4736]{2,1,0:T(2,128)(2,1)S(1)}, u32[]{:S(2)}, u32[]{:S(2)}) async-start(bf16[8,2,4736]{2,1,0:T(2,128)(2,1)} %broadcast_in_dim.8), calls=%async_computation | async-start | bytes 303104 | tf_op jit(solution)/shard_map/all_to_all | solution.py:23
  21.8 8.4 %collective-permute-start.1 = (bf16[16,2304]{1,0:T(8,128)(2,1)S(1)}, bf16[16,2304]{1,0:T(8,128)(2,1)S(1)}, u32[]{:S(2)}, u32[]{:S(2)}) collective-permute-start(bf16[16,2304]{1,0:T(8,128)(2,1)S(1)} %slice.78), channel_id=1, source_target_pairs={{0,64},{64,128},{128,192},{192,0},{1,65},{65,129},{129,193},{193,1... | collective-permute-start | bytes 221192 | tf_op jit(solution)/shard_map/ppermute | solution.py:18
  23.3 9.2 %collective-permute-start.2 = (bf16[16,2304]{1,0:T(8,128)(2,1)S(1)}, bf16[16,2304]{1,0:T(8,128)(2,1)S(1)}, u32[]{:S(2)}, u32[]{:S(2)}) collective-permute-start(bf16[16,2304]{1,0:T(8,128)(2,1)S(1)} %slice.78), channel_id=1, source_target_pairs={{0,128},{64,192},{128,0},{192,64},{1,129},{65,193},{129,1},{193,65... | collective-permute-start | bytes 221192 | tf_op jit(solution)/shard_map/ppermute | solution.py:18
  26.1 6.5 %collective-permute-start.3 = (bf16[16,2304]{1,0:T(8,128)(2,1)S(1)}, bf16[16,2304]{1,0:T(8,128)(2,1)S(1)}, u32[]{:S(2)}, u32[]{:S(2)}) collective-permute-start(bf16[16,2304]{1,0:T(8,128)(2,1)S(1)} %slice.78), channel_id=1, source_target_pairs={{0,192},{64,0},{128,64},{192,128},{1,193},{65,1},{129,65},{193,129... | collective-permute-start | bytes 221192 | tf_op jit(solution)/shard_map/ppermute | solution.py:18
  27.5 5.1 %collective-permute-start.4 = (bf16[16,2432]{1,0:T(8,128)(2,1)S(1)}, bf16[16,2432]{1,0:T(8,128)(2,1)S(1)}, u32[]{:S(2)}, u32[]{:S(2)}) collective-permute-start(bf16[16,2432]{1,0:T(8,128)(2,1)S(1)} %slice.79), channel_id=1, source_target_pairs={{0,8},{8,16},{16,24},{24,0},{1,9},{9,17},{17,25},{25,1},{2,10},{10... | collective-permute-start | bytes 233480 | tf_op jit(solution)/shard_map/ppermute | solution.py:18
  29.2 6.0 %collective-permute-start.5 = (bf16[16,2432]{1,0:T(8,128)(2,1)S(1)}, bf16[16,2432]{1,0:T(8,128)(2,1)S(1)}, u32[]{:S(2)}, u32[]{:S(2)}) collective-permute-start(bf16[16,2432]{1,0:T(8,128)(2,1)S(1)} %slice.79), channel_id=1, source_target_pairs={{0,16},{8,24},{16,0},{24,8},{1,17},{9,25},{17,1},{25,9},{2,18},{10... | collective-permute-start | bytes 233480 | tf_op jit(solution)/shard_map/ppermute | solution.py:18
  30.1 5.2 %collective-permute-start.6 = (bf16[16,2432]{1,0:T(8,128)(2,1)S(1)}, bf16[16,2432]{1,0:T(8,128)(2,1)S(1)}, u32[]{:S(2)}, u32[]{:S(2)}) collective-permute-start(bf16[16,2432]{1,0:T(8,128)(2,1)S(1)} %slice.79), channel_id=1, source_target_pairs={{0,24},{8,0},{16,8},{24,16},{1,25},{9,1},{17,9},{25,17},{2,26},{10... | collective-permute-start | bytes 233480 | tf_op jit(solution)/shard_map/ppermute | solution.py:18
  35.4 14.2 %collective-permute-start.7 = (bf16[64,2432]{1,0:T(8,128)(2,1)S(1)}, bf16[64,2432]{1,0:T(8,128)(2,1)S(1)}, u32[]{:S(2)}, u32[]{:S(2)}) collective-permute-start(bf16[64,2432]{1,0:T(8,128)(2,1)S(1)} %pad_maximum_fusion.refs_0_), channel_id=1, source_target_pairs={{0,64},{64,128},{128,192},{192,0},{1,65},{65,129},{129,193},{193,1... | collective-permute-start | bytes 933896 | tf_op jit(solution)/shard_map/ppermute | solution.py:18
  36.1 15.1 %collective-permute-start.8 = (bf16[64,2432]{1,0:T(8,128)(2,1)S(1)}, bf16[64,2432]{1,0:T(8,128)(2,1)S(1)}, u32[]{:S(2)}, u32[]{:S(2)}) collective-permute-start(bf16[64,2432]{1,0:T(8,128)(2,1)S(1)} %pad_maximum_fusion.refs_0_), channel_id=1, source_target_pairs={{0,128},{64,192},{128,0},{192,64},{1,129},{65,193},{129,1},{193,65... | collective-permute-start | bytes 933896 | tf_op jit(solution)/shard_map/ppermute | solution.py:18
  36.9 14.2 %collective-permute-start.9 = (bf16[64,2432]{1,0:T(8,128)(2,1)S(1)}, bf16[64,2432]{1,0:T(8,128)(2,1)S(1)}, u32[]{:S(2)}, u32[]{:S(2)}) collective-permute-start(bf16[64,2432]{1,0:T(8,128)(2,1)S(1)} %pad_maximum_fusion.refs_0_), channel_id=1, source_target_pairs={{0,192},{64,0},{128,64},{192,128},{1,193},{65,1},{129,65},{193,129... | collective-permute-start | bytes 933896 | tf_op jit(solution)/shard_map/ppermute | solution.py:18
  39.1 12.4 %collective-permute-start.11 = (bf16[64,2304]{1,0:T(8,128)(2,1)S(1)}, bf16[64,2304]{1,0:T(8,128)(2,1)S(1)}, u32[]{:S(2)}, u32[]{:S(2)}) collective-permute-start(bf16[64,2304]{1,0:T(8,128)(2,1)S(1)} %pad_maximum_fusion.1.refs_4_), channel_id=1, source_target_pairs={{0,8},{8,16},{16,24},{24,0},{1,9},{9,17},{17,25},{25,1},{2,10},{10... | collective-permute-start | bytes 884744 | tf_op jit(solution)/shard_map/ppermute | solution.py:18
  40.2 11.3 %collective-permute-start.12 = (bf16[64,2304]{1,0:T(8,128)(2,1)S(1)}, bf16[64,2304]{1,0:T(8,128)(2,1)S(1)}, u32[]{:S(2)}, u32[]{:S(2)}) collective-permute-start(bf16[64,2304]{1,0:T(8,128)(2,1)S(1)} %pad_maximum_fusion.1.refs_4_), channel_id=1, source_target_pairs={{0,16},{8,24},{16,0},{24,8},{1,17},{9,25},{17,1},{25,9},{2,18},{10... | collective-permute-start | bytes 884744 | tf_op jit(solution)/shard_map/ppermute | solution.py:18
  49.5 6.7 %collective-permute-start.13 = (bf16[64,2304]{1,0:T(8,128)(2,1)S(1)}, bf16[64,2304]{1,0:T(8,128)(2,1)S(1)}, u32[]{:S(2)}, u32[]{:S(2)}) collective-permute-start(bf16[64,2304]{1,0:T(8,128)(2,1)S(1)} %pad_maximum_fusion.1.refs_4_), channel_id=1, source_target_pairs={{0,24},{8,0},{16,8},{24,16},{1,25},{9,1},{17,9},{25,17},{2,26},{10... | collective-permute-start | bytes 884744 | tf_op jit(solution)/shard_map/ppermute | solution.py:18
  51.1 5.1 %copy-start.2 = (bf16[64,2432]{1,0:T(8,128)(2,1)}, bf16[64,2432]{1,0:T(8,128)(2,1)S(1)}, u32[]{:S(2)}) copy-start(bf16[64,2432]{1,0:T(8,128)(2,1)S(1)} %collective-permute-done.8.refs_2_) | copy-start | bytes 933892
  51.2 5.1 %copy-start.4 = (bf16[64,2432]{1,0:T(8,128)(2,1)}, bf16[64,2432]{1,0:T(8,128)(2,1)S(1)}, u32[]{:S(2)}) copy-start(bf16[64,2432]{1,0:T(8,128)(2,1)S(1)} %collective-permute-done.9.refs_3_) | copy-start | bytes 933892
  51.2 15.5 %collective-permute-start.10 = (bf16[256,128]{1,0:T(8,128)(2,1)S(1)}, bf16[256,128]{1,0:T(8,128)(2,1)S(1)}, u32[]{:S(2)}, u32[]{:S(2)}) collective-permute-start(bf16[256,128]{1,0:T(8,128)(2,1)S(1)} %pad_maximum_fusion.3), channel_id=1, source_target_pairs={{0,32},{32,0},{1,33},{33,1},{2,34},{34,2},{3,35},{35,3},{4,36},{36... | collective-permute-start | bytes 196616 | tf_op jit(solution)/shard_map/ppermute | solution.py:227
  66.7 1.2 copy-start
  67.9 1.2 copy-start.1
  69.2 1.0 copy-start.3
  70.1 1.0 copy-start.5
  73.1 21.7 %all-to-all-start.1 = ((f32[128,4,128]{2,1,0:T(4,128)}), f32[128,4,128]{2,1,0:T(4,128)S(1)}, u32[]{:S(2)}, u32[]{:S(2)}) async-start(f32[128,4,128]{2,1,0:T(4,128)} %broadcast_in_dim.10), calls=%async_computation.1 | async-start | bytes 524288 | tf_op jit(solution)/shard_map/all_to_all | solution.py:23
  96.5 1.1 collective-permute-start.26
  106.5 14.5 %collective-permute-start.14 = (bf16[64,2304]{1,0:T(8,128)(2,1)S(1)}, bf16[64,2304]{1,0:T(8,128)(2,1)S(1)}, u32[]{:S(2)}, u32[]{:S(2)}) collective-permute-start(bf16[64,2304]{1,0:T(8,128)(2,1)S(1)} %get-tuple-element.25), channel_id=1, source_target_pairs={{0,24},{8,0},{16,8},{24,16},{1,25},{9,1},{17,9},{25,17},{2,26},{10... | collective-permute-start | bytes 884744 | tf_op jit(solution)/shard_map/ppermute | solution.py:18
  108.8 13.8 %collective-permute-start.15 = (bf16[64,2304]{1,0:T(8,128)(2,1)S(1)}, bf16[64,2304]{1,0:T(8,128)(2,1)S(1)}, u32[]{:S(2)}, u32[]{:S(2)}) collective-permute-start(bf16[64,2304]{1,0:T(8,128)(2,1)S(1)} %get-tuple-element.26), channel_id=1, source_target_pairs={{0,16},{8,24},{16,0},{24,8},{1,17},{9,25},{17,1},{25,9},{2,18},{10... | collective-permute-start | bytes 884744 | tf_op jit(solution)/shard_map/ppermute | solution.py:18
  109.2 14.6 %collective-permute-start.16 = (bf16[64,2304]{1,0:T(8,128)(2,1)S(1)}, bf16[64,2304]{1,0:T(8,128)(2,1)S(1)}, u32[]{:S(2)}, u32[]{:S(2)}) collective-permute-start(bf16[64,2304]{1,0:T(8,128)(2,1)S(1)} %get-tuple-element.27), channel_id=1, source_target_pairs={{0,8},{8,16},{16,24},{24,0},{1,9},{9,17},{17,25},{25,1},{2,10},{10... | collective-permute-start | bytes 884744 | tf_op jit(solution)/shard_map/ppermute | solution.py:18
  118.1 12.8 %collective-permute-start.20 = (bf16[64,2304]{1,0:T(8,128)(2,1)S(1)}, bf16[64,2304]{1,0:T(8,128)(2,1)S(1)}, u32[]{:S(2)}, u32[]{:S(2)}) collective-permute-start(bf16[64,2304]{1,0:T(8,128)(2,1)S(1)} %get-tuple-element.29), channel_id=1, source_target_pairs={{0,192},{64,0},{128,64},{192,128},{1,193},{65,1},{129,65},{193,129... | collective-permute-start | bytes 884744 | tf_op jit(solution)/shard_map/ppermute | solution.py:18
  119.3 15.8 %collective-permute-start.21 = (bf16[64,2304]{1,0:T(8,128)(2,1)S(1)}, bf16[64,2304]{1,0:T(8,128)(2,1)S(1)}, u32[]{:S(2)}, u32[]{:S(2)}) collective-permute-start(bf16[64,2304]{1,0:T(8,128)(2,1)S(1)} %get-tuple-element.30), channel_id=1, source_target_pairs={{0,128},{64,192},{128,0},{192,64},{1,129},{65,193},{129,1},{193,65... | collective-permute-start | bytes 884744 | tf_op jit(solution)/shard_map/ppermute | solution.py:18
  121.0 15.0 %collective-permute-start.22 = (bf16[64,2304]{1,0:T(8,128)(2,1)S(1)}, bf16[64,2304]{1,0:T(8,128)(2,1)S(1)}, u32[]{:S(2)}, u32[]{:S(2)}) collective-permute-start(bf16[64,2304]{1,0:T(8,128)(2,1)S(1)} %get-tuple-element.31), channel_id=1, source_target_pairs={{0,64},{64,128},{128,192},{192,0},{1,65},{65,129},{129,193},{193,1... | collective-permute-start | bytes 884744 | tf_op jit(solution)/shard_map/ppermute | solution.py:18
  124.0 15.6 %collective-permute-start.17 = (bf16[16,2304]{1,0:T(8,128)(2,1)S(1)}, bf16[16,2304]{1,0:T(8,128)(2,1)S(1)}, u32[]{:S(2)}, u32[]{:S(2)}) collective-permute-start(bf16[16,2304]{1,0:T(8,128)(2,1)S(1)} %get-tuple-element.38), channel_id=1, source_target_pairs={{0,192},{64,0},{128,64},{192,128},{1,193},{65,1},{129,65},{193,129... | collective-permute-start | bytes 221192 | tf_op jit(solution)/shard_map/ppermute | solution.py:18
  125.0 15.6 %collective-permute-start.18 = (bf16[16,2304]{1,0:T(8,128)(2,1)S(1)}, bf16[16,2304]{1,0:T(8,128)(2,1)S(1)}, u32[]{:S(2)}, u32[]{:S(2)}) collective-permute-start(bf16[16,2304]{1,0:T(8,128)(2,1)S(1)} %get-tuple-element.40), channel_id=1, source_target_pairs={{0,128},{64,192},{128,0},{192,64},{1,129},{65,193},{129,1},{193,65... | collective-permute-start | bytes 221192 | tf_op jit(solution)/shard_map/ppermute | solution.py:18
  130.9 9.7 %collective-permute-start.19 = (bf16[16,2304]{1,0:T(8,128)(2,1)S(1)}, bf16[16,2304]{1,0:T(8,128)(2,1)S(1)}, u32[]{:S(2)}, u32[]{:S(2)}) collective-permute-start(bf16[16,2304]{1,0:T(8,128)(2,1)S(1)} %get-tuple-element.39), channel_id=1, source_target_pairs={{0,64},{64,128},{128,192},{192,0},{1,65},{65,129},{129,193},{193,1... | collective-permute-start | bytes 221192 | tf_op jit(solution)/shard_map/ppermute | solution.py:18
  136.2 4.4 %collective-permute-start.23 = (bf16[16,2304]{1,0:T(8,128)(2,1)S(1)}, bf16[16,2304]{1,0:T(8,128)(2,1)S(1)}, u32[]{:S(2)}, u32[]{:S(2)}) collective-permute-start(bf16[16,2304]{1,0:T(8,128)(2,1)S(1)} %get-tuple-element.41), channel_id=1, source_target_pairs={{0,24},{8,0},{16,8},{24,16},{1,25},{9,1},{17,9},{25,17},{2,26},{10... | collective-permute-start | bytes 221192 | tf_op jit(solution)/shard_map/ppermute | solution.py:18
  136.4 6.8 %collective-permute-start.24 = (bf16[16,2304]{1,0:T(8,128)(2,1)S(1)}, bf16[16,2304]{1,0:T(8,128)(2,1)S(1)}, u32[]{:S(2)}, u32[]{:S(2)}) collective-permute-start(bf16[16,2304]{1,0:T(8,128)(2,1)S(1)} %get-tuple-element.43), channel_id=1, source_target_pairs={{0,16},{8,24},{16,0},{24,8},{1,17},{9,25},{17,1},{25,9},{2,18},{10... | collective-permute-start | bytes 221192 | tf_op jit(solution)/shard_map/ppermute | solution.py:18
  139.6 4.4 %collective-permute-start.25 = (bf16[16,2304]{1,0:T(8,128)(2,1)S(1)}, bf16[16,2304]{1,0:T(8,128)(2,1)S(1)}, u32[]{:S(2)}, u32[]{:S(2)}) collective-permute-start(bf16[16,2304]{1,0:T(8,128)(2,1)S(1)} %get-tuple-element.42), channel_id=1, source_target_pairs={{0,8},{8,16},{16,24},{24,0},{1,9},{9,17},{17,25},{25,1},{2,10},{10... | collective-permute-start | bytes 221192 | tf_op jit(solution)/shard_map/ppermute | solution.py:18

commit v4 on v3

--- a/solution.py
+++ b/solution.py
@@ -79,13 +79,13 @@
     n = len(late)
     vocab, width = own.shape
     plane = n * late[0].shape[0]
-    vmem, anywhere = pl.BlockSpec(memory_space=pltpu.VMEM), pl.BlockSpec(memory_space=pl.ANY)
+    vmem, hbm = pl.BlockSpec(memory_space=pltpu.VMEM), pl.BlockSpec(memory_space=pltpu.HBM)
     capped = jax.ShapeDtypeStruct((plane, vocab), jnp.float32)
     sums = jax.ShapeDtypeStruct((plane, TAIL), jnp.float32)
     return pl.pallas_call(
         functools.partial(logits_kernel, n),
         out_shape=(sums, capped, capped),
-        in_specs=[pl.BlockSpec(memory_space=pltpu.SMEM)] + [vmem] * (2 * n) + [anywhere] * 2,
+        in_specs=[pl.BlockSpec(memory_space=pltpu.SMEM)] + [vmem] * (2 * n) + [hbm] * 2,
         out_specs=(vmem,) * 3,
         scratch_shapes=[
             pltpu.VMEM((vocab, width), jnp.bfloat16),
@@ -101,19 +101,14 @@
     )(where, *late, *early, own, sib)
 
 
-def labels_kernel(n, where_ref, *refs):
-    late = refs[:n]
-    tail_ref, sums_ref, own_c, sib_c, rows_ref, own_tail, sib_tail = refs[n:]
+def labels_kernel(n, where_ref, own_ref, sib_ref, sums_ref, own_c, sib_c, rows_ref, own_tail, sib_tail):
     plane, vocab = own_c.shape
-    half = late[0].shape[1] - TAIL
     rows = plane // (n * n)
-    for e in range(n):
-        for d in range(n):
-            i = e * n + d
-            at = pl.ds(pl.multiple_of(where_ref[i] * rows, rows), rows)
-            own_tail[at, :] = late[e][d * rows : (d + 1) * rows, half:].astype(jnp.float32)
-            at = pl.ds(pl.multiple_of(where_ref[n * n + 2 + i] * rows, rows), rows)
-            sib_tail[at, :] = tail_ref[i * rows : (i + 1) * rows, :].astype(jnp.float32)
+    for i in range(n * n):
+        here = slice(i * rows, (i + 1) * rows)
+        own_tail[pl.ds(pl.multiple_of(where_ref[i] * rows, rows), rows), :] = own_ref[here, :].astype(jnp.float32)
+        at = pl.ds(pl.multiple_of(where_ref[n * n + 2 + i] * rows, rows), rows)
+        sib_tail[at, :] = sib_ref[here, :].astype(jnp.float32)
     labels = sib_tail[:, 0:1] + 256.0 * sib_tail[:, 1:2] + 65536.0 * sib_tail[:, 2:3]
     picked = 0.0
     for j, capped in enumerate((own_c, sib_c)):
@@ -127,18 +122,17 @@
     rows_ref[...] = columns.T
 
 
-def labels_and_sums(where, late, tail, sums, own_c, sib_c):
-    n = len(late)
+def labels_and_sums(n, where, own_tail, sib_tail, sums, own_c, sib_c):
     plane = own_c.shape[0]
     vmem = pl.BlockSpec(memory_space=pltpu.VMEM)
     return pl.pallas_call(
         functools.partial(labels_kernel, n),
         out_shape=jax.ShapeDtypeStruct((8, plane), jnp.float32),
-        in_specs=[pl.BlockSpec(memory_space=pltpu.SMEM)] + [vmem] * (n + 4),
+        in_specs=[pl.BlockSpec(memory_space=pltpu.SMEM)] + [vmem] * 5,
         out_specs=vmem,
         scratch_shapes=[pltpu.VMEM((plane, TAIL), jnp.float32)] * 2,
-        compiler_params=pltpu.CompilerParams(vmem_limit_bytes=16 * 1024 * 1024),
-    )(where, *late, tail, sums, own_c, sib_c)
+        compiler_params=pltpu.CompilerParams(vmem_limit_bytes=8 * 1024 * 1024),
+    )(where, own_tail, sib_tail, sums, own_c, sib_c)
 
 
 def gradient_kernel(n, where_ref, rows_ref, own_c, sib_c, own_ref, sib_ref, *refs):
@@ -168,15 +162,13 @@
         outs[i][...] = part[i * n * rows : (i + 1) * n * rows, :]
 
 
-def gradient_half(n, where, rows, own_c, sib_c, own, sib, second):
+def gradient_part(n, where, rows, own_c, sib_c, own, sib, start, size):
     plane, vocab = own_c.shape
-    half = own.shape[1] // 2
-    chunk = 1152 if half % 1152 == 0 else 128
-    steps = half // chunk
-    skip = steps if second else 0
+    chunk = next(c for c in range(1152, 0, -128) if size % c == 0 and start % c == 0)
+    steps, skip = size // chunk, start // chunk
     whole = lambda a: pl.BlockSpec(a.shape, lambda i: (0, 0))
     block = pl.BlockSpec((vocab, chunk), lambda i: (0, i + skip))
-    piece = jax.ShapeDtypeStruct((plane // n, half), jnp.bfloat16)
+    piece = jax.ShapeDtypeStruct((plane // n, size), jnp.bfloat16)
     return pl.pallas_call(
         functools.partial(gradient_kernel, n),
         grid=(steps,),
@@ -190,7 +182,7 @@
         ],
         compiler_params=pltpu.CompilerParams(vmem_limit_bytes=VMEM_BYTES),
         cost_estimate=pl.CostEstimate(
-            flops=4 * plane * vocab * half, bytes_accessed=4 * vocab * half + 2 * plane * half, transcendentals=0
+            flops=4 * plane * vocab * size, bytes_accessed=4 * vocab * size + 2 * plane * size, transcendentals=0
         ),
     )(where, rows, own_c, sib_c, own, sib)
 
@@ -224,7 +216,8 @@
     along_x, along_y = lax.optimization_barrier((along_x, along_y))
     late = [along_y] + [shifted(along_y, "x", e) for e in range(1, n)]
     early = [along_x] + [shifted(along_x, "y", d) for d in range(1, n)]
-    tail_sib = lax.ppermute(jnp.concatenate([v[:, half:] for v in late]), "core", [(0, 1), (1, 0)])
+    tail_own = jnp.concatenate([v[:, half:] for v in late])
+    tail_sib = lax.ppermute(tail_own, "core", [(0, 1), (1, 0)])
 
     device = lax.axis_index(ALL)
     bases = vocab * jnp.stack([device, device + (1 - 2 * core) * ny * nz])
@@ -235,7 +228,7 @@
     where_yx = jnp.concatenate([places.T.ravel(), bases]).astype(i32)
 
     sums, own_c, sib_c = capped_logits(where_xy, late, early, unembed, unembed_sib)
-    known = labels_and_sums(where_xy, late, tail_sib, sums, own_c, sib_c)
+    known = labels_and_sums(n, where_xy, tail_own, tail_sib, sums, own_c, sib_c)
     stats = gather(known[:2].reshape(2 * plane // 128, 128), ("x", "y", "z"))
     labels, weights = known[2], known[3]
     by_x = lambda v: jnp.sum(v.reshape(nx, per_x), axis=1)
@@ -248,12 +241,14 @@
     lse = SOFTCAP + jnp.log(total)
     rows = jnp.stack([lse, coef, labels] + [jnp.zeros_like(lse)] * 5)
 
-    to_x = gradient_half(n, where_xy, rows, own_c, sib_c, unembed, unembed_sib, True)
-    to_y = gradient_half(n, where_yx, rows, own_c, sib_c, unembed, unembed_sib, False)
+    split = half
+    to_x = gradient_part(n, where_xy, rows, own_c, sib_c, unembed, unembed_sib, 0, split)
+    to_y = gradient_part(n, where_yx, rows, own_c, sib_c, unembed, unembed_sib, split, width - split)
+    to_y, lse, picked = lax.optimization_barrier((to_y, lse, picked))
     got_x = [to_x[0]] + [shifted(to_x[e], "x", -e) for e in range(1, n)]
     got_y = [to_y[0]] + [shifted(to_y[d], "y", -d) for d in range(1, n)]
 
-    sums = jnp.sum((weights * (lse - picked)).reshape(nx, per_x), axis=1)
+    sums = by_x(weights * (lse - picked))
     sums = jnp.where(core == 0, sums, jnp.roll(sums, 1))
     losses = (sums + lax.ppermute(sums, "core", [(0, 1), (1, 0)])) / counts
 
@@ -261,7 +256,7 @@
     cut = lambda v, i: v[i * nz * own_rows : (i + 1) * nz * own_rows]
     got_y = [cut(part_x, 0)] + [shifted(cut(part_x, d), "y", -d) for d in range(1, n)]
     got_x = [cut(part_y, 0)] + [shifted(cut(part_y, e), "x", -e) for e in range(1, n)]
-    part = jnp.concatenate([summed(got_x), summed(got_y)], axis=1).reshape(nz, own_rows, width)
+    part = jnp.concatenate([summed(got_y), summed(got_x)], axis=1).reshape(nz, own_rows, width)
     got = lax.all_to_all(part, "z", 0, 0, tiled=True)
     return jnp.sum(got.astype(f32), axis=0), losses
 

time: 158 us -> 150 us (0.949)
  blocking collectives: 11.6 us -> 0 us
  waiting for transfers between devices: 46.9 us -> 52.9 us
    all_to_all x1 -> x0, blocking collectives: 11.6 us -> none  [body(): got = lax.all_to_all(part, 'z', 0, 0, tiled=True)]
    all_to_all x0 -> x1, waiting for transfers between devices: none -> 6.78 us  [body(): got = lax.all_to_all(part, 'z', 0, 0, tiled=True)]
    ppermute x24, starting transfers between devices: 38.1 us -> 34.7 us  [shifted(): return lax.ppermute(v, axis, [(i, (i + by) % n) for i in range(n)])]
    all_to_all x0 -> x1, starting transfers between devices: none -> 3.38 us  [body(): got = lax.all_to_all(part, 'z', 0, 0, tiled=True)]
    unnamed x13 -> x9, local copies, waits for them, and re-layouts: 4.49 us -> 2.56 us
  transfers between devices with their start and end apart: 29 -> 30, of which waited for: 15 -> 16; matrix products, arithmetic and copies ran while one was open for 3% -> 4% of each run, Pallas kernels for 11% -> 12%
where the time goes in v4:
time: 150 us
  starting transfers between devices  56.6 us (38%)
  waiting for transfers between devices  52.9 us (35%)
  Pallas kernels  26.1 us (17%)
  local copies, waits for them, and re-layouts  6.81 us (5%)
  other arithmetic  5.56 us (4%)
  between operations  1.55 us (1%)
    ppermute x24, starting transfers between devices, shifted(): return lax.ppermute(v, axis, [(i, (i + by) % n) for i in range(n)])  34.7 us
    ppermute x24, waiting for transfers between devices, shifted(): return lax.ppermute(v, axis, [(i, (i + by) % n) for i in range(n)])  23.8 us
    all_to_all x2, waiting for transfers between devices, gather(): lax.all_to_all(jnp.broadcast_to(v[None], (peers, *v.shape)), axis, 0, 0,...  21.2 us
    all_to_all x2, starting transfers between devices, gather(): lax.all_to_all(jnp.broadcast_to(v[None], (peers, *v.shape)), axis, 0, 0,...  18.2 us
    pallas_call x2, Pallas kernels, gradient_part(): pl.pallas_call(functools.partial(gradient_kernel, n), grid=(steps,), out_...  14.5 us
    pallas_call x1, Pallas kernels, capped_logits(): pl.pallas_call(functools.partial(logits_kernel, n), out_shape=(sums, capp...  10.4 us
    all_to_all x1, waiting for transfers between devices, body(): got = lax.all_to_all(part, 'z', 0, 0, tiled=True)  6.78 us
    all_to_all x1, starting transfers between devices, body(): got = lax.all_to_all(part, 'z', 0, 0, tiled=True)  3.38 us
  transfers between devices with their start and end apart: 30, of which 16 were waited for; matrix products, arithmetic and copies ran while one was open for 4% of the time, Pallas kernels for 12%

profile of v4, /device:TPU:8, one launch (start us, length us, event | category | flops | bytes accessed | tf_op | source)
XLA Modules:
  0.0 149.6 jit_solution(8665353455507085076)
XLA Ops:
  0.7 0.7 fusion.4
  1.6 0.7 fusion
  2.3 0.7 broadcast_in_dim.8
  3.0 8.5 %all-to-all-start = ((bf16[8,2,4736]{2,1,0:T(2,128)(2,1)}), bf16[8,2,4736]{2,1,0:T(2,128)(2,1)S(1)}, u32[]{:S(2)}, u32[]{:S(2)}) async-start(bf16[8,2,4736]{2,1,0:T(2,128)(2,1)} %broadcast_in_dim.8), calls=%async_computation | async-start | bytes 303104 | tf_op jit(solution)/shard_map/all_to_all | solution.py:23
  11.5 10.1 %all-to-all-done = bf16[8,2,4736]{2,1,0:T(2,128)(2,1)S(1)} async-done(((bf16[8,2,4736]{2,1,0:T(2,128)(2,1)}), bf16[8,2,4736]{2,1,0:T(2,128)(2,1)S(1)}, u32[]{:S(2)}, u32[]{:S(2)}) %all-to-all-start) | async-done | bytes 151584 | tf_op jit(solution)/shard_map/all_to_all | solution.py:23
  21.7 1.6 %collective-permute-start.1 = (bf16[16,2304]{1,0:T(8,128)(2,1)S(1)}, bf16[16,2304]{1,0:T(8,128)(2,1)S(1)}, u32[]{:S(2)}, u32[]{:S(2)}) collective-permute-start(bf16[16,2304]{1,0:T(8,128)(2,1)S(1)} %slice.78), channel_id=1, source_target_pairs={{0,64},{64,128},{128,192},{192,0},{1,65},{65,129},{129,193},{193,1... | collective-permute-start | bytes 221192 | tf_op jit(solution)/shard_map/ppermute | solution.py:18
  23.3 2.7 %collective-permute-start.2 = (bf16[16,2304]{1,0:T(8,128)(2,1)S(1)}, bf16[16,2304]{1,0:T(8,128)(2,1)S(1)}, u32[]{:S(2)}, u32[]{:S(2)}) collective-permute-start(bf16[16,2304]{1,0:T(8,128)(2,1)S(1)} %slice.78), channel_id=1, source_target_pairs={{0,128},{64,192},{128,0},{192,64},{1,129},{65,193},{129,1},{193,65... | collective-permute-start | bytes 221192 | tf_op jit(solution)/shard_map/ppermute | solution.py:18
  26.0 1.4 collective-permute-start.3
  27.5 1.7 %collective-permute-start.4 = (bf16[16,2432]{1,0:T(8,128)(2,1)S(1)}, bf16[16,2432]{1,0:T(8,128)(2,1)S(1)}, u32[]{:S(2)}, u32[]{:S(2)}) collective-permute-start(bf16[16,2432]{1,0:T(8,128)(2,1)S(1)} %slice.79), channel_id=1, source_target_pairs={{0,8},{8,16},{16,24},{24,0},{1,9},{9,17},{17,25},{25,1},{2,10},{10... | collective-permute-start | bytes 233480 | tf_op jit(solution)/shard_map/ppermute | solution.py:18
  29.2 0.9 collective-permute-start.5
  30.1 2.4 %collective-permute-start.6 = (bf16[16,2432]{1,0:T(8,128)(2,1)S(1)}, bf16[16,2432]{1,0:T(8,128)(2,1)S(1)}, u32[]{:S(2)}, u32[]{:S(2)}) collective-permute-start(bf16[16,2432]{1,0:T(8,128)(2,1)S(1)} %slice.79), channel_id=1, source_target_pairs={{0,24},{8,0},{16,8},{24,16},{1,25},{9,1},{17,9},{25,17},{2,26},{10... | collective-permute-start | bytes 233480 | tf_op jit(solution)/shard_map/ppermute | solution.py:18
  32.6 2.5 %collective-permute-done.5 = bf16[16,2432]{1,0:T(8,128)(2,1)S(1)} collective-permute-done((bf16[16,2432]{1,0:T(8,128)(2,1)S(1)}, bf16[16,2432]{1,0:T(8,128)(2,1)S(1)}, u32[]{:S(2)}, u32[]{:S(2)}) %collective-permute-start.5) | collective-permute-done | bytes 77856 | tf_op jit(solution)/shard_map/ppermute | solution.py:18
  35.2 0.2 collective-permute-done.6
  35.4 0.7 collective-permute-start.7
  37.0 0.9 collective-permute-start.8
  37.9 1.9 %collective-permute-start.9 = (bf16[64,2432]{1,0:T(8,128)(2,1)S(1)}, bf16[64,2432]{1,0:T(8,128)(2,1)S(1)}, u32[]{:S(2)}, u32[]{:S(2)}) collective-permute-start(bf16[64,2432]{1,0:T(8,128)(2,1)S(1)} %pad_maximum_fusion.refs_0_), channel_id=1, source_target_pairs={{0,192},{64,0},{128,64},{192,128},{1,193},{65,1},{129,65},{193,129... | collective-permute-start | bytes 933896 | tf_op jit(solution)/shard_map/ppermute | solution.py:18
  39.9 1.1 collective-permute-start.11
  41.0 2.5 %collective-permute-start.12 = (bf16[64,2304]{1,0:T(8,128)(2,1)S(1)}, bf16[64,2304]{1,0:T(8,128)(2,1)S(1)}, u32[]{:S(2)}, u32[]{:S(2)}) collective-permute-start(bf16[64,2304]{1,0:T(8,128)(2,1)S(1)} %pad_maximum_fusion.1.refs_4_), channel_id=1, source_target_pairs={{0,16},{8,24},{16,0},{24,8},{1,17},{9,25},{17,1},{25,9},{2,18},{10... | collective-permute-start | bytes 884744 | tf_op jit(solution)/shard_map/ppermute | solution.py:18
  43.5 6.0 %collective-permute-done.7.refs_1_ = bf16[64,2432]{1,0:T(8,128)(2,1)S(1)} collective-permute-done((bf16[64,2432]{1,0:T(8,128)(2,1)S(1)}, bf16[64,2432]{1,0:T(8,128)(2,1)S(1)}, u32[]{:S(2)}, u32[]{:S(2)}) %collective-permute-start.7) | collective-permute-done | bytes 311328 | tf_op jit(solution)/shard_map/ppermute | solution.py:18
  49.5 1.4 collective-permute-start.13
  51.2 0.3 collective-permute-start.10
  51.5 0.2 collective-permute-done.12.refs_6_
  51.6 4.6 %collective-permute-done.13.refs_7_ = bf16[64,2304]{1,0:T(8,128)(2,1)S(1)} collective-permute-done((bf16[64,2304]{1,0:T(8,128)(2,1)S(1)}, bf16[64,2304]{1,0:T(8,128)(2,1)S(1)}, u32[]{:S(2)}, u32[]{:S(2)}) %collective-permute-start.13) | collective-permute-done | bytes 294944 | tf_op jit(solution)/shard_map/ppermute | solution.py:18
  56.2 10.4 %shard_map.68 = (f32[256,128]{1,0:T(8,128)S(1)}, f32[256,1000]{1,0:T(8,128)}, f32[256,1000]{1,0:T(8,128)}) custom-call(s32[34]{0:T(128)S(1)} %pad_add_fusion.where_ref, bf16[64,2432]{1,0:T(8,128)(2,1)S(1)} %pad_maximum_fusion.refs_0_, bf16[64,2432]{1,0:T(8,128)(2,1)S(1)} %collective-permute-done.7.refs_1_, bf16[64,2432]{1,0:T(8,128)(2,1)} %copy-done.2, ...), custom_call_target="tpu_custom_call" | custom-call | flops 4718592000 | bytes 23150592 | tf_op jit(solution)/shard_map/pallas_call | solution.py:85
  66.7 1.2 copy-done
  67.9 1.2 copy-done.1
  69.1 1.2 shard_map.69
  70.5 0.1 reduce_sum.47
  70.6 0.6 slice.87
  71.4 0.7 broadcast_in_dim.10
  72.1 9.7 %all-to-all-start.1 = ((f32[128,4,128]{2,1,0:T(4,128)}), f32[128,4,128]{2,1,0:T(4,128)S(1)}, u32[]{:S(2)}, u32[]{:S(2)}) async-start(f32[128,4,128]{2,1,0:T(4,128)} %broadcast_in_dim.10), calls=%async_computation.1 | async-start | bytes 524288 | tf_op jit(solution)/shard_map/all_to_all | solution.py:23
  81.8 0.7 fusion.1
  82.9 11.1 %all-to-all-done.1 = f32[128,4,128]{2,1,0:T(4,128)S(1)} async-done(((f32[128,4,128]{2,1,0:T(4,128)}), f32[128,4,128]{2,1,0:T(4,128)S(1)}, u32[]{:S(2)}, u32[]{:S(2)}) %all-to-all-start.1) | async-done | bytes 262176 | tf_op jit(solution)/shard_map/all_to_all | solution.py:23
  94.0 0.1 reduce_sum.45
  94.2 7.3 %shard_map.70 = (bf16[64,2304]{1,0:T(8,128)(2,1)S(1)}, bf16[64,2304]{1,0:T(8,128)(2,1)S(1)}, bf16[64,2304]{1,0:T(8,128)(2,1)S(1)}, bf16[64,2304]{1,0:T(8,128)(2,1)S(1)}) custom-call(s32[34]{0:T(128)S(1)} %pad_add_fusion.where_ref, f32[8,256]{1,0:T(8,128)S(1)} %stack.46.rows_ref, f32[256,1000]{1,0:T(8,128)} %get-tuple-element.28.own_c, ...), custom_call_target="tpu_custom_call" | custom-call | flops 2359296000 | bytes 10395648 | tf_op jit(solution)/shard_map/pallas_call | solution.py:172
  101.4 0.9 collective-permute-start.14
  102.3 1.9 %collective-permute-start.15 = (bf16[64,2304]{1,0:T(8,128)(2,1)S(1)}, bf16[64,2304]{1,0:T(8,128)(2,1)S(1)}, u32[]{:S(2)}, u32[]{:S(2)}) collective-permute-start(bf16[64,2304]{1,0:T(8,128)(2,1)S(1)} %get-tuple-element.32), channel_id=1, source_target_pairs={{0,128},{64,192},{128,0},{192,64},{1,129},{65,193},{129,1},{193,65... | collective-permute-start | bytes 884744 | tf_op jit(solution)/shard_map/ppermute | solution.py:18
  104.2 0.3 collective-permute-start.16
  104.5 7.2 %shard_map.71 = (bf16[64,2304]{1,0:T(8,128)(2,1)S(1)}, bf16[64,2304]{1,0:T(8,128)(2,1)S(1)}, bf16[64,2304]{1,0:T(8,128)(2,1)S(1)}, bf16[64,2304]{1,0:T(8,128)(2,1)S(1)}) custom-call(s32[18]{0:T(128)S(1)} %pad_add_fusion.1.where_ref, f32[8,256]{1,0:T(8,128)S(1)} %stack.46.rows_ref, f32[256,1000]{1,0:T(8,128)} %get-tuple-element.28.own_c, ...), custom_call_target="tpu_custom_call" | custom-call | flops 2359296000 | bytes 10395648 | tf_op jit(solution)/shard_map/pallas_call | solution.py:172
  112.0 0.6 slice.100
  112.5 1.4 collective-permute-start.20
  114.0 0.9 collective-permute-start.21
  114.9 1.7 %collective-permute-start.22 = (bf16[64,2304]{1,0:T(8,128)(2,1)S(1)}, bf16[64,2304]{1,0:T(8,128)(2,1)S(1)}, u32[]{:S(2)}, u32[]{:S(2)}) collective-permute-start(bf16[64,2304]{1,0:T(8,128)(2,1)S(1)} %get-tuple-element.41), channel_id=1, source_target_pairs={{0,8},{8,16},{16,24},{24,0},{1,9},{9,17},{17,25},{25,1},{2,10},{10... | collective-permute-start | bytes 884744 | tf_op jit(solution)/shard_map/ppermute | solution.py:18
  116.6 0.1 add_convert_fusion.1
  116.8 0.4 collective-permute-start.17
  117.2 2.6 %collective-permute-start.18 = (bf16[16,2304]{1,0:T(8,128)(2,1)S(1)}, bf16[16,2304]{1,0:T(8,128)(2,1)S(1)}, u32[]{:S(2)}, u32[]{:S(2)}) collective-permute-start(bf16[16,2304]{1,0:T(8,128)(2,1)S(1)} %get-tuple-element.48), channel_id=1, source_target_pairs={{0,16},{8,24},{16,0},{24,8},{1,17},{9,25},{17,1},{25,9},{2,18},{10... | collective-permute-start | bytes 221192 | tf_op jit(solution)/shard_map/ppermute | solution.py:18
  119.8 1.5 collective-permute-done.20
  121.3 0.6 collective-permute-start.19
  121.9 2.7 %collective-permute-done.21 = bf16[64,2304]{1,0:T(8,128)(2,1)S(1)} collective-permute-done((bf16[64,2304]{1,0:T(8,128)(2,1)S(1)}, bf16[64,2304]{1,0:T(8,128)(2,1)S(1)}, u32[]{:S(2)}, u32[]{:S(2)}) %collective-permute-start.21) | collective-permute-done | bytes 294944 | tf_op jit(solution)/shard_map/ppermute | solution.py:18
  124.6 1.1 collective-permute-done.22
  125.7 0.1 add_convert_fusion
  125.9 3.0 %collective-permute-start.23 = (bf16[16,2304]{1,0:T(8,128)(2,1)S(1)}, bf16[16,2304]{1,0:T(8,128)(2,1)S(1)}, u32[]{:S(2)}, u32[]{:S(2)}) collective-permute-start(bf16[16,2304]{1,0:T(8,128)(2,1)S(1)} %get-tuple-element.49), channel_id=1, source_target_pairs={{0,192},{64,0},{128,64},{192,128},{1,193},{65,1},{129,65},{193,129... | collective-permute-start | bytes 221192 | tf_op jit(solution)/shard_map/ppermute | solution.py:18
  128.9 0.3 collective-permute-start.24
  129.2 1.3 collective-permute-start.25
  130.6 0.3 collective-permute-done.23
  130.9 4.0 %collective-permute-done.24 = bf16[16,2304]{1,0:T(8,128)(2,1)S(1)} collective-permute-done((bf16[16,2304]{1,0:T(8,128)(2,1)S(1)}, bf16[16,2304]{1,0:T(8,128)(2,1)S(1)}, u32[]{:S(2)}, u32[]{:S(2)}) %collective-permute-start.24) | collective-permute-done | bytes 73760 | tf_op jit(solution)/shard_map/ppermute | solution.py:18
  134.8 0.7 collective-permute-done.25
  135.6 0.7 reshape.105
  136.3 3.4 %all-to-all-start.2 = ((bf16[8,2,4608]{2,1,0:T(2,128)(2,1)}), bf16[8,2,4608]{2,1,0:T(2,128)(2,1)S(1)}, u32[]{:S(2)}, u32[]{:S(2)}) async-start(bf16[8,2,4608]{2,1,0:T(2,128)(2,1)} %reshape.105), calls=%async_computation.2 | async-start | bytes 294912 | tf_op jit(solution)/shard_map/all_to_all | solution.py:260
  139.7 0.7 broadcast_select_fusion
  140.4 1.1 collective-permute-done.26
  141.5 0.5 add_divide_fusion
  142.1 6.8 %all-to-all-done.2 = bf16[8,2,4608]{2,1,0:T(2,128)(2,1)S(1)} async-done(((bf16[8,2,4608]{2,1,0:T(2,128)(2,1)}), bf16[8,2,4608]{2,1,0:T(2,128)(2,1)S(1)}, u32[]{:S(2)}, u32[]{:S(2)}) %all-to-all-start.2) | async-done | bytes 147488 | tf_op jit(solution)/shard_map/all_to_all | solution.py:260
  148.8 0.7 convert_reduce_fusion
  (67 shorter events, 2.2 us)
Async XLA Ops:
  0.6 21.1 %collective-permute-start = (bf16[1000,4608]{1,0:T(8,128)(2,1)}, bf16[1000,4608]{1,0:T(8,128)(2,1)}, u32[]{:S(2)}, u32[]{:S(2)}) collective-permute-start(bf16[1000,4608]{1,0:T(8,128)(2,1)} %own_ref.3), channel_id=1, source_target_pairs={{0,32},{32,0},{1,33},{33,1},{2,34},{34,2},{3,35},{35,3},{4,36},{36... | collective-permute-start | bytes 27648008 | tf_op jit(solution)/shard_map/ppermute | solution.py:205
  3.0 18.6 %all-to-all-start = ((bf16[8,2,4736]{2,1,0:T(2,128)(2,1)}), bf16[8,2,4736]{2,1,0:T(2,128)(2,1)S(1)}, u32[]{:S(2)}, u32[]{:S(2)}) async-start(bf16[8,2,4736]{2,1,0:T(2,128)(2,1)} %broadcast_in_dim.8), calls=%async_computation | async-start | bytes 303104 | tf_op jit(solution)/shard_map/all_to_all | solution.py:23
  21.7 8.4 %collective-permute-start.1 = (bf16[16,2304]{1,0:T(8,128)(2,1)S(1)}, bf16[16,2304]{1,0:T(8,128)(2,1)S(1)}, u32[]{:S(2)}, u32[]{:S(2)}) collective-permute-start(bf16[16,2304]{1,0:T(8,128)(2,1)S(1)} %slice.78), channel_id=1, source_target_pairs={{0,64},{64,128},{128,192},{192,0},{1,65},{65,129},{129,193},{193,1... | collective-permute-start | bytes 221192 | tf_op jit(solution)/shard_map/ppermute | solution.py:18
  23.3 9.2 %collective-permute-start.2 = (bf16[16,2304]{1,0:T(8,128)(2,1)S(1)}, bf16[16,2304]{1,0:T(8,128)(2,1)S(1)}, u32[]{:S(2)}, u32[]{:S(2)}) collective-permute-start(bf16[16,2304]{1,0:T(8,128)(2,1)S(1)} %slice.78), channel_id=1, source_target_pairs={{0,128},{64,192},{128,0},{192,64},{1,129},{65,193},{129,1},{193,65... | collective-permute-start | bytes 221192 | tf_op jit(solution)/shard_map/ppermute | solution.py:18
  26.0 6.5 %collective-permute-start.3 = (bf16[16,2304]{1,0:T(8,128)(2,1)S(1)}, bf16[16,2304]{1,0:T(8,128)(2,1)S(1)}, u32[]{:S(2)}, u32[]{:S(2)}) collective-permute-start(bf16[16,2304]{1,0:T(8,128)(2,1)S(1)} %slice.78), channel_id=1, source_target_pairs={{0,192},{64,0},{128,64},{192,128},{1,193},{65,1},{129,65},{193,129... | collective-permute-start | bytes 221192 | tf_op jit(solution)/shard_map/ppermute | solution.py:18
  27.5 5.1 %collective-permute-start.4 = (bf16[16,2432]{1,0:T(8,128)(2,1)S(1)}, bf16[16,2432]{1,0:T(8,128)(2,1)S(1)}, u32[]{:S(2)}, u32[]{:S(2)}) collective-permute-start(bf16[16,2432]{1,0:T(8,128)(2,1)S(1)} %slice.79), channel_id=1, source_target_pairs={{0,8},{8,16},{16,24},{24,0},{1,9},{9,17},{17,25},{25,1},{2,10},{10... | collective-permute-start | bytes 233480 | tf_op jit(solution)/shard_map/ppermute | solution.py:18
  29.2 6.0 %collective-permute-start.5 = (bf16[16,2432]{1,0:T(8,128)(2,1)S(1)}, bf16[16,2432]{1,0:T(8,128)(2,1)S(1)}, u32[]{:S(2)}, u32[]{:S(2)}) collective-permute-start(bf16[16,2432]{1,0:T(8,128)(2,1)S(1)} %slice.79), channel_id=1, source_target_pairs={{0,16},{8,24},{16,0},{24,8},{1,17},{9,25},{17,1},{25,9},{2,18},{10... | collective-permute-start | bytes 233480 | tf_op jit(solution)/shard_map/ppermute | solution.py:18
  30.1 5.2 %collective-permute-start.6 = (bf16[16,2432]{1,0:T(8,128)(2,1)S(1)}, bf16[16,2432]{1,0:T(8,128)(2,1)S(1)}, u32[]{:S(2)}, u32[]{:S(2)}) collective-permute-start(bf16[16,2432]{1,0:T(8,128)(2,1)S(1)} %slice.79), channel_id=1, source_target_pairs={{0,24},{8,0},{16,8},{24,16},{1,25},{9,1},{17,9},{25,17},{2,26},{10... | collective-permute-start | bytes 233480 | tf_op jit(solution)/shard_map/ppermute | solution.py:18
  35.4 14.2 %collective-permute-start.7 = (bf16[64,2432]{1,0:T(8,128)(2,1)S(1)}, bf16[64,2432]{1,0:T(8,128)(2,1)S(1)}, u32[]{:S(2)}, u32[]{:S(2)}) collective-permute-start(bf16[64,2432]{1,0:T(8,128)(2,1)S(1)} %pad_maximum_fusion.refs_0_), channel_id=1, source_target_pairs={{0,64},{64,128},{128,192},{192,0},{1,65},{65,129},{129,193},{193,1... | collective-permute-start | bytes 933896 | tf_op jit(solution)/shard_map/ppermute | solution.py:18
  37.0 14.1 %collective-permute-start.8 = (bf16[64,2432]{1,0:T(8,128)(2,1)S(1)}, bf16[64,2432]{1,0:T(8,128)(2,1)S(1)}, u32[]{:S(2)}, u32[]{:S(2)}) collective-permute-start(bf16[64,2432]{1,0:T(8,128)(2,1)S(1)} %pad_maximum_fusion.refs_0_), channel_id=1, source_target_pairs={{0,128},{64,192},{128,0},{192,64},{1,129},{65,193},{129,1},{193,65... | collective-permute-start | bytes 933896 | tf_op jit(solution)/shard_map/ppermute | solution.py:18
  37.9 13.2 %collective-permute-start.9 = (bf16[64,2432]{1,0:T(8,128)(2,1)S(1)}, bf16[64,2432]{1,0:T(8,128)(2,1)S(1)}, u32[]{:S(2)}, u32[]{:S(2)}) collective-permute-start(bf16[64,2432]{1,0:T(8,128)(2,1)S(1)} %pad_maximum_fusion.refs_0_), channel_id=1, source_target_pairs={{0,192},{64,0},{128,64},{192,128},{1,193},{65,1},{129,65},{193,129... | collective-permute-start | bytes 933896 | tf_op jit(solution)/shard_map/ppermute | solution.py:18
  39.9 11.6 %collective-permute-start.11 = (bf16[64,2304]{1,0:T(8,128)(2,1)S(1)}, bf16[64,2304]{1,0:T(8,128)(2,1)S(1)}, u32[]{:S(2)}, u32[]{:S(2)}) collective-permute-start(bf16[64,2304]{1,0:T(8,128)(2,1)S(1)} %pad_maximum_fusion.1.refs_4_), channel_id=1, source_target_pairs={{0,8},{8,16},{16,24},{24,0},{1,9},{9,17},{17,25},{25,1},{2,10},{10... | collective-permute-start | bytes 884744 | tf_op jit(solution)/shard_map/ppermute | solution.py:18
  41.0 10.6 %collective-permute-start.12 = (bf16[64,2304]{1,0:T(8,128)(2,1)S(1)}, bf16[64,2304]{1,0:T(8,128)(2,1)S(1)}, u32[]{:S(2)}, u32[]{:S(2)}) collective-permute-start(bf16[64,2304]{1,0:T(8,128)(2,1)S(1)} %pad_maximum_fusion.1.refs_4_), channel_id=1, source_target_pairs={{0,16},{8,24},{16,0},{24,8},{1,17},{9,25},{17,1},{25,9},{2,18},{10... | collective-permute-start | bytes 884744 | tf_op jit(solution)/shard_map/ppermute | solution.py:18
  49.5 6.7 %collective-permute-start.13 = (bf16[64,2304]{1,0:T(8,128)(2,1)S(1)}, bf16[64,2304]{1,0:T(8,128)(2,1)S(1)}, u32[]{:S(2)}, u32[]{:S(2)}) collective-permute-start(bf16[64,2304]{1,0:T(8,128)(2,1)S(1)} %pad_maximum_fusion.1.refs_4_), channel_id=1, source_target_pairs={{0,24},{8,0},{16,8},{24,16},{1,25},{9,1},{17,9},{25,17},{2,26},{10... | collective-permute-start | bytes 884744 | tf_op jit(solution)/shard_map/ppermute | solution.py:18
  51.1 5.1 %copy-start.2 = (bf16[64,2432]{1,0:T(8,128)(2,1)}, bf16[64,2432]{1,0:T(8,128)(2,1)S(1)}, u32[]{:S(2)}) copy-start(bf16[64,2432]{1,0:T(8,128)(2,1)S(1)} %collective-permute-done.8.refs_2_) | copy-start | bytes 933892
  51.1 5.1 %copy-start.3 = (bf16[64,2432]{1,0:T(8,128)(2,1)}, bf16[64,2432]{1,0:T(8,128)(2,1)S(1)}, u32[]{:S(2)}) copy-start(bf16[64,2432]{1,0:T(8,128)(2,1)S(1)} %collective-permute-done.9.refs_3_) | copy-start | bytes 933892
  51.2 15.5 %collective-permute-start.10 = (bf16[256,128]{1,0:T(8,128)(2,1)S(1)}, bf16[256,128]{1,0:T(8,128)(2,1)S(1)}, u32[]{:S(2)}, u32[]{:S(2)}) collective-permute-start(bf16[256,128]{1,0:T(8,128)(2,1)S(1)} %pad_maximum_fusion.3.own_ref), channel_id=1, source_target_pairs={{0,32},{32,0},{1,33},{33,1},{2,34},{34,2},{3,35},{35,3},{4,36},{36... | collective-permute-start | bytes 196616 | tf_op jit(solution)/shard_map/ppermute | solution.py:220
  66.7 1.2 copy-start
  67.9 1.2 copy-start.1
  72.1 21.9 %all-to-all-start.1 = ((f32[128,4,128]{2,1,0:T(4,128)}), f32[128,4,128]{2,1,0:T(4,128)S(1)}, u32[]{:S(2)}, u32[]{:S(2)}) async-start(f32[128,4,128]{2,1,0:T(4,128)} %broadcast_in_dim.10), calls=%async_computation.1 | async-start | bytes 524288 | tf_op jit(solution)/shard_map/all_to_all | solution.py:23
  101.4 13.5 %collective-permute-start.14 = (bf16[64,2304]{1,0:T(8,128)(2,1)S(1)}, bf16[64,2304]{1,0:T(8,128)(2,1)S(1)}, u32[]{:S(2)}, u32[]{:S(2)}) collective-permute-start(bf16[64,2304]{1,0:T(8,128)(2,1)S(1)} %get-tuple-element.31), channel_id=1, source_target_pairs={{0,192},{64,0},{128,64},{192,128},{1,193},{65,1},{129,65},{193,129... | collective-permute-start | bytes 884744 | tf_op jit(solution)/shard_map/ppermute | solution.py:18
  102.3 14.3 %collective-permute-start.15 = (bf16[64,2304]{1,0:T(8,128)(2,1)S(1)}, bf16[64,2304]{1,0:T(8,128)(2,1)S(1)}, u32[]{:S(2)}, u32[]{:S(2)}) collective-permute-start(bf16[64,2304]{1,0:T(8,128)(2,1)S(1)} %get-tuple-element.32), channel_id=1, source_target_pairs={{0,128},{64,192},{128,0},{192,64},{1,129},{65,193},{129,1},{193,65... | collective-permute-start | bytes 884744 | tf_op jit(solution)/shard_map/ppermute | solution.py:18
  104.2 12.5 %collective-permute-start.16 = (bf16[64,2304]{1,0:T(8,128)(2,1)S(1)}, bf16[64,2304]{1,0:T(8,128)(2,1)S(1)}, u32[]{:S(2)}, u32[]{:S(2)}) collective-permute-start(bf16[64,2304]{1,0:T(8,128)(2,1)S(1)} %get-tuple-element.33), channel_id=1, source_target_pairs={{0,64},{64,128},{128,192},{192,0},{1,65},{65,129},{129,193},{193,1... | collective-permute-start | bytes 884744 | tf_op jit(solution)/shard_map/ppermute | solution.py:18
  112.5 8.7 %collective-permute-start.20 = (bf16[64,2304]{1,0:T(8,128)(2,1)S(1)}, bf16[64,2304]{1,0:T(8,128)(2,1)S(1)}, u32[]{:S(2)}, u32[]{:S(2)}) collective-permute-start(bf16[64,2304]{1,0:T(8,128)(2,1)S(1)} %get-tuple-element.39), channel_id=1, source_target_pairs={{0,24},{8,0},{16,8},{24,16},{1,25},{9,1},{17,9},{25,17},{2,26},{10... | collective-permute-start | bytes 884744 | tf_op jit(solution)/shard_map/ppermute | solution.py:18
  114.0 10.6 %collective-permute-start.21 = (bf16[64,2304]{1,0:T(8,128)(2,1)S(1)}, bf16[64,2304]{1,0:T(8,128)(2,1)S(1)}, u32[]{:S(2)}, u32[]{:S(2)}) collective-permute-start(bf16[64,2304]{1,0:T(8,128)(2,1)S(1)} %get-tuple-element.40), channel_id=1, source_target_pairs={{0,16},{8,24},{16,0},{24,8},{1,17},{9,25},{17,1},{25,9},{2,18},{10... | collective-permute-start | bytes 884744 | tf_op jit(solution)/shard_map/ppermute | solution.py:18
  114.9 10.8 %collective-permute-start.22 = (bf16[64,2304]{1,0:T(8,128)(2,1)S(1)}, bf16[64,2304]{1,0:T(8,128)(2,1)S(1)}, u32[]{:S(2)}, u32[]{:S(2)}) collective-permute-start(bf16[64,2304]{1,0:T(8,128)(2,1)S(1)} %get-tuple-element.41), channel_id=1, source_target_pairs={{0,8},{8,16},{16,24},{24,0},{1,9},{9,17},{17,25},{25,1},{2,10},{10... | collective-permute-start | bytes 884744 | tf_op jit(solution)/shard_map/ppermute | solution.py:18
  116.8 12.4 %collective-permute-start.17 = (bf16[16,2304]{1,0:T(8,128)(2,1)S(1)}, bf16[16,2304]{1,0:T(8,128)(2,1)S(1)}, u32[]{:S(2)}, u32[]{:S(2)}) collective-permute-start(bf16[16,2304]{1,0:T(8,128)(2,1)S(1)} %get-tuple-element.46), channel_id=1, source_target_pairs={{0,24},{8,0},{16,8},{24,16},{1,25},{9,1},{17,9},{25,17},{2,26},{10... | collective-permute-start | bytes 221192 | tf_op jit(solution)/shard_map/ppermute | solution.py:18
  117.2 13.4 %collective-permute-start.18 = (bf16[16,2304]{1,0:T(8,128)(2,1)S(1)}, bf16[16,2304]{1,0:T(8,128)(2,1)S(1)}, u32[]{:S(2)}, u32[]{:S(2)}) collective-permute-start(bf16[16,2304]{1,0:T(8,128)(2,1)S(1)} %get-tuple-element.48), channel_id=1, source_target_pairs={{0,16},{8,24},{16,0},{24,8},{1,17},{9,25},{17,1},{25,9},{2,18},{10... | collective-permute-start | bytes 221192 | tf_op jit(solution)/shard_map/ppermute | solution.py:18
  121.3 9.3 %collective-permute-start.19 = (bf16[16,2304]{1,0:T(8,128)(2,1)S(1)}, bf16[16,2304]{1,0:T(8,128)(2,1)S(1)}, u32[]{:S(2)}, u32[]{:S(2)}) collective-permute-start(bf16[16,2304]{1,0:T(8,128)(2,1)S(1)} %get-tuple-element.47), channel_id=1, source_target_pairs={{0,8},{8,16},{16,24},{24,0},{1,9},{9,17},{17,25},{25,1},{2,10},{10... | collective-permute-start | bytes 221192 | tf_op jit(solution)/shard_map/ppermute | solution.py:18
  125.9 5.0 %collective-permute-start.23 = (bf16[16,2304]{1,0:T(8,128)(2,1)S(1)}, bf16[16,2304]{1,0:T(8,128)(2,1)S(1)}, u32[]{:S(2)}, u32[]{:S(2)}) collective-permute-start(bf16[16,2304]{1,0:T(8,128)(2,1)S(1)} %get-tuple-element.49), channel_id=1, source_target_pairs={{0,192},{64,0},{128,64},{192,128},{1,193},{65,1},{129,65},{193,129... | collective-permute-start | bytes 221192 | tf_op jit(solution)/shard_map/ppermute | solution.py:18
  128.9 5.9 %collective-permute-start.24 = (bf16[16,2304]{1,0:T(8,128)(2,1)S(1)}, bf16[16,2304]{1,0:T(8,128)(2,1)S(1)}, u32[]{:S(2)}, u32[]{:S(2)}) collective-permute-start(bf16[16,2304]{1,0:T(8,128)(2,1)S(1)} %get-tuple-element.51), channel_id=1, source_target_pairs={{0,128},{64,192},{128,0},{192,64},{1,129},{65,193},{129,1},{193,65... | collective-permute-start | bytes 221192 | tf_op jit(solution)/shard_map/ppermute | solution.py:18
  129.2 6.3 %collective-permute-start.25 = (bf16[16,2304]{1,0:T(8,128)(2,1)S(1)}, bf16[16,2304]{1,0:T(8,128)(2,1)S(1)}, u32[]{:S(2)}, u32[]{:S(2)}) collective-permute-start(bf16[16,2304]{1,0:T(8,128)(2,1)S(1)} %get-tuple-element.50), channel_id=1, source_target_pairs={{0,64},{64,128},{128,192},{192,0},{1,65},{65,129},{129,193},{193,1... | collective-permute-start | bytes 221192 | tf_op jit(solution)/shard_map/ppermute | solution.py:18
  136.3 12.6 %all-to-all-start.2 = ((bf16[8,2,4608]{2,1,0:T(2,128)(2,1)}), bf16[8,2,4608]{2,1,0:T(2,128)(2,1)S(1)}, u32[]{:S(2)}, u32[]{:S(2)}) async-start(bf16[8,2,4608]{2,1,0:T(2,128)(2,1)} %reshape.105), calls=%async_computation.2 | async-start | bytes 294912 | tf_op jit(solution)/shard_map/all_to_all | solution.py:260
  140.4 1.1 collective-permute-start.26

commit v5 on v4

--- a/solution.py
+++ b/solution.py
@@ -16,11 +16,6 @@
 def shifted(v, axis, by):
     n = lax.axis_size(axis)
     return lax.ppermute(v, axis, [(i, (i + by) % n) for i in range(n)])
-
-
-def gather(v, axis):
-    peers = lax.axis_size(axis)
-    return lax.all_to_all(jnp.broadcast_to(v[None], (peers, *v.shape)), axis, 0, 0, tiled=True)
 
 
 def column_chunks(width, most):
@@ -101,7 +96,7 @@
     )(where, *late, *early, own, sib)
 
 
-def labels_kernel(n, where_ref, own_ref, sib_ref, sums_ref, own_c, sib_c, rows_ref, own_tail, sib_tail):
+def labels_kernel(n, where_ref, own_ref, sib_ref, sums_ref, own_c, sib_c, rows_ref, send_ref, own_tail, sib_tail):
     plane, vocab = own_c.shape
     rows = plane // (n * n)
     for i in range(n * n):
@@ -119,17 +114,26 @@
     columns = jnp.zeros((plane, 8), jnp.float32)
     for i, column in enumerate((sums_ref[:, 0:1], picked, labels, sib_tail[:, 3:4], own_tail[:, 3:4])):
         columns = jnp.where(lane == i, column, columns)
-    rows_ref[...] = columns.T
-
-
-def labels_and_sums(n, where, own_tail, sib_tail, sums, own_c, sib_c):
+    known = columns.T
+    rows_ref[...] = known
+    lanes = send_ref.shape[1]
+    one = [known[i : i + 1, at : at + lanes] for i in range(2) for at in range(0, plane, lanes)]
+    block = jnp.concatenate(one * (8 // len(one)), axis=0)
+    for i in range(send_ref.shape[0] // 8):
+        send_ref[i * 8 : (i + 1) * 8, :] = block
+
+
+def labels_and_sums(n, peers, where, own_tail, sib_tail, sums, own_c, sib_c):
     plane = own_c.shape[0]
     vmem = pl.BlockSpec(memory_space=pltpu.VMEM)
     return pl.pallas_call(
         functools.partial(labels_kernel, n),
-        out_shape=jax.ShapeDtypeStruct((8, plane), jnp.float32),
+        out_shape=(
+            jax.ShapeDtypeStruct((8, plane), jnp.float32),
+            jax.ShapeDtypeStruct((peers * 2 * plane // 128, 128), jnp.float32),
+        ),
         in_specs=[pl.BlockSpec(memory_space=pltpu.SMEM)] + [vmem] * 5,
-        out_specs=vmem,
+        out_specs=(vmem, vmem),
         scratch_shapes=[pltpu.VMEM((plane, TAIL), jnp.float32)] * 2,
         compiler_params=pltpu.CompilerParams(vmem_limit_bytes=8 * 1024 * 1024),
     )(where, own_tail, sib_tail, sums, own_c, sib_c)
@@ -206,8 +210,9 @@
 
     digits = jnp.stack([targets % 256, (targets // 256) % 256, targets // 65536, valid_mask], axis=1)
     tail = jnp.pad(digits, ((0, 0), (0, TAIL - digits.shape[1]))).astype(jnp.bfloat16)
-    by_z = gather(jnp.concatenate([hidden, tail], axis=1), "z").reshape(nz * own_rows, width + TAIL)
-
+    for_all = lambda v: jnp.broadcast_to(v[None], (nz, *v.shape))
+    mine = jnp.concatenate([for_all(hidden), for_all(tail)], axis=2)
+    by_z = lax.all_to_all(mine, "z", 0, 0, tiled=True).reshape(nz * own_rows, width + TAIL)
     by_z, unembed_sib = lax.optimization_barrier((by_z, unembed_sib))
 
     first, second = by_z[:, :half], by_z[:, half:]
@@ -228,15 +233,16 @@
     where_yx = jnp.concatenate([places.T.ravel(), bases]).astype(i32)
 
     sums, own_c, sib_c = capped_logits(where_xy, late, early, unembed, unembed_sib)
-    known = labels_and_sums(n, where_xy, tail_own, tail_sib, sums, own_c, sib_c)
-    stats = gather(known[:2].reshape(2 * plane // 128, 128), ("x", "y", "z"))
+    peers, lines = nx * ny * nz, 2 * plane // 128
+    known, send = labels_and_sums(n, peers, where_xy, tail_own, tail_sib, sums, own_c, sib_c)
+    stats = lax.all_to_all(send.reshape(peers, lines, 128), ("x", "y", "z"), 0, 0, tiled=True)
     labels, weights = known[2], known[3]
     by_x = lambda v: jnp.sum(v.reshape(nx, per_x), axis=1)
     of_tokens = by_x(weights)
     counts = by_x(known[4]) + jnp.where(core == 0, of_tokens, jnp.roll(of_tokens, 1))
     counts_tok = jnp.repeat(jnp.where(core == 0, counts, jnp.roll(counts, -1)), per_x)
     coef = loss_scale * weights / counts_tok
-    stats = jnp.sum(stats.reshape(nx * ny * nz, 2 * plane // 128, 128), axis=0)
+    stats = jnp.sum(stats, axis=0)
     total, picked = stats.reshape(2, plane)
     lse = SOFTCAP + jnp.log(total)
     rows = jnp.stack([lse, coef, labels] + [jnp.zeros_like(lse)] * 5)

time: 150 us -> 149 us (level)
  waiting for transfers between devices: 52.9 us -> 50.6 us
    ppermute x24, waiting for transfers between devices: 23.8 us -> 21.5 us  [shifted(): return lax.ppermute(v, axis, [(i, (i + by) % n) for i in range(n)])]
where the time goes in v5:
time: 149 us; the launch traced here: 148 us
  starting transfers between devices  57.4 us (39%)
  waiting for transfers between devices  50.6 us (34%)
  Pallas kernels  26.9 us (18%)
  local copies, waits for them, and re-layouts  6.16 us (4%)
  other arithmetic  5.62 us (4%)
  between operations  1.55 us (1%)
    ppermute x24, starting transfers between devices, shifted(): return lax.ppermute(v, axis, [(i, (i + by) % n) for i in range(n)])  34.1 us
    ppermute x24, waiting for transfers between devices, shifted(): return lax.ppermute(v, axis, [(i, (i + by) % n) for i in range(n)])  21.5 us
    pallas_call x2, Pallas kernels, gradient_part(): pl.pallas_call(functools.partial(gradient_kernel, n), grid=(steps,), out_...  14.5 us
    all_to_all x1, waiting for transfers between devices, body(): lax.all_to_all(send.reshape(peers, lines, 128), ('x', 'y', 'z'), 0, 0, ti...  11.1 us
    all_to_all x1, starting transfers between devices, body(): lax.all_to_all(send.reshape(peers, lines, 128), ('x', 'y', 'z'), 0, 0, ti...  11 us
    pallas_call x1, Pallas kernels, capped_logits(): pl.pallas_call(functools.partial(logits_kernel, n), out_shape=(sums, capp...  10.4 us
    all_to_all x1, waiting for transfers between devices, body(): lax.all_to_all(mine, 'z', 0, 0, tiled=True)  10.1 us
    all_to_all x1, starting transfers between devices, body(): lax.all_to_all(mine, 'z', 0, 0, tiled=True)  8.47 us
  transfers between devices with their start and end apart: 30, of which 16 were waited for; matrix products, arithmetic and copies ran while one was open for 4% of the time, Pallas kernels for 12%

profile of v5, /device:TPU:8, one launch (start us, length us, event | category | flops | bytes accessed | tf_op | source)
XLA Modules:
  0.0 148.2 jit_solution(15795820717450644697)
XLA Ops:
  0.7 0.7 fusion.3
  1.6 0.8 broadcast_in_dim.6
  2.4 0.8 pad_maximum_fusion.2
  3.2 8.5 %all-to-all-start = ((bf16[8,2,4736]{2,1,0:T(2,128)(2,1)}), bf16[8,2,4736]{2,1,0:T(2,128)(2,1)S(1)}, u32[]{:S(2)}, u32[]{:S(2)}) async-start(bf16[8,2,4736]{2,1,0:T(2,128)(2,1)} %pad_maximum_fusion.2), calls=%async_computation | async-start | bytes 303104 | tf_op jit(solution)/shard_map/all_to_all | solution.py:215
  11.7 10.1 %all-to-all-done = bf16[8,2,4736]{2,1,0:T(2,128)(2,1)S(1)} async-done(((bf16[8,2,4736]{2,1,0:T(2,128)(2,1)}), bf16[8,2,4736]{2,1,0:T(2,128)(2,1)S(1)}, u32[]{:S(2)}, u32[]{:S(2)}) %all-to-all-start) | async-done | bytes 151584 | tf_op jit(solution)/shard_map/all_to_all | solution.py:215
  21.9 1.6 %collective-permute-start.1 = (bf16[16,2304]{1,0:T(8,128)(2,1)S(1)}, bf16[16,2304]{1,0:T(8,128)(2,1)S(1)}, u32[]{:S(2)}, u32[]{:S(2)}) collective-permute-start(bf16[16,2304]{1,0:T(8,128)(2,1)S(1)} %slice.75), channel_id=1, source_target_pairs={{0,64},{64,128},{128,192},{192,0},{1,65},{65,129},{129,193},{193,1... | collective-permute-start | bytes 221192 | tf_op jit(solution)/shard_map/ppermute | solution.py:18
  23.5 2.7 %collective-permute-start.2 = (bf16[16,2304]{1,0:T(8,128)(2,1)S(1)}, bf16[16,2304]{1,0:T(8,128)(2,1)S(1)}, u32[]{:S(2)}, u32[]{:S(2)}) collective-permute-start(bf16[16,2304]{1,0:T(8,128)(2,1)S(1)} %slice.75), channel_id=1, source_target_pairs={{0,128},{64,192},{128,0},{192,64},{1,129},{65,193},{129,1},{193,65... | collective-permute-start | bytes 221192 | tf_op jit(solution)/shard_map/ppermute | solution.py:18
  26.2 1.4 collective-permute-start.3
  27.6 1.7 %collective-permute-start.4 = (bf16[16,2432]{1,0:T(8,128)(2,1)S(1)}, bf16[16,2432]{1,0:T(8,128)(2,1)S(1)}, u32[]{:S(2)}, u32[]{:S(2)}) collective-permute-start(bf16[16,2432]{1,0:T(8,128)(2,1)S(1)} %slice.76), channel_id=1, source_target_pairs={{0,8},{8,16},{16,24},{24,0},{1,9},{9,17},{17,25},{25,1},{2,10},{10... | collective-permute-start | bytes 233480 | tf_op jit(solution)/shard_map/ppermute | solution.py:18
  29.3 0.9 collective-permute-start.5
  30.2 2.4 %collective-permute-start.6 = (bf16[16,2432]{1,0:T(8,128)(2,1)S(1)}, bf16[16,2432]{1,0:T(8,128)(2,1)S(1)}, u32[]{:S(2)}, u32[]{:S(2)}) collective-permute-start(bf16[16,2432]{1,0:T(8,128)(2,1)S(1)} %slice.76), channel_id=1, source_target_pairs={{0,24},{8,0},{16,8},{24,16},{1,25},{9,1},{17,9},{25,17},{2,26},{10... | collective-permute-start | bytes 233480 | tf_op jit(solution)/shard_map/ppermute | solution.py:18
  32.8 2.5 %collective-permute-done.5 = bf16[16,2432]{1,0:T(8,128)(2,1)S(1)} collective-permute-done((bf16[16,2432]{1,0:T(8,128)(2,1)S(1)}, bf16[16,2432]{1,0:T(8,128)(2,1)S(1)}, u32[]{:S(2)}, u32[]{:S(2)}) %collective-permute-start.5) | collective-permute-done | bytes 77856 | tf_op jit(solution)/shard_map/ppermute | solution.py:18
  35.3 0.2 collective-permute-done.6
  36.6 2.0 %collective-permute-start.7 = (bf16[64,2432]{1,0:T(8,128)(2,1)S(1)}, bf16[64,2432]{1,0:T(8,128)(2,1)S(1)}, u32[]{:S(2)}, u32[]{:S(2)}) collective-permute-start(bf16[64,2432]{1,0:T(8,128)(2,1)S(1)} %pad_maximum_fusion.refs_0_), channel_id=1, source_target_pairs={{0,64},{64,128},{128,192},{192,0},{1,65},{65,129},{129,193},{193,1... | collective-permute-start | bytes 933896 | tf_op jit(solution)/shard_map/ppermute | solution.py:18
  38.6 0.7 collective-permute-start.8
  39.4 1.1 collective-permute-start.11
  40.6 2.5 %collective-permute-start.12 = (bf16[64,2304]{1,0:T(8,128)(2,1)S(1)}, bf16[64,2304]{1,0:T(8,128)(2,1)S(1)}, u32[]{:S(2)}, u32[]{:S(2)}) collective-permute-start(bf16[64,2304]{1,0:T(8,128)(2,1)S(1)} %pad_maximum_fusion.1.refs_4_), channel_id=1, source_target_pairs={{0,16},{8,24},{16,0},{24,8},{1,17},{9,25},{17,1},{25,9},{2,18},{10... | collective-permute-start | bytes 884744 | tf_op jit(solution)/shard_map/ppermute | solution.py:18
  43.1 2.0 %collective-permute-done.9.refs_3_ = bf16[64,2432]{1,0:T(8,128)(2,1)S(1)} collective-permute-done((bf16[64,2432]{1,0:T(8,128)(2,1)S(1)}, bf16[64,2432]{1,0:T(8,128)(2,1)S(1)}, u32[]{:S(2)}, u32[]{:S(2)}) %collective-permute-start.9) | collective-permute-done | bytes 311328 | tf_op jit(solution)/shard_map/ppermute | solution.py:18
  45.1 1.4 collective-permute-start.13
  46.7 4.0 %collective-permute-done.7.refs_1_ = bf16[64,2432]{1,0:T(8,128)(2,1)S(1)} collective-permute-done((bf16[64,2432]{1,0:T(8,128)(2,1)S(1)}, bf16[64,2432]{1,0:T(8,128)(2,1)S(1)}, u32[]{:S(2)}, u32[]{:S(2)}) %collective-permute-start.7) | collective-permute-done | bytes 311328 | tf_op jit(solution)/shard_map/ppermute | solution.py:18
  50.7 0.3 collective-permute-start.10
  51.0 2.8 %collective-permute-done.13.refs_7_ = bf16[64,2304]{1,0:T(8,128)(2,1)S(1)} collective-permute-done((bf16[64,2304]{1,0:T(8,128)(2,1)S(1)}, bf16[64,2304]{1,0:T(8,128)(2,1)S(1)}, u32[]{:S(2)}, u32[]{:S(2)}) %collective-permute-start.13) | collective-permute-done | bytes 294944 | tf_op jit(solution)/shard_map/ppermute | solution.py:18
  53.8 10.4 %shard_map.68 = (f32[256,128]{1,0:T(8,128)S(1)}, f32[256,1000]{1,0:T(8,128)}, f32[256,1000]{1,0:T(8,128)}) custom-call(s32[34]{0:T(128)S(1)} %pad_add_fusion.where_ref, bf16[64,2432]{1,0:T(8,128)(2,1)S(1)} %pad_maximum_fusion.refs_0_, bf16[64,2432]{1,0:T(8,128)(2,1)S(1)} %collective-permute-done.7.refs_1_, bf16[64,2432]{1,0:T(8,128)(2,1)} %copy-done.3, ...), custom_call_target="tpu_custom_call" | custom-call | flops 4718592000 | bytes 23150592 | tf_op jit(solution)/shard_map/pallas_call | solution.py:80
  64.2 1.2 copy-done
  65.5 1.2 copy-done.1
  66.7 1.9 %shard_map.69 = (f32[8,256]{1,0:T(8,128)S(1)}, f32[512,128]{1,0:T(8,128)}) custom-call(s32[34]{0:T(128)S(1)} %pad_add_fusion.where_ref, bf16[256,128]{1,0:T(8,128)(2,1)S(1)} %pad_maximum_fusion.4.own_ref, bf16[256,128]{1,0:T(8,128)(2,1)S(1)} %collective-permute-done.10.sib_ref, f32[256,128]{1,0:T(8,128)S(1)} %get-tuple-element.29.sums_ref, ...), custom_call_target="tpu_custom_call" | custom-call | tf_op jit(solution)/shard_map/pallas_call | solution.py:129
  68.7 0.1 reduce_sum.47
  68.8 0.6 slice.83
  69.5 0.1 reduce_sum.46
  69.6 11.0 %all-to-all-start.1 = ((f32[128,4,128]{2,1,0:T(4,128)}), f32[128,4,128]{2,1,0:T(4,128)S(1)}, u32[]{:S(2)}, u32[]{:S(2)}) async-start(f32[128,4,128]{2,1,0:T(4,128)} %bitcast.6), calls=%async_computation.1 | async-start | bytes 524288 | tf_op jit(solution)/shard_map/all_to_all | solution.py:238
  80.6 0.7 fusion
  81.7 11.1 %all-to-all-done.1 = f32[128,4,128]{2,1,0:T(4,128)S(1)} async-done(((f32[128,4,128]{2,1,0:T(4,128)}), f32[128,4,128]{2,1,0:T(4,128)S(1)}, u32[]{:S(2)}, u32[]{:S(2)}) %all-to-all-start.1) | async-done | bytes 262176 | tf_op jit(solution)/shard_map/all_to_all | solution.py:238
  92.8 0.1 reduce_sum.45
  93.0 7.3 %shard_map.70 = (bf16[64,2304]{1,0:T(8,128)(2,1)S(1)}, bf16[64,2304]{1,0:T(8,128)(2,1)S(1)}, bf16[64,2304]{1,0:T(8,128)(2,1)S(1)}, bf16[64,2304]{1,0:T(8,128)(2,1)S(1)}) custom-call(s32[34]{0:T(128)S(1)} %pad_add_fusion.where_ref, f32[8,256]{1,0:T(8,128)S(1)} %stack.46.rows_ref, f32[256,1000]{1,0:T(8,128)} %get-tuple-element.30.own_c, ...), custom_call_target="tpu_custom_call" | custom-call | flops 2359296000 | bytes 10395648 | tf_op jit(solution)/shard_map/pallas_call | solution.py:176
  100.3 0.9 collective-permute-start.14
  101.1 1.8 %collective-permute-start.15 = (bf16[64,2304]{1,0:T(8,128)(2,1)S(1)}, bf16[64,2304]{1,0:T(8,128)(2,1)S(1)}, u32[]{:S(2)}, u32[]{:S(2)}) collective-permute-start(bf16[64,2304]{1,0:T(8,128)(2,1)S(1)} %get-tuple-element.36), channel_id=1, source_target_pairs={{0,128},{64,192},{128,0},{192,64},{1,129},{65,193},{129,1},{193,65... | collective-permute-start | bytes 884744 | tf_op jit(solution)/shard_map/ppermute | solution.py:18
  103.0 0.4 collective-permute-start.16
  103.3 7.2 %shard_map.71 = (bf16[64,2304]{1,0:T(8,128)(2,1)S(1)}, bf16[64,2304]{1,0:T(8,128)(2,1)S(1)}, bf16[64,2304]{1,0:T(8,128)(2,1)S(1)}, bf16[64,2304]{1,0:T(8,128)(2,1)S(1)}) custom-call(s32[18]{0:T(128)S(1)} %pad_add_fusion.1.where_ref, f32[8,256]{1,0:T(8,128)S(1)} %stack.46.rows_ref, f32[256,1000]{1,0:T(8,128)} %get-tuple-element.30.own_c, ...), custom_call_target="tpu_custom_call" | custom-call | flops 2359296000 | bytes 10395648 | tf_op jit(solution)/shard_map/pallas_call | solution.py:176
  110.7 0.1 reduce_sum.49
  110.8 0.6 slice.96
  111.4 1.4 collective-permute-start.20
  112.8 0.9 collective-permute-start.21
  113.7 1.7 %collective-permute-start.22 = (bf16[64,2304]{1,0:T(8,128)(2,1)S(1)}, bf16[64,2304]{1,0:T(8,128)(2,1)S(1)}, u32[]{:S(2)}, u32[]{:S(2)}) collective-permute-start(bf16[64,2304]{1,0:T(8,128)(2,1)S(1)} %get-tuple-element.45), channel_id=1, source_target_pairs={{0,8},{8,16},{16,24},{24,0},{1,9},{9,17},{17,25},{25,1},{2,10},{10... | collective-permute-start | bytes 884744 | tf_op jit(solution)/shard_map/ppermute | solution.py:18
  115.4 0.1 add_convert_fusion.1
  115.6 0.4 collective-permute-start.17
  116.0 2.6 %collective-permute-start.18 = (bf16[16,2304]{1,0:T(8,128)(2,1)S(1)}, bf16[16,2304]{1,0:T(8,128)(2,1)S(1)}, u32[]{:S(2)}, u32[]{:S(2)}) collective-permute-start(bf16[16,2304]{1,0:T(8,128)(2,1)S(1)} %get-tuple-element.52), channel_id=1, source_target_pairs={{0,16},{8,24},{16,0},{24,8},{1,17},{9,25},{17,1},{25,9},{2,18},{10... | collective-permute-start | bytes 221192 | tf_op jit(solution)/shard_map/ppermute | solution.py:18
  118.6 1.2 collective-permute-done.20
  119.9 0.6 collective-permute-start.19
  120.5 2.7 %collective-permute-done.21 = bf16[64,2304]{1,0:T(8,128)(2,1)S(1)} collective-permute-done((bf16[64,2304]{1,0:T(8,128)(2,1)S(1)}, bf16[64,2304]{1,0:T(8,128)(2,1)S(1)}, u32[]{:S(2)}, u32[]{:S(2)}) %collective-permute-start.21) | collective-permute-done | bytes 294944 | tf_op jit(solution)/shard_map/ppermute | solution.py:18
  123.2 1.1 collective-permute-done.22
  124.2 0.1 add_convert_fusion
  124.4 3.0 %collective-permute-start.23 = (bf16[16,2304]{1,0:T(8,128)(2,1)S(1)}, bf16[16,2304]{1,0:T(8,128)(2,1)S(1)}, u32[]{:S(2)}, u32[]{:S(2)}) collective-permute-start(bf16[16,2304]{1,0:T(8,128)(2,1)S(1)} %get-tuple-element.53), channel_id=1, source_target_pairs={{0,192},{64,0},{128,64},{192,128},{1,193},{65,1},{129,65},{193,129... | collective-permute-start | bytes 221192 | tf_op jit(solution)/shard_map/ppermute | solution.py:18
  127.4 0.4 collective-permute-start.24
  127.8 1.3 collective-permute-start.25
  129.2 0.2 collective-permute-done.23
  129.4 3.9 %collective-permute-done.24 = bf16[16,2304]{1,0:T(8,128)(2,1)S(1)} collective-permute-done((bf16[16,2304]{1,0:T(8,128)(2,1)S(1)}, bf16[16,2304]{1,0:T(8,128)(2,1)S(1)}, u32[]{:S(2)}, u32[]{:S(2)}) %collective-permute-start.24) | collective-permute-done | bytes 73760 | tf_op jit(solution)/shard_map/ppermute | solution.py:18
  133.4 0.7 collective-permute-done.25
  134.1 0.7 reshape.109
  134.9 3.4 %all-to-all-start.2 = ((bf16[8,2,4608]{2,1,0:T(2,128)(2,1)}), bf16[8,2,4608]{2,1,0:T(2,128)(2,1)S(1)}, u32[]{:S(2)}, u32[]{:S(2)}) async-start(bf16[8,2,4608]{2,1,0:T(2,128)(2,1)} %reshape.109), calls=%async_computation.2 | async-start | bytes 294912 | tf_op jit(solution)/shard_map/all_to_all | solution.py:266
  138.3 0.7 broadcast_select_fusion
  139.0 1.1 collective-permute-done.26
  140.1 0.5 add_divide_fusion
  140.6 6.8 %all-to-all-done.2 = bf16[8,2,4608]{2,1,0:T(2,128)(2,1)S(1)} async-done(((bf16[8,2,4608]{2,1,0:T(2,128)(2,1)}), bf16[8,2,4608]{2,1,0:T(2,128)(2,1)S(1)}, u32[]{:S(2)}, u32[]{:S(2)}) %all-to-all-start.2) | async-done | bytes 147488 | tf_op jit(solution)/shard_map/all_to_all | solution.py:266
  147.4 0.7 convert_reduce_fusion
  (66 shorter events, 2.0 us)
Async XLA Ops:
  0.6 21.2 %collective-permute-start = (bf16[1000,4608]{1,0:T(8,128)(2,1)}, bf16[1000,4608]{1,0:T(8,128)(2,1)}, u32[]{:S(2)}, u32[]{:S(2)}) collective-permute-start(bf16[1000,4608]{1,0:T(8,128)(2,1)} %own_ref.3), channel_id=1, source_target_pairs={{0,32},{32,0},{1,33},{33,1},{2,34},{34,2},{3,35},{35,3},{4,36},{36... | collective-permute-start | bytes 27648008 | tf_op jit(solution)/shard_map/ppermute | solution.py:209
  3.2 18.6 %all-to-all-start = ((bf16[8,2,4736]{2,1,0:T(2,128)(2,1)}), bf16[8,2,4736]{2,1,0:T(2,128)(2,1)S(1)}, u32[]{:S(2)}, u32[]{:S(2)}) async-start(bf16[8,2,4736]{2,1,0:T(2,128)(2,1)} %pad_maximum_fusion.2), calls=%async_computation | async-start | bytes 303104 | tf_op jit(solution)/shard_map/all_to_all | solution.py:215
  21.9 8.4 %collective-permute-start.1 = (bf16[16,2304]{1,0:T(8,128)(2,1)S(1)}, bf16[16,2304]{1,0:T(8,128)(2,1)S(1)}, u32[]{:S(2)}, u32[]{:S(2)}) collective-permute-start(bf16[16,2304]{1,0:T(8,128)(2,1)S(1)} %slice.75), channel_id=1, source_target_pairs={{0,64},{64,128},{128,192},{192,0},{1,65},{65,129},{129,193},{193,1... | collective-permute-start | bytes 221192 | tf_op jit(solution)/shard_map/ppermute | solution.py:18
  23.5 9.2 %collective-permute-start.2 = (bf16[16,2304]{1,0:T(8,128)(2,1)S(1)}, bf16[16,2304]{1,0:T(8,128)(2,1)S(1)}, u32[]{:S(2)}, u32[]{:S(2)}) collective-permute-start(bf16[16,2304]{1,0:T(8,128)(2,1)S(1)} %slice.75), channel_id=1, source_target_pairs={{0,128},{64,192},{128,0},{192,64},{1,129},{65,193},{129,1},{193,65... | collective-permute-start | bytes 221192 | tf_op jit(solution)/shard_map/ppermute | solution.py:18
  26.2 6.5 %collective-permute-start.3 = (bf16[16,2304]{1,0:T(8,128)(2,1)S(1)}, bf16[16,2304]{1,0:T(8,128)(2,1)S(1)}, u32[]{:S(2)}, u32[]{:S(2)}) collective-permute-start(bf16[16,2304]{1,0:T(8,128)(2,1)S(1)} %slice.75), channel_id=1, source_target_pairs={{0,192},{64,0},{128,64},{192,128},{1,193},{65,1},{129,65},{193,129... | collective-permute-start | bytes 221192 | tf_op jit(solution)/shard_map/ppermute | solution.py:18
  27.6 5.1 %collective-permute-start.4 = (bf16[16,2432]{1,0:T(8,128)(2,1)S(1)}, bf16[16,2432]{1,0:T(8,128)(2,1)S(1)}, u32[]{:S(2)}, u32[]{:S(2)}) collective-permute-start(bf16[16,2432]{1,0:T(8,128)(2,1)S(1)} %slice.76), channel_id=1, source_target_pairs={{0,8},{8,16},{16,24},{24,0},{1,9},{9,17},{17,25},{25,1},{2,10},{10... | collective-permute-start | bytes 233480 | tf_op jit(solution)/shard_map/ppermute | solution.py:18
  29.3 6.0 %collective-permute-start.5 = (bf16[16,2432]{1,0:T(8,128)(2,1)S(1)}, bf16[16,2432]{1,0:T(8,128)(2,1)S(1)}, u32[]{:S(2)}, u32[]{:S(2)}) collective-permute-start(bf16[16,2432]{1,0:T(8,128)(2,1)S(1)} %slice.76), channel_id=1, source_target_pairs={{0,16},{8,24},{16,0},{24,8},{1,17},{9,25},{17,1},{25,9},{2,18},{10... | collective-permute-start | bytes 233480 | tf_op jit(solution)/shard_map/ppermute | solution.py:18
  30.2 5.2 %collective-permute-start.6 = (bf16[16,2432]{1,0:T(8,128)(2,1)S(1)}, bf16[16,2432]{1,0:T(8,128)(2,1)S(1)}, u32[]{:S(2)}, u32[]{:S(2)}) collective-permute-start(bf16[16,2432]{1,0:T(8,128)(2,1)S(1)} %slice.76), channel_id=1, source_target_pairs={{0,24},{8,0},{16,8},{24,16},{1,25},{9,1},{17,9},{25,17},{2,26},{10... | collective-permute-start | bytes 233480 | tf_op jit(solution)/shard_map/ppermute | solution.py:18
  35.5 9.6 %collective-permute-start.9 = (bf16[64,2432]{1,0:T(8,128)(2,1)S(1)}, bf16[64,2432]{1,0:T(8,128)(2,1)S(1)}, u32[]{:S(2)}, u32[]{:S(2)}) collective-permute-start(bf16[64,2432]{1,0:T(8,128)(2,1)S(1)} %pad_maximum_fusion.refs_0_), channel_id=1, source_target_pairs={{0,192},{64,0},{128,64},{192,128},{1,193},{65,1},{129,65},{193,129... | collective-permute-start | bytes 933896 | tf_op jit(solution)/shard_map/ppermute | solution.py:18
  36.6 14.1 %collective-permute-start.7 = (bf16[64,2432]{1,0:T(8,128)(2,1)S(1)}, bf16[64,2432]{1,0:T(8,128)(2,1)S(1)}, u32[]{:S(2)}, u32[]{:S(2)}) collective-permute-start(bf16[64,2432]{1,0:T(8,128)(2,1)S(1)} %pad_maximum_fusion.refs_0_), channel_id=1, source_target_pairs={{0,64},{64,128},{128,192},{192,0},{1,65},{65,129},{129,193},{193,1... | collective-permute-start | bytes 933896 | tf_op jit(solution)/shard_map/ppermute | solution.py:18
  38.6 12.1 %collective-permute-start.8 = (bf16[64,2432]{1,0:T(8,128)(2,1)S(1)}, bf16[64,2432]{1,0:T(8,128)(2,1)S(1)}, u32[]{:S(2)}, u32[]{:S(2)}) collective-permute-start(bf16[64,2432]{1,0:T(8,128)(2,1)S(1)} %pad_maximum_fusion.refs_0_), channel_id=1, source_target_pairs={{0,128},{64,192},{128,0},{192,64},{1,129},{65,193},{129,1},{193,65... | collective-permute-start | bytes 933896 | tf_op jit(solution)/shard_map/ppermute | solution.py:18
  39.4 11.6 %collective-permute-start.11 = (bf16[64,2304]{1,0:T(8,128)(2,1)S(1)}, bf16[64,2304]{1,0:T(8,128)(2,1)S(1)}, u32[]{:S(2)}, u32[]{:S(2)}) collective-permute-start(bf16[64,2304]{1,0:T(8,128)(2,1)S(1)} %pad_maximum_fusion.1.refs_4_), channel_id=1, source_target_pairs={{0,8},{8,16},{16,24},{24,0},{1,9},{9,17},{17,25},{25,1},{2,10},{10... | collective-permute-start | bytes 884744 | tf_op jit(solution)/shard_map/ppermute | solution.py:18
  40.6 10.4 %collective-permute-start.12 = (bf16[64,2304]{1,0:T(8,128)(2,1)S(1)}, bf16[64,2304]{1,0:T(8,128)(2,1)S(1)}, u32[]{:S(2)}, u32[]{:S(2)}) collective-permute-start(bf16[64,2304]{1,0:T(8,128)(2,1)S(1)} %pad_maximum_fusion.1.refs_4_), channel_id=1, source_target_pairs={{0,16},{8,24},{16,0},{24,8},{1,17},{9,25},{17,1},{25,9},{2,18},{10... | collective-permute-start | bytes 884744 | tf_op jit(solution)/shard_map/ppermute | solution.py:18
  45.1 8.7 %copy-start.2 = (bf16[64,2432]{1,0:T(8,128)(2,1)}, bf16[64,2432]{1,0:T(8,128)(2,1)S(1)}, u32[]{:S(2)}) copy-start(bf16[64,2432]{1,0:T(8,128)(2,1)S(1)} %collective-permute-done.9.refs_3_) | copy-start | bytes 933892
  45.1 8.7 %collective-permute-start.13 = (bf16[64,2304]{1,0:T(8,128)(2,1)S(1)}, bf16[64,2304]{1,0:T(8,128)(2,1)S(1)}, u32[]{:S(2)}, u32[]{:S(2)}) collective-permute-start(bf16[64,2304]{1,0:T(8,128)(2,1)S(1)} %pad_maximum_fusion.1.refs_4_), channel_id=1, source_target_pairs={{0,24},{8,0},{16,8},{24,16},{1,25},{9,1},{17,9},{25,17},{2,26},{10... | collective-permute-start | bytes 884744 | tf_op jit(solution)/shard_map/ppermute | solution.py:18
  50.7 3.1 %copy-start.3 = (bf16[64,2432]{1,0:T(8,128)(2,1)}, bf16[64,2432]{1,0:T(8,128)(2,1)S(1)}, u32[]{:S(2)}) copy-start(bf16[64,2432]{1,0:T(8,128)(2,1)S(1)} %collective-permute-done.8.refs_2_) | copy-start | bytes 933892
  50.7 13.5 %collective-permute-start.10 = (bf16[256,128]{1,0:T(8,128)(2,1)S(1)}, bf16[256,128]{1,0:T(8,128)(2,1)S(1)}, u32[]{:S(2)}, u32[]{:S(2)}) collective-permute-start(bf16[256,128]{1,0:T(8,128)(2,1)S(1)} %pad_maximum_fusion.4.own_ref), channel_id=1, source_target_pairs={{0,32},{32,0},{1,33},{33,1},{2,34},{34,2},{3,35},{35,3},{4,36},{36... | collective-permute-start | bytes 196616 | tf_op jit(solution)/shard_map/ppermute | solution.py:225
  64.2 1.2 copy-start
  65.5 1.2 copy-start.1
  69.6 23.2 %all-to-all-start.1 = ((f32[128,4,128]{2,1,0:T(4,128)}), f32[128,4,128]{2,1,0:T(4,128)S(1)}, u32[]{:S(2)}, u32[]{:S(2)}) async-start(f32[128,4,128]{2,1,0:T(4,128)} %bitcast.6), calls=%async_computation.1 | async-start | bytes 524288 | tf_op jit(solution)/shard_map/all_to_all | solution.py:238
  100.3 13.5 %collective-permute-start.14 = (bf16[64,2304]{1,0:T(8,128)(2,1)S(1)}, bf16[64,2304]{1,0:T(8,128)(2,1)S(1)}, u32[]{:S(2)}, u32[]{:S(2)}) collective-permute-start(bf16[64,2304]{1,0:T(8,128)(2,1)S(1)} %get-tuple-element.35), channel_id=1, source_target_pairs={{0,192},{64,0},{128,64},{192,128},{1,193},{65,1},{129,65},{193,129... | collective-permute-start | bytes 884744 | tf_op jit(solution)/shard_map/ppermute | solution.py:18
  101.1 14.3 %collective-permute-start.15 = (bf16[64,2304]{1,0:T(8,128)(2,1)S(1)}, bf16[64,2304]{1,0:T(8,128)(2,1)S(1)}, u32[]{:S(2)}, u32[]{:S(2)}) collective-permute-start(bf16[64,2304]{1,0:T(8,128)(2,1)S(1)} %get-tuple-element.36), channel_id=1, source_target_pairs={{0,128},{64,192},{128,0},{192,64},{1,129},{65,193},{129,1},{193,65... | collective-permute-start | bytes 884744 | tf_op jit(solution)/shard_map/ppermute | solution.py:18
  103.0 12.5 %collective-permute-start.16 = (bf16[64,2304]{1,0:T(8,128)(2,1)S(1)}, bf16[64,2304]{1,0:T(8,128)(2,1)S(1)}, u32[]{:S(2)}, u32[]{:S(2)}) collective-permute-start(bf16[64,2304]{1,0:T(8,128)(2,1)S(1)} %get-tuple-element.37), channel_id=1, source_target_pairs={{0,64},{64,128},{128,192},{192,0},{1,65},{65,129},{129,193},{193,1... | collective-permute-start | bytes 884744 | tf_op jit(solution)/shard_map/ppermute | solution.py:18
  111.4 8.5 %collective-permute-start.20 = (bf16[64,2304]{1,0:T(8,128)(2,1)S(1)}, bf16[64,2304]{1,0:T(8,128)(2,1)S(1)}, u32[]{:S(2)}, u32[]{:S(2)}) collective-permute-start(bf16[64,2304]{1,0:T(8,128)(2,1)S(1)} %get-tuple-element.43), channel_id=1, source_target_pairs={{0,24},{8,0},{16,8},{24,16},{1,25},{9,1},{17,9},{25,17},{2,26},{10... | collective-permute-start | bytes 884744 | tf_op jit(solution)/shard_map/ppermute | solution.py:18
  112.8 10.4 %collective-permute-start.21 = (bf16[64,2304]{1,0:T(8,128)(2,1)S(1)}, bf16[64,2304]{1,0:T(8,128)(2,1)S(1)}, u32[]{:S(2)}, u32[]{:S(2)}) collective-permute-start(bf16[64,2304]{1,0:T(8,128)(2,1)S(1)} %get-tuple-element.44), channel_id=1, source_target_pairs={{0,16},{8,24},{16,0},{24,8},{1,17},{9,25},{17,1},{25,9},{2,18},{10... | collective-permute-start | bytes 884744 | tf_op jit(solution)/shard_map/ppermute | solution.py:18
  113.7 10.5 %collective-permute-start.22 = (bf16[64,2304]{1,0:T(8,128)(2,1)S(1)}, bf16[64,2304]{1,0:T(8,128)(2,1)S(1)}, u32[]{:S(2)}, u32[]{:S(2)}) collective-permute-start(bf16[64,2304]{1,0:T(8,128)(2,1)S(1)} %get-tuple-element.45), channel_id=1, source_target_pairs={{0,8},{8,16},{16,24},{24,0},{1,9},{9,17},{17,25},{25,1},{2,10},{10... | collective-permute-start | bytes 884744 | tf_op jit(solution)/shard_map/ppermute | solution.py:18
  115.6 12.3 %collective-permute-start.17 = (bf16[16,2304]{1,0:T(8,128)(2,1)S(1)}, bf16[16,2304]{1,0:T(8,128)(2,1)S(1)}, u32[]{:S(2)}, u32[]{:S(2)}) collective-permute-start(bf16[16,2304]{1,0:T(8,128)(2,1)S(1)} %get-tuple-element.50), channel_id=1, source_target_pairs={{0,24},{8,0},{16,8},{24,16},{1,25},{9,1},{17,9},{25,17},{2,26},{10... | collective-permute-start | bytes 221192 | tf_op jit(solution)/shard_map/ppermute | solution.py:18
  116.0 13.1 %collective-permute-start.18 = (bf16[16,2304]{1,0:T(8,128)(2,1)S(1)}, bf16[16,2304]{1,0:T(8,128)(2,1)S(1)}, u32[]{:S(2)}, u32[]{:S(2)}) collective-permute-start(bf16[16,2304]{1,0:T(8,128)(2,1)S(1)} %get-tuple-element.52), channel_id=1, source_target_pairs={{0,16},{8,24},{16,0},{24,8},{1,17},{9,25},{17,1},{25,9},{2,18},{10... | collective-permute-start | bytes 221192 | tf_op jit(solution)/shard_map/ppermute | solution.py:18
  119.9 9.3 %collective-permute-start.19 = (bf16[16,2304]{1,0:T(8,128)(2,1)S(1)}, bf16[16,2304]{1,0:T(8,128)(2,1)S(1)}, u32[]{:S(2)}, u32[]{:S(2)}) collective-permute-start(bf16[16,2304]{1,0:T(8,128)(2,1)S(1)} %get-tuple-element.51), channel_id=1, source_target_pairs={{0,8},{8,16},{16,24},{24,0},{1,9},{9,17},{17,25},{25,1},{2,10},{10... | collective-permute-start | bytes 221192 | tf_op jit(solution)/shard_map/ppermute | solution.py:18
  124.4 5.0 %collective-permute-start.23 = (bf16[16,2304]{1,0:T(8,128)(2,1)S(1)}, bf16[16,2304]{1,0:T(8,128)(2,1)S(1)}, u32[]{:S(2)}, u32[]{:S(2)}) collective-permute-start(bf16[16,2304]{1,0:T(8,128)(2,1)S(1)} %get-tuple-element.53), channel_id=1, source_target_pairs={{0,192},{64,0},{128,64},{192,128},{1,193},{65,1},{129,65},{193,129... | collective-permute-start | bytes 221192 | tf_op jit(solution)/shard_map/ppermute | solution.py:18
  127.4 5.9 %collective-permute-start.24 = (bf16[16,2304]{1,0:T(8,128)(2,1)S(1)}, bf16[16,2304]{1,0:T(8,128)(2,1)S(1)}, u32[]{:S(2)}, u32[]{:S(2)}) collective-permute-start(bf16[16,2304]{1,0:T(8,128)(2,1)S(1)} %get-tuple-element.55), channel_id=1, source_target_pairs={{0,128},{64,192},{128,0},{192,64},{1,129},{65,193},{129,1},{193,65... | collective-permute-start | bytes 221192 | tf_op jit(solution)/shard_map/ppermute | solution.py:18
  127.8 6.2 %collective-permute-start.25 = (bf16[16,2304]{1,0:T(8,128)(2,1)S(1)}, bf16[16,2304]{1,0:T(8,128)(2,1)S(1)}, u32[]{:S(2)}, u32[]{:S(2)}) collective-permute-start(bf16[16,2304]{1,0:T(8,128)(2,1)S(1)} %get-tuple-element.54), channel_id=1, source_target_pairs={{0,64},{64,128},{128,192},{192,0},{1,65},{65,129},{129,193},{193,1... | collective-permute-start | bytes 221192 | tf_op jit(solution)/shard_map/ppermute | solution.py:18
  134.9 12.6 %all-to-all-start.2 = ((bf16[8,2,4608]{2,1,0:T(2,128)(2,1)}), bf16[8,2,4608]{2,1,0:T(2,128)(2,1)S(1)}, u32[]{:S(2)}, u32[]{:S(2)}) async-start(bf16[8,2,4608]{2,1,0:T(2,128)(2,1)} %reshape.109), calls=%async_computation.2 | async-start | bytes 294912 | tf_op jit(solution)/shard_map/all_to_all | solution.py:266
  139.0 1.1 collective-permute-start.26

commit v6 on v5

--- a/solution.py
+++ b/solution.py
@@ -218,7 +218,6 @@
     first, second = by_z[:, :half], by_z[:, half:]
     along_x = jnp.concatenate([first] + [shifted(first, "x", e) for e in range(1, n)])
     along_y = jnp.concatenate([second] + [shifted(second, "y", d) for d in range(1, n)])
-    along_x, along_y = lax.optimization_barrier((along_x, along_y))
     late = [along_y] + [shifted(along_y, "x", e) for e in range(1, n)]
     early = [along_x] + [shifted(along_x, "y", d) for d in range(1, n)]
     tail_own = jnp.concatenate([v[:, half:] for v in late])

time: 149 us -> 148 us (level)
  starting transfers between devices: 57.4 us -> 55.7 us
    all_to_all x1, starting transfers between devices: 11 us -> 8.45 us  [body(): lax.all_to_all(send.reshape(peers, lines, 128), ('x', 'y', 'z'), 0, 0, ti...]
    ppermute x24, waiting for transfers between devices: 21.5 us -> 23.3 us  [shifted(): return lax.ppermute(v, axis, [(i, (i + by) % n) for i in range(n)])]
  transfers between devices with their start and end apart: 30 -> 30, of which waited for: 16 -> 13; matrix products, arithmetic and copies ran while one was open for 4% -> 4% of each run, Pallas kernels for 12% -> 12%
where the time goes in v6:
time: 148 us; the launch traced here: 147 us
  starting transfers between devices  55.7 us (38%)
  waiting for transfers between devices  51.5 us (35%)
  Pallas kernels  26.8 us (18%)
  local copies, waits for them, and re-layouts  6.16 us (4%)
  other arithmetic  5.63 us (4%)
  between operations  1.58 us (1%)
    ppermute x24, starting transfers between devices, shifted(): return lax.ppermute(v, axis, [(i, (i + by) % n) for i in range(n)])  35 us
    ppermute x24, waiting for transfers between devices, shifted(): return lax.ppermute(v, axis, [(i, (i + by) % n) for i in range(n)])  23.3 us
    pallas_call x2, Pallas kernels, gradient_part(): pl.pallas_call(functools.partial(gradient_kernel, n), grid=(steps,), out_...  14.5 us
    all_to_all x1, waiting for transfers between devices, body(): lax.all_to_all(send.reshape(peers, lines, 128), ('x', 'y', 'z'), 0, 0, ti...  11.2 us
    pallas_call x1, Pallas kernels, capped_logits(): pl.pallas_call(functools.partial(logits_kernel, n), out_shape=(sums, capp...  10.4 us
    all_to_all x1, waiting for transfers between devices, body(): lax.all_to_all(mine, 'z', 0, 0, tiled=True)  9.15 us
    all_to_all x1, starting transfers between devices, body(): lax.all_to_all(mine, 'z', 0, 0, tiled=True)  8.47 us
    all_to_all x1, starting transfers between devices, body(): lax.all_to_all(send.reshape(peers, lines, 128), ('x', 'y', 'z'), 0, 0, ti...  8.45 us
  transfers between devices with their start and end apart: 30, of which 13 were waited for; matrix products, arithmetic and copies ran while one was open for 4% of the time, Pallas kernels for 12%

profile of v6, /device:TPU:8, one launch (start us, length us, event | category | flops | bytes accessed | tf_op | source)
XLA Modules:
  0.0 147.5 jit_solution(2728938063408944465)
XLA Ops:
  0.6 0.1 collective-permute-start
  0.7 0.7 fusion.3
  1.4 0.1 copy.9
  1.6 0.8 broadcast_in_dim.6
  2.4 0.8 pad_maximum_fusion.2
  3.2 8.5 %all-to-all-start = ((bf16[8,2,4736]{2,1,0:T(2,128)(2,1)}), bf16[8,2,4736]{2,1,0:T(2,128)(2,1)S(1)}, u32[]{:S(2)}, u32[]{:S(2)}) async-start(bf16[8,2,4736]{2,1,0:T(2,128)(2,1)} %pad_maximum_fusion.2), calls=%async_computation | async-start | bytes 303104 | tf_op jit(solution)/shard_map/all_to_all | solution.py:215
  12.7 9.1 %all-to-all-done = bf16[8,2,4736]{2,1,0:T(2,128)(2,1)S(1)} async-done(((bf16[8,2,4736]{2,1,0:T(2,128)(2,1)}), bf16[8,2,4736]{2,1,0:T(2,128)(2,1)S(1)}, u32[]{:S(2)}, u32[]{:S(2)}) %all-to-all-start) | async-done | bytes 151584 | tf_op jit(solution)/shard_map/all_to_all | solution.py:215
  21.9 1.7 %collective-permute-start.1 = (bf16[16,2432]{1,0:T(8,128)(2,1)S(1)}, bf16[16,2432]{1,0:T(8,128)(2,1)S(1)}, u32[]{:S(2)}, u32[]{:S(2)}) collective-permute-start(bf16[16,2432]{1,0:T(8,128)(2,1)S(1)} %slice.75), channel_id=1, source_target_pairs={{0,8},{8,16},{16,24},{24,0},{1,9},{9,17},{17,25},{25,1},{2,10},{10... | collective-permute-start | bytes 233480 | tf_op jit(solution)/shard_map/ppermute | solution.py:18
  23.6 0.9 collective-permute-start.2
  24.5 2.4 %collective-permute-start.3 = (bf16[16,2432]{1,0:T(8,128)(2,1)S(1)}, bf16[16,2432]{1,0:T(8,128)(2,1)S(1)}, u32[]{:S(2)}, u32[]{:S(2)}) collective-permute-start(bf16[16,2432]{1,0:T(8,128)(2,1)S(1)} %slice.75), channel_id=1, source_target_pairs={{0,24},{8,0},{16,8},{24,16},{1,25},{9,1},{17,9},{25,17},{2,26},{10... | collective-permute-start | bytes 233480 | tf_op jit(solution)/shard_map/ppermute | solution.py:18
  27.0 2.8 %collective-permute-start.10 = (bf16[16,2304]{1,0:T(8,128)(2,1)S(1)}, bf16[16,2304]{1,0:T(8,128)(2,1)S(1)}, u32[]{:S(2)}, u32[]{:S(2)}) collective-permute-start(bf16[16,2304]{1,0:T(8,128)(2,1)S(1)} %slice.80), channel_id=1, source_target_pairs={{0,192},{64,0},{128,64},{192,128},{1,193},{65,1},{129,65},{193,129... | collective-permute-start | bytes 221192 | tf_op jit(solution)/shard_map/ppermute | solution.py:18
  29.8 2.3 %collective-permute-start.9 = (bf16[16,2304]{1,0:T(8,128)(2,1)S(1)}, bf16[16,2304]{1,0:T(8,128)(2,1)S(1)}, u32[]{:S(2)}, u32[]{:S(2)}) collective-permute-start(bf16[16,2304]{1,0:T(8,128)(2,1)S(1)} %slice.80), channel_id=1, source_target_pairs={{0,128},{64,192},{128,0},{192,64},{1,129},{65,193},{129,1},{193,65... | collective-permute-start | bytes 221192 | tf_op jit(solution)/shard_map/ppermute | solution.py:18
  32.1 1.9 %collective-permute-start.4 = (bf16[64,2432]{1,0:T(8,128)(2,1)S(1)}, bf16[64,2432]{1,0:T(8,128)(2,1)S(1)}, u32[]{:S(2)}, u32[]{:S(2)}) collective-permute-start(bf16[64,2432]{1,0:T(8,128)(2,1)S(1)} %pad_maximum_fusion.refs_0_), channel_id=1, source_target_pairs={{0,64},{64,128},{128,192},{192,0},{1,65},{65,129},{129,193},{193,1... | collective-permute-start | bytes 933896 | tf_op jit(solution)/shard_map/ppermute | solution.py:18
  34.0 0.8 collective-permute-start.5
  34.8 2.0 %collective-permute-start.6 = (bf16[64,2432]{1,0:T(8,128)(2,1)S(1)}, bf16[64,2432]{1,0:T(8,128)(2,1)S(1)}, u32[]{:S(2)}, u32[]{:S(2)}) collective-permute-start(bf16[64,2432]{1,0:T(8,128)(2,1)S(1)} %pad_maximum_fusion.refs_0_), channel_id=1, source_target_pairs={{0,192},{64,0},{128,64},{192,128},{1,193},{65,1},{129,65},{193,129... | collective-permute-start | bytes 933896 | tf_op jit(solution)/shard_map/ppermute | solution.py:18
  36.8 0.2 collective-permute-done.8
  37.1 3.4 %collective-permute-start.12 = (bf16[64,2304]{1,0:T(8,128)(2,1)S(1)}, bf16[64,2304]{1,0:T(8,128)(2,1)S(1)}, u32[]{:S(2)}, u32[]{:S(2)}) collective-permute-start(bf16[64,2304]{1,0:T(8,128)(2,1)S(1)} %pad_maximum_fusion.1.refs_4_), channel_id=1, source_target_pairs={{0,16},{8,24},{16,0},{24,8},{1,17},{9,25},{17,1},{25,9},{2,18},{10... | collective-permute-start | bytes 884744 | tf_op jit(solution)/shard_map/ppermute | solution.py:18
  40.5 7.4 %collective-permute-done.5.refs_2_ = bf16[64,2432]{1,0:T(8,128)(2,1)S(1)} collective-permute-done((bf16[64,2432]{1,0:T(8,128)(2,1)S(1)}, bf16[64,2432]{1,0:T(8,128)(2,1)S(1)}, u32[]{:S(2)}, u32[]{:S(2)}) %collective-permute-start.5) | collective-permute-done | bytes 311328 | tf_op jit(solution)/shard_map/ppermute | solution.py:18
  47.8 1.7 %collective-permute-start.13 = (bf16[64,2304]{1,0:T(8,128)(2,1)S(1)}, bf16[64,2304]{1,0:T(8,128)(2,1)S(1)}, u32[]{:S(2)}, u32[]{:S(2)}) collective-permute-start(bf16[64,2304]{1,0:T(8,128)(2,1)S(1)} %pad_maximum_fusion.1.refs_4_), channel_id=1, source_target_pairs={{0,24},{8,0},{16,8},{24,16},{1,25},{9,1},{17,9},{25,17},{2,26},{10... | collective-permute-start | bytes 884744 | tf_op jit(solution)/shard_map/ppermute | solution.py:18
  49.8 0.3 collective-permute-start.7
  50.1 4.5 %collective-permute-done.13.refs_7_ = bf16[64,2304]{1,0:T(8,128)(2,1)S(1)} collective-permute-done((bf16[64,2304]{1,0:T(8,128)(2,1)S(1)}, bf16[64,2304]{1,0:T(8,128)(2,1)S(1)}, u32[]{:S(2)}, u32[]{:S(2)}) %collective-permute-start.13) | collective-permute-done | bytes 294944 | tf_op jit(solution)/shard_map/ppermute | solution.py:18
  54.6 10.4 %shard_map.68 = (f32[256,128]{1,0:T(8,128)S(1)}, f32[256,1000]{1,0:T(8,128)}, f32[256,1000]{1,0:T(8,128)}) custom-call(s32[34]{0:T(128)S(1)} %pad_add_fusion.where_ref, bf16[64,2432]{1,0:T(8,128)(2,1)S(1)} %pad_maximum_fusion.refs_0_, bf16[64,2432]{1,0:T(8,128)(2,1)S(1)} %collective-permute-done.4.refs_1_, bf16[64,2432]{1,0:T(8,128)(2,1)} %copy-done.2, ...), custom_call_target="tpu_custom_call" | custom-call | flops 4718592000 | bytes 23150592 | tf_op jit(solution)/shard_map/pallas_call | solution.py:80
  65.0 1.2 copy-done
  66.3 1.2 copy-done.1
  67.5 1.9 %shard_map.69 = (f32[8,256]{1,0:T(8,128)S(1)}, f32[512,128]{1,0:T(8,128)}) custom-call(s32[34]{0:T(128)S(1)} %pad_add_fusion.where_ref, bf16[256,128]{1,0:T(8,128)(2,1)S(1)} %pad_maximum_fusion.4.own_ref, bf16[256,128]{1,0:T(8,128)(2,1)S(1)} %collective-permute-done.7.sib_ref, f32[256,128]{1,0:T(8,128)S(1)} %get-tuple-element.25.sums_ref, ...), custom_call_target="tpu_custom_call" | custom-call | tf_op jit(solution)/shard_map/pallas_call | solution.py:129
  69.5 0.1 reduce_sum.47
  69.6 0.6 slice.83
  70.3 0.1 reduce_sum.46
  70.4 8.5 %all-to-all-start.1 = ((f32[128,4,128]{2,1,0:T(4,128)}), f32[128,4,128]{2,1,0:T(4,128)S(1)}, u32[]{:S(2)}, u32[]{:S(2)}) async-start(f32[128,4,128]{2,1,0:T(4,128)} %bitcast.6), calls=%async_computation.1 | async-start | bytes 524288 | tf_op jit(solution)/shard_map/all_to_all | solution.py:237
  78.9 0.7 fusion
  79.7 0.1 broadcast_select_fusion.1
  80.0 11.2 %all-to-all-done.1 = f32[128,4,128]{2,1,0:T(4,128)S(1)} async-done(((f32[128,4,128]{2,1,0:T(4,128)}), f32[128,4,128]{2,1,0:T(4,128)S(1)}, u32[]{:S(2)}, u32[]{:S(2)}) %all-to-all-start.1) | async-done | bytes 262176 | tf_op jit(solution)/shard_map/all_to_all | solution.py:237
  91.1 0.1 reduce_sum.45
  91.3 7.2 %shard_map.70 = (bf16[64,2304]{1,0:T(8,128)(2,1)S(1)}, bf16[64,2304]{1,0:T(8,128)(2,1)S(1)}, bf16[64,2304]{1,0:T(8,128)(2,1)S(1)}, bf16[64,2304]{1,0:T(8,128)(2,1)S(1)}) custom-call(s32[34]{0:T(128)S(1)} %pad_add_fusion.where_ref, f32[8,256]{1,0:T(8,128)S(1)} %stack.46.rows_ref, f32[256,1000]{1,0:T(8,128)} %get-tuple-element.26.own_c, ...), custom_call_target="tpu_custom_call" | custom-call | flops 2359296000 | bytes 10395648 | tf_op jit(solution)/shard_map/pallas_call | solution.py:176
  98.6 0.9 collective-permute-start.14
  99.4 1.9 %collective-permute-start.15 = (bf16[64,2304]{1,0:T(8,128)(2,1)S(1)}, bf16[64,2304]{1,0:T(8,128)(2,1)S(1)}, u32[]{:S(2)}, u32[]{:S(2)}) collective-permute-start(bf16[64,2304]{1,0:T(8,128)(2,1)S(1)} %get-tuple-element.32), channel_id=1, source_target_pairs={{0,128},{64,192},{128,0},{192,64},{1,129},{65,193},{129,1},{193,65... | collective-permute-start | bytes 884744 | tf_op jit(solution)/shard_map/ppermute | solution.py:18
  101.3 0.3 collective-permute-start.16
  101.6 7.2 %shard_map.71 = (bf16[64,2304]{1,0:T(8,128)(2,1)S(1)}, bf16[64,2304]{1,0:T(8,128)(2,1)S(1)}, bf16[64,2304]{1,0:T(8,128)(2,1)S(1)}, bf16[64,2304]{1,0:T(8,128)(2,1)S(1)}) custom-call(s32[18]{0:T(128)S(1)} %pad_add_fusion.1.where_ref, f32[8,256]{1,0:T(8,128)S(1)} %stack.46.rows_ref, f32[256,1000]{1,0:T(8,128)} %get-tuple-element.26.own_c, ...), custom_call_target="tpu_custom_call" | custom-call | flops 2359296000 | bytes 10395648 | tf_op jit(solution)/shard_map/pallas_call | solution.py:176
  108.9 0.1 reduce_sum.49
  109.1 0.6 slice.96
  109.7 1.4 collective-permute-start.20
  111.0 1.0 collective-permute-start.21
  112.0 1.6 %collective-permute-start.22 = (bf16[64,2304]{1,0:T(8,128)(2,1)S(1)}, bf16[64,2304]{1,0:T(8,128)(2,1)S(1)}, u32[]{:S(2)}, u32[]{:S(2)}) collective-permute-start(bf16[64,2304]{1,0:T(8,128)(2,1)S(1)} %get-tuple-element.41), channel_id=1, source_target_pairs={{0,8},{8,16},{16,24},{24,0},{1,9},{9,17},{17,25},{25,1},{2,10},{10... | collective-permute-start | bytes 884744 | tf_op jit(solution)/shard_map/ppermute | solution.py:18
  113.7 0.1 add_convert_fusion.1
  113.9 0.8 collective-permute-start.17
  114.7 2.2 %collective-permute-start.18 = (bf16[16,2304]{1,0:T(8,128)(2,1)S(1)}, bf16[16,2304]{1,0:T(8,128)(2,1)S(1)}, u32[]{:S(2)}, u32[]{:S(2)}) collective-permute-start(bf16[16,2304]{1,0:T(8,128)(2,1)S(1)} %get-tuple-element.48), channel_id=1, source_target_pairs={{0,16},{8,24},{16,0},{24,8},{1,17},{9,25},{17,1},{25,9},{2,18},{10... | collective-permute-start | bytes 221192 | tf_op jit(solution)/shard_map/ppermute | solution.py:18
  116.9 2.3 %collective-permute-done.20 = bf16[64,2304]{1,0:T(8,128)(2,1)S(1)} collective-permute-done((bf16[64,2304]{1,0:T(8,128)(2,1)S(1)}, bf16[64,2304]{1,0:T(8,128)(2,1)S(1)}, u32[]{:S(2)}, u32[]{:S(2)}) %collective-permute-start.20) | collective-permute-done | bytes 294944 | tf_op jit(solution)/shard_map/ppermute | solution.py:18
  119.1 0.6 collective-permute-start.19
  119.7 2.7 %collective-permute-done.21 = bf16[64,2304]{1,0:T(8,128)(2,1)S(1)} collective-permute-done((bf16[64,2304]{1,0:T(8,128)(2,1)S(1)}, bf16[64,2304]{1,0:T(8,128)(2,1)S(1)}, u32[]{:S(2)}, u32[]{:S(2)}) %collective-permute-start.21) | collective-permute-done | bytes 294944 | tf_op jit(solution)/shard_map/ppermute | solution.py:18
  122.4 1.4 collective-permute-done.22
  123.8 0.1 add_convert_fusion
  124.0 2.7 %collective-permute-start.23 = (bf16[16,2304]{1,0:T(8,128)(2,1)S(1)}, bf16[16,2304]{1,0:T(8,128)(2,1)S(1)}, u32[]{:S(2)}, u32[]{:S(2)}) collective-permute-start(bf16[16,2304]{1,0:T(8,128)(2,1)S(1)} %get-tuple-element.49), channel_id=1, source_target_pairs={{0,192},{64,0},{128,64},{192,128},{1,193},{65,1},{129,65},{193,129... | collective-permute-start | bytes 221192 | tf_op jit(solution)/shard_map/ppermute | solution.py:18
  126.7 0.4 collective-permute-start.24
  127.2 1.2 collective-permute-start.25
  128.5 0.2 collective-permute-done.23
  128.7 3.9 %collective-permute-done.24 = bf16[16,2304]{1,0:T(8,128)(2,1)S(1)} collective-permute-done((bf16[16,2304]{1,0:T(8,128)(2,1)S(1)}, bf16[16,2304]{1,0:T(8,128)(2,1)S(1)}, u32[]{:S(2)}, u32[]{:S(2)}) %collective-permute-start.24) | collective-permute-done | bytes 73760 | tf_op jit(solution)/shard_map/ppermute | solution.py:18
  132.7 0.7 collective-permute-done.25
  133.5 0.7 reshape.109
  134.2 3.4 %all-to-all-start.2 = ((bf16[8,2,4608]{2,1,0:T(2,128)(2,1)}), bf16[8,2,4608]{2,1,0:T(2,128)(2,1)S(1)}, u32[]{:S(2)}, u32[]{:S(2)}) async-start(bf16[8,2,4608]{2,1,0:T(2,128)(2,1)} %reshape.109), calls=%async_computation.2 | async-start | bytes 294912 | tf_op jit(solution)/shard_map/all_to_all | solution.py:265
  137.6 0.7 broadcast_select_fusion
  138.3 1.1 collective-permute-done.26
  139.4 0.5 add_divide_fusion
  139.9 6.8 %all-to-all-done.2 = bf16[8,2,4608]{2,1,0:T(2,128)(2,1)S(1)} async-done(((bf16[8,2,4608]{2,1,0:T(2,128)(2,1)}), bf16[8,2,4608]{2,1,0:T(2,128)(2,1)S(1)}, u32[]{:S(2)}, u32[]{:S(2)}) %all-to-all-start.2) | async-done | bytes 147488 | tf_op jit(solution)/shard_map/all_to_all | solution.py:265
  146.7 0.7 convert_reduce_fusion
  (66 shorter events, 1.6 us)
Async XLA Ops:
  0.6 21.2 %collective-permute-start = (bf16[1000,4608]{1,0:T(8,128)(2,1)}, bf16[1000,4608]{1,0:T(8,128)(2,1)}, u32[]{:S(2)}, u32[]{:S(2)}) collective-permute-start(bf16[1000,4608]{1,0:T(8,128)(2,1)} %own_ref.3), channel_id=1, source_target_pairs={{0,32},{32,0},{1,33},{33,1},{2,34},{34,2},{3,35},{35,3},{4,36},{36... | collective-permute-start | bytes 27648008 | tf_op jit(solution)/shard_map/ppermute | solution.py:209
  3.2 18.6 %all-to-all-start = ((bf16[8,2,4736]{2,1,0:T(2,128)(2,1)}), bf16[8,2,4736]{2,1,0:T(2,128)(2,1)S(1)}, u32[]{:S(2)}, u32[]{:S(2)}) async-start(bf16[8,2,4736]{2,1,0:T(2,128)(2,1)} %pad_maximum_fusion.2), calls=%async_computation | async-start | bytes 303104 | tf_op jit(solution)/shard_map/all_to_all | solution.py:215
  21.9 7.9 %collective-permute-start.1 = (bf16[16,2432]{1,0:T(8,128)(2,1)S(1)}, bf16[16,2432]{1,0:T(8,128)(2,1)S(1)}, u32[]{:S(2)}, u32[]{:S(2)}) collective-permute-start(bf16[16,2432]{1,0:T(8,128)(2,1)S(1)} %slice.75), channel_id=1, source_target_pairs={{0,8},{8,16},{16,24},{24,0},{1,9},{9,17},{17,25},{25,1},{2,10},{10... | collective-permute-start | bytes 233480 | tf_op jit(solution)/shard_map/ppermute | solution.py:18
  23.6 8.5 %collective-permute-start.2 = (bf16[16,2432]{1,0:T(8,128)(2,1)S(1)}, bf16[16,2432]{1,0:T(8,128)(2,1)S(1)}, u32[]{:S(2)}, u32[]{:S(2)}) collective-permute-start(bf16[16,2432]{1,0:T(8,128)(2,1)S(1)} %slice.75), channel_id=1, source_target_pairs={{0,16},{8,24},{16,0},{24,8},{1,17},{9,25},{17,1},{25,9},{2,18},{10... | collective-permute-start | bytes 233480 | tf_op jit(solution)/shard_map/ppermute | solution.py:18
  24.5 7.6 %collective-permute-start.3 = (bf16[16,2432]{1,0:T(8,128)(2,1)S(1)}, bf16[16,2432]{1,0:T(8,128)(2,1)S(1)}, u32[]{:S(2)}, u32[]{:S(2)}) collective-permute-start(bf16[16,2432]{1,0:T(8,128)(2,1)S(1)} %slice.75), channel_id=1, source_target_pairs={{0,24},{8,0},{16,8},{24,16},{1,25},{9,1},{17,9},{25,17},{2,26},{10... | collective-permute-start | bytes 233480 | tf_op jit(solution)/shard_map/ppermute | solution.py:18
  27.0 7.8 %collective-permute-start.10 = (bf16[16,2304]{1,0:T(8,128)(2,1)S(1)}, bf16[16,2304]{1,0:T(8,128)(2,1)S(1)}, u32[]{:S(2)}, u32[]{:S(2)}) collective-permute-start(bf16[16,2304]{1,0:T(8,128)(2,1)S(1)} %slice.80), channel_id=1, source_target_pairs={{0,192},{64,0},{128,64},{192,128},{1,193},{65,1},{129,65},{193,129... | collective-permute-start | bytes 221192 | tf_op jit(solution)/shard_map/ppermute | solution.py:18
  29.8 7.2 %collective-permute-start.8 = (bf16[16,2304]{1,0:T(8,128)(2,1)S(1)}, bf16[16,2304]{1,0:T(8,128)(2,1)S(1)}, u32[]{:S(2)}, u32[]{:S(2)}) collective-permute-start(bf16[16,2304]{1,0:T(8,128)(2,1)S(1)} %slice.80), channel_id=1, source_target_pairs={{0,64},{64,128},{128,192},{192,0},{1,65},{65,129},{129,193},{193,1... | collective-permute-start | bytes 221192 | tf_op jit(solution)/shard_map/ppermute | solution.py:18
  29.8 7.2 %collective-permute-start.9 = (bf16[16,2304]{1,0:T(8,128)(2,1)S(1)}, bf16[16,2304]{1,0:T(8,128)(2,1)S(1)}, u32[]{:S(2)}, u32[]{:S(2)}) collective-permute-start(bf16[16,2304]{1,0:T(8,128)(2,1)S(1)} %slice.80), channel_id=1, source_target_pairs={{0,128},{64,192},{128,0},{192,64},{1,129},{65,193},{129,1},{193,65... | collective-permute-start | bytes 221192 | tf_op jit(solution)/shard_map/ppermute | solution.py:18
  32.1 17.6 %collective-permute-start.4 = (bf16[64,2432]{1,0:T(8,128)(2,1)S(1)}, bf16[64,2432]{1,0:T(8,128)(2,1)S(1)}, u32[]{:S(2)}, u32[]{:S(2)}) collective-permute-start(bf16[64,2432]{1,0:T(8,128)(2,1)S(1)} %pad_maximum_fusion.refs_0_), channel_id=1, source_target_pairs={{0,64},{64,128},{128,192},{192,0},{1,65},{65,129},{129,193},{193,1... | collective-permute-start | bytes 933896 | tf_op jit(solution)/shard_map/ppermute | solution.py:18
  34.0 13.8 %collective-permute-start.5 = (bf16[64,2432]{1,0:T(8,128)(2,1)S(1)}, bf16[64,2432]{1,0:T(8,128)(2,1)S(1)}, u32[]{:S(2)}, u32[]{:S(2)}) collective-permute-start(bf16[64,2432]{1,0:T(8,128)(2,1)S(1)} %pad_maximum_fusion.refs_0_), channel_id=1, source_target_pairs={{0,128},{64,192},{128,0},{192,64},{1,129},{65,193},{129,1},{193,65... | collective-permute-start | bytes 933896 | tf_op jit(solution)/shard_map/ppermute | solution.py:18
  34.8 14.9 %collective-permute-start.6 = (bf16[64,2432]{1,0:T(8,128)(2,1)S(1)}, bf16[64,2432]{1,0:T(8,128)(2,1)S(1)}, u32[]{:S(2)}, u32[]{:S(2)}) collective-permute-start(bf16[64,2432]{1,0:T(8,128)(2,1)S(1)} %pad_maximum_fusion.refs_0_), channel_id=1, source_target_pairs={{0,192},{64,0},{128,64},{192,128},{1,193},{65,1},{129,65},{193,129... | collective-permute-start | bytes 933896 | tf_op jit(solution)/shard_map/ppermute | solution.py:18
  37.0 13.1 %collective-permute-start.11 = (bf16[64,2304]{1,0:T(8,128)(2,1)S(1)}, bf16[64,2304]{1,0:T(8,128)(2,1)S(1)}, u32[]{:S(2)}, u32[]{:S(2)}) collective-permute-start(bf16[64,2304]{1,0:T(8,128)(2,1)S(1)} %pad_maximum_fusion.1.refs_4_), channel_id=1, source_target_pairs={{0,8},{8,16},{16,24},{24,0},{1,9},{9,17},{17,25},{25,1},{2,10},{10... | collective-permute-start | bytes 884744 | tf_op jit(solution)/shard_map/ppermute | solution.py:18
  37.1 13.0 %collective-permute-start.12 = (bf16[64,2304]{1,0:T(8,128)(2,1)S(1)}, bf16[64,2304]{1,0:T(8,128)(2,1)S(1)}, u32[]{:S(2)}, u32[]{:S(2)}) collective-permute-start(bf16[64,2304]{1,0:T(8,128)(2,1)S(1)} %pad_maximum_fusion.1.refs_4_), channel_id=1, source_target_pairs={{0,16},{8,24},{16,0},{24,8},{1,17},{9,25},{17,1},{25,9},{2,18},{10... | collective-permute-start | bytes 884744 | tf_op jit(solution)/shard_map/ppermute | solution.py:18
  47.8 6.7 %copy-start.2 = (bf16[64,2432]{1,0:T(8,128)(2,1)}, bf16[64,2432]{1,0:T(8,128)(2,1)S(1)}, u32[]{:S(2)}) copy-start(bf16[64,2432]{1,0:T(8,128)(2,1)S(1)} %collective-permute-done.5.refs_2_) | copy-start | bytes 933892
  47.8 6.7 %collective-permute-start.13 = (bf16[64,2304]{1,0:T(8,128)(2,1)S(1)}, bf16[64,2304]{1,0:T(8,128)(2,1)S(1)}, u32[]{:S(2)}, u32[]{:S(2)}) collective-permute-start(bf16[64,2304]{1,0:T(8,128)(2,1)S(1)} %pad_maximum_fusion.1.refs_4_), channel_id=1, source_target_pairs={{0,24},{8,0},{16,8},{24,16},{1,25},{9,1},{17,9},{25,17},{2,26},{10... | collective-permute-start | bytes 884744 | tf_op jit(solution)/shard_map/ppermute | solution.py:18
  49.7 4.8 %copy-start.3 = (bf16[64,2432]{1,0:T(8,128)(2,1)}, bf16[64,2432]{1,0:T(8,128)(2,1)S(1)}, u32[]{:S(2)}) copy-start(bf16[64,2432]{1,0:T(8,128)(2,1)S(1)} %collective-permute-done.6.refs_3_) | copy-start | bytes 933892
  49.8 15.2 %collective-permute-start.7 = (bf16[256,128]{1,0:T(8,128)(2,1)S(1)}, bf16[256,128]{1,0:T(8,128)(2,1)S(1)}, u32[]{:S(2)}, u32[]{:S(2)}) collective-permute-start(bf16[256,128]{1,0:T(8,128)(2,1)S(1)} %pad_maximum_fusion.4.own_ref), channel_id=1, source_target_pairs={{0,32},{32,0},{1,33},{33,1},{2,34},{34,2},{3,35},{35,3},{4,36},{36... | collective-permute-start | bytes 196616 | tf_op jit(solution)/shard_map/ppermute | solution.py:224
  65.0 1.2 copy-start
  66.3 1.2 copy-start.1
  70.4 20.7 %all-to-all-start.1 = ((f32[128,4,128]{2,1,0:T(4,128)}), f32[128,4,128]{2,1,0:T(4,128)S(1)}, u32[]{:S(2)}, u32[]{:S(2)}) async-start(f32[128,4,128]{2,1,0:T(4,128)} %bitcast.6), calls=%async_computation.1 | async-start | bytes 524288 | tf_op jit(solution)/shard_map/all_to_all | solution.py:237
  98.6 13.5 %collective-permute-start.14 = (bf16[64,2304]{1,0:T(8,128)(2,1)S(1)}, bf16[64,2304]{1,0:T(8,128)(2,1)S(1)}, u32[]{:S(2)}, u32[]{:S(2)}) collective-permute-start(bf16[64,2304]{1,0:T(8,128)(2,1)S(1)} %get-tuple-element.31), channel_id=1, source_target_pairs={{0,192},{64,0},{128,64},{192,128},{1,193},{65,1},{129,65},{193,129... | collective-permute-start | bytes 884744 | tf_op jit(solution)/shard_map/ppermute | solution.py:18
  99.4 14.3 %collective-permute-start.15 = (bf16[64,2304]{1,0:T(8,128)(2,1)S(1)}, bf16[64,2304]{1,0:T(8,128)(2,1)S(1)}, u32[]{:S(2)}, u32[]{:S(2)}) collective-permute-start(bf16[64,2304]{1,0:T(8,128)(2,1)S(1)} %get-tuple-element.32), channel_id=1, source_target_pairs={{0,128},{64,192},{128,0},{192,64},{1,129},{65,193},{129,1},{193,65... | collective-permute-start | bytes 884744 | tf_op jit(solution)/shard_map/ppermute | solution.py:18
  101.3 12.4 %collective-permute-start.16 = (bf16[64,2304]{1,0:T(8,128)(2,1)S(1)}, bf16[64,2304]{1,0:T(8,128)(2,1)S(1)}, u32[]{:S(2)}, u32[]{:S(2)}) collective-permute-start(bf16[64,2304]{1,0:T(8,128)(2,1)S(1)} %get-tuple-element.33), channel_id=1, source_target_pairs={{0,64},{64,128},{128,192},{192,0},{1,65},{65,129},{129,193},{193,1... | collective-permute-start | bytes 884744 | tf_op jit(solution)/shard_map/ppermute | solution.py:18
  109.7 9.5 %collective-permute-start.20 = (bf16[64,2304]{1,0:T(8,128)(2,1)S(1)}, bf16[64,2304]{1,0:T(8,128)(2,1)S(1)}, u32[]{:S(2)}, u32[]{:S(2)}) collective-permute-start(bf16[64,2304]{1,0:T(8,128)(2,1)S(1)} %get-tuple-element.39), channel_id=1, source_target_pairs={{0,24},{8,0},{16,8},{24,16},{1,25},{9,1},{17,9},{25,17},{2,26},{10... | collective-permute-start | bytes 884744 | tf_op jit(solution)/shard_map/ppermute | solution.py:18
  111.0 11.4 %collective-permute-start.21 = (bf16[64,2304]{1,0:T(8,128)(2,1)S(1)}, bf16[64,2304]{1,0:T(8,128)(2,1)S(1)}, u32[]{:S(2)}, u32[]{:S(2)}) collective-permute-start(bf16[64,2304]{1,0:T(8,128)(2,1)S(1)} %get-tuple-element.40), channel_id=1, source_target_pairs={{0,16},{8,24},{16,0},{24,8},{1,17},{9,25},{17,1},{25,9},{2,18},{10... | collective-permute-start | bytes 884744 | tf_op jit(solution)/shard_map/ppermute | solution.py:18
  112.0 11.8 %collective-permute-start.22 = (bf16[64,2304]{1,0:T(8,128)(2,1)S(1)}, bf16[64,2304]{1,0:T(8,128)(2,1)S(1)}, u32[]{:S(2)}, u32[]{:S(2)}) collective-permute-start(bf16[64,2304]{1,0:T(8,128)(2,1)S(1)} %get-tuple-element.41), channel_id=1, source_target_pairs={{0,8},{8,16},{16,24},{24,0},{1,9},{9,17},{17,25},{25,1},{2,10},{10... | collective-permute-start | bytes 884744 | tf_op jit(solution)/shard_map/ppermute | solution.py:18
  113.9 13.3 %collective-permute-start.17 = (bf16[16,2304]{1,0:T(8,128)(2,1)S(1)}, bf16[16,2304]{1,0:T(8,128)(2,1)S(1)}, u32[]{:S(2)}, u32[]{:S(2)}) collective-permute-start(bf16[16,2304]{1,0:T(8,128)(2,1)S(1)} %get-tuple-element.46), channel_id=1, source_target_pairs={{0,24},{8,0},{16,8},{24,16},{1,25},{9,1},{17,9},{25,17},{2,26},{10... | collective-permute-start | bytes 221192 | tf_op jit(solution)/shard_map/ppermute | solution.py:18
  114.7 13.7 %collective-permute-start.18 = (bf16[16,2304]{1,0:T(8,128)(2,1)S(1)}, bf16[16,2304]{1,0:T(8,128)(2,1)S(1)}, u32[]{:S(2)}, u32[]{:S(2)}) collective-permute-start(bf16[16,2304]{1,0:T(8,128)(2,1)S(1)} %get-tuple-element.48), channel_id=1, source_target_pairs={{0,16},{8,24},{16,0},{24,8},{1,17},{9,25},{17,1},{25,9},{2,18},{10... | collective-permute-start | bytes 221192 | tf_op jit(solution)/shard_map/ppermute | solution.py:18
  119.1 9.3 %collective-permute-start.19 = (bf16[16,2304]{1,0:T(8,128)(2,1)S(1)}, bf16[16,2304]{1,0:T(8,128)(2,1)S(1)}, u32[]{:S(2)}, u32[]{:S(2)}) collective-permute-start(bf16[16,2304]{1,0:T(8,128)(2,1)S(1)} %get-tuple-element.47), channel_id=1, source_target_pairs={{0,8},{8,16},{16,24},{24,0},{1,9},{9,17},{17,25},{25,1},{2,10},{10... | collective-permute-start | bytes 221192 | tf_op jit(solution)/shard_map/ppermute | solution.py:18
  124.0 4.7 %collective-permute-start.23 = (bf16[16,2304]{1,0:T(8,128)(2,1)S(1)}, bf16[16,2304]{1,0:T(8,128)(2,1)S(1)}, u32[]{:S(2)}, u32[]{:S(2)}) collective-permute-start(bf16[16,2304]{1,0:T(8,128)(2,1)S(1)} %get-tuple-element.49), channel_id=1, source_target_pairs={{0,192},{64,0},{128,64},{192,128},{1,193},{65,1},{129,65},{193,129... | collective-permute-start | bytes 221192 | tf_op jit(solution)/shard_map/ppermute | solution.py:18
  126.7 5.9 %collective-permute-start.24 = (bf16[16,2304]{1,0:T(8,128)(2,1)S(1)}, bf16[16,2304]{1,0:T(8,128)(2,1)S(1)}, u32[]{:S(2)}, u32[]{:S(2)}) collective-permute-start(bf16[16,2304]{1,0:T(8,128)(2,1)S(1)} %get-tuple-element.51), channel_id=1, source_target_pairs={{0,128},{64,192},{128,0},{192,64},{1,129},{65,193},{129,1},{193,65... | collective-permute-start | bytes 221192 | tf_op jit(solution)/shard_map/ppermute | solution.py:18
  127.2 6.2 %collective-permute-start.25 = (bf16[16,2304]{1,0:T(8,128)(2,1)S(1)}, bf16[16,2304]{1,0:T(8,128)(2,1)S(1)}, u32[]{:S(2)}, u32[]{:S(2)}) collective-permute-start(bf16[16,2304]{1,0:T(8,128)(2,1)S(1)} %get-tuple-element.50), channel_id=1, source_target_pairs={{0,64},{64,128},{128,192},{192,0},{1,65},{65,129},{129,193},{193,1... | collective-permute-start | bytes 221192 | tf_op jit(solution)/shard_map/ppermute | solution.py:18
  134.2 12.6 %all-to-all-start.2 = ((bf16[8,2,4608]{2,1,0:T(2,128)(2,1)}), bf16[8,2,4608]{2,1,0:T(2,128)(2,1)S(1)}, u32[]{:S(2)}, u32[]{:S(2)}) async-start(bf16[8,2,4608]{2,1,0:T(2,128)(2,1)} %reshape.109), calls=%async_computation.2 | async-start | bytes 294912 | tf_op jit(solution)/shard_map/all_to_all | solution.py:265
  138.3 1.1 collective-permute-start.26

commit v7 on v6

--- a/solution.py
+++ b/solution.py
@@ -135,7 +135,7 @@
         in_specs=[pl.BlockSpec(memory_space=pltpu.SMEM)] + [vmem] * 5,
         out_specs=(vmem, vmem),
         scratch_shapes=[pltpu.VMEM((plane, TAIL), jnp.float32)] * 2,
-        compiler_params=pltpu.CompilerParams(vmem_limit_bytes=8 * 1024 * 1024),
+        compiler_params=pltpu.CompilerParams(vmem_limit_bytes=60 * 1024 * 1024),
     )(where, own_tail, sib_tail, sums, own_c, sib_c)
 
 

time: 148 us -> 150 us (1.014)
  transfers between devices with their start and end apart: 30 -> 30, of which waited for: 13 -> 13; matrix products, arithmetic and copies ran while one was open for 4% -> 5% of each run, Pallas kernels for 12% -> 12%
where the time goes in v7:
time: 150 us; the launch traced here: 149 us
  starting transfers between devices  55.8 us (37%)
  waiting for transfers between devices  50.8 us (34%)
  Pallas kernels  27.9 us (19%)
  local copies, waits for them, and re-layouts  6.51 us (4%)
  other arithmetic  6.38 us (4%)
  between operations  1.61 us (1%)
    ppermute x24, starting transfers between devices, shifted(): return lax.ppermute(v, axis, [(i, (i + by) % n) for i in range(n)])  35.1 us
    ppermute x24, waiting for transfers between devices, shifted(): return lax.ppermute(v, axis, [(i, (i + by) % n) for i in range(n)])  23.3 us
    pallas_call x2, Pallas kernels, gradient_part(): pl.pallas_call(functools.partial(gradient_kernel, n), grid=(steps,), out_...  14.5 us
    pallas_call x1, Pallas kernels, capped_logits(): pl.pallas_call(functools.partial(logits_kernel, n), out_shape=(sums, capp...  10.4 us
    all_to_all x1, waiting for transfers between devices, body(): lax.all_to_all(send.reshape(peers, lines, 128), ('x', 'y', 'z'), 0, 0, ti...  10.4 us
    all_to_all x1, waiting for transfers between devices, body(): lax.all_to_all(mine, 'z', 0, 0, tiled=True)  9.15 us
    all_to_all x1, starting transfers between devices, body(): lax.all_to_all(mine, 'z', 0, 0, tiled=True)  8.47 us
    all_to_all x1, starting transfers between devices, body(): lax.all_to_all(send.reshape(peers, lines, 128), ('x', 'y', 'z'), 0, 0, ti...  8.45 us
  transfers between devices with their start and end apart: 30, of which 13 were waited for; matrix products, arithmetic and copies ran while one was open for 5% of the time, Pallas kernels for 12%

profile of v7, /device:TPU:8, one launch (start us, length us, event | category | flops | bytes accessed | tf_op | source)
XLA Modules:
  0.0 149.0 jit_solution(4447254991910171936)
XLA Ops:
  0.7 0.7 fusion.3
  1.6 0.8 broadcast_in_dim.6
  2.4 0.8 pad_maximum_fusion.2
  3.2 8.5 %all-to-all-start = ((bf16[8,2,4736]{2,1,0:T(2,128)(2,1)}), bf16[8,2,4736]{2,1,0:T(2,128)(2,1)S(1)}, u32[]{:S(2)}, u32[]{:S(2)}) async-start(bf16[8,2,4736]{2,1,0:T(2,128)(2,1)} %pad_maximum_fusion.2), calls=%async_computation | async-start | bytes 303104 | tf_op jit(solution)/shard_map/all_to_all | solution.py:215
  12.7 9.1 %all-to-all-done = bf16[8,2,4736]{2,1,0:T(2,128)(2,1)S(1)} async-done(((bf16[8,2,4736]{2,1,0:T(2,128)(2,1)}), bf16[8,2,4736]{2,1,0:T(2,128)(2,1)S(1)}, u32[]{:S(2)}, u32[]{:S(2)}) %all-to-all-start) | async-done | bytes 151584 | tf_op jit(solution)/shard_map/all_to_all | solution.py:215
  21.9 1.7 %collective-permute-start.1 = (bf16[16,2432]{1,0:T(8,128)(2,1)S(1)}, bf16[16,2432]{1,0:T(8,128)(2,1)S(1)}, u32[]{:S(2)}, u32[]{:S(2)}) collective-permute-start(bf16[16,2432]{1,0:T(8,128)(2,1)S(1)} %slice.75), channel_id=1, source_target_pairs={{0,8},{8,16},{16,24},{24,0},{1,9},{9,17},{17,25},{25,1},{2,10},{10... | collective-permute-start | bytes 233480 | tf_op jit(solution)/shard_map/ppermute | solution.py:18
  23.6 0.9 collective-permute-start.2
  24.5 2.4 %collective-permute-start.3 = (bf16[16,2432]{1,0:T(8,128)(2,1)S(1)}, bf16[16,2432]{1,0:T(8,128)(2,1)S(1)}, u32[]{:S(2)}, u32[]{:S(2)}) collective-permute-start(bf16[16,2432]{1,0:T(8,128)(2,1)S(1)} %slice.75), channel_id=1, source_target_pairs={{0,24},{8,0},{16,8},{24,16},{1,25},{9,1},{17,9},{25,17},{2,26},{10... | collective-permute-start | bytes 233480 | tf_op jit(solution)/shard_map/ppermute | solution.py:18
  27.0 2.8 %collective-permute-start.10 = (bf16[16,2304]{1,0:T(8,128)(2,1)S(1)}, bf16[16,2304]{1,0:T(8,128)(2,1)S(1)}, u32[]{:S(2)}, u32[]{:S(2)}) collective-permute-start(bf16[16,2304]{1,0:T(8,128)(2,1)S(1)} %slice.80), channel_id=1, source_target_pairs={{0,192},{64,0},{128,64},{192,128},{1,193},{65,1},{129,65},{193,129... | collective-permute-start | bytes 221192 | tf_op jit(solution)/shard_map/ppermute | solution.py:18
  29.8 2.3 %collective-permute-start.9 = (bf16[16,2304]{1,0:T(8,128)(2,1)S(1)}, bf16[16,2304]{1,0:T(8,128)(2,1)S(1)}, u32[]{:S(2)}, u32[]{:S(2)}) collective-permute-start(bf16[16,2304]{1,0:T(8,128)(2,1)S(1)} %slice.80), channel_id=1, source_target_pairs={{0,128},{64,192},{128,0},{192,64},{1,129},{65,193},{129,1},{193,65... | collective-permute-start | bytes 221192 | tf_op jit(solution)/shard_map/ppermute | solution.py:18
  32.1 1.9 %collective-permute-start.4 = (bf16[64,2432]{1,0:T(8,128)(2,1)S(1)}, bf16[64,2432]{1,0:T(8,128)(2,1)S(1)}, u32[]{:S(2)}, u32[]{:S(2)}) collective-permute-start(bf16[64,2432]{1,0:T(8,128)(2,1)S(1)} %pad_maximum_fusion.refs_0_), channel_id=1, source_target_pairs={{0,64},{64,128},{128,192},{192,0},{1,65},{65,129},{129,193},{193,1... | collective-permute-start | bytes 933896 | tf_op jit(solution)/shard_map/ppermute | solution.py:18
  34.0 0.8 collective-permute-start.5
  34.8 2.0 %collective-permute-start.6 = (bf16[64,2432]{1,0:T(8,128)(2,1)S(1)}, bf16[64,2432]{1,0:T(8,128)(2,1)S(1)}, u32[]{:S(2)}, u32[]{:S(2)}) collective-permute-start(bf16[64,2432]{1,0:T(8,128)(2,1)S(1)} %pad_maximum_fusion.refs_0_), channel_id=1, source_target_pairs={{0,192},{64,0},{128,64},{192,128},{1,193},{65,1},{129,65},{193,129... | collective-permute-start | bytes 933896 | tf_op jit(solution)/shard_map/ppermute | solution.py:18
  36.8 0.2 collective-permute-done.8
  37.1 3.4 %collective-permute-start.12 = (bf16[64,2304]{1,0:T(8,128)(2,1)S(1)}, bf16[64,2304]{1,0:T(8,128)(2,1)S(1)}, u32[]{:S(2)}, u32[]{:S(2)}) collective-permute-start(bf16[64,2304]{1,0:T(8,128)(2,1)S(1)} %pad_maximum_fusion.1.refs_4_), channel_id=1, source_target_pairs={{0,16},{8,24},{16,0},{24,8},{1,17},{9,25},{17,1},{25,9},{2,18},{10... | collective-permute-start | bytes 884744 | tf_op jit(solution)/shard_map/ppermute | solution.py:18
  40.5 7.4 %collective-permute-done.5.refs_2_ = bf16[64,2432]{1,0:T(8,128)(2,1)S(1)} collective-permute-done((bf16[64,2432]{1,0:T(8,128)(2,1)S(1)}, bf16[64,2432]{1,0:T(8,128)(2,1)S(1)}, u32[]{:S(2)}, u32[]{:S(2)}) %collective-permute-start.5) | collective-permute-done | bytes 311328 | tf_op jit(solution)/shard_map/ppermute | solution.py:18
  47.9 1.7 %collective-permute-start.13 = (bf16[64,2304]{1,0:T(8,128)(2,1)S(1)}, bf16[64,2304]{1,0:T(8,128)(2,1)S(1)}, u32[]{:S(2)}, u32[]{:S(2)}) collective-permute-start(bf16[64,2304]{1,0:T(8,128)(2,1)S(1)} %pad_maximum_fusion.1.refs_4_), channel_id=1, source_target_pairs={{0,24},{8,0},{16,8},{24,16},{1,25},{9,1},{17,9},{25,17},{2,26},{10... | collective-permute-start | bytes 884744 | tf_op jit(solution)/shard_map/ppermute | solution.py:18
  49.8 0.3 collective-permute-start.7
  50.1 4.5 %collective-permute-done.13.refs_7_ = bf16[64,2304]{1,0:T(8,128)(2,1)S(1)} collective-permute-done((bf16[64,2304]{1,0:T(8,128)(2,1)S(1)}, bf16[64,2304]{1,0:T(8,128)(2,1)S(1)}, u32[]{:S(2)}, u32[]{:S(2)}) %collective-permute-start.13) | collective-permute-done | bytes 294944 | tf_op jit(solution)/shard_map/ppermute | solution.py:18
  54.6 10.4 %shard_map.68 = (f32[256,128]{1,0:T(8,128)S(1)}, f32[256,1000]{1,0:T(8,128)}, f32[256,1000]{1,0:T(8,128)}) custom-call(s32[34]{0:T(128)S(1)} %pad_add_fusion.where_ref, bf16[64,2432]{1,0:T(8,128)(2,1)S(1)} %pad_maximum_fusion.refs_0_, bf16[64,2432]{1,0:T(8,128)(2,1)S(1)} %collective-permute-done.4.refs_1_, bf16[64,2432]{1,0:T(8,128)(2,1)} %copy-done.3, ...), custom_call_target="tpu_custom_call" | custom-call | flops 4718592000 | bytes 23150592 | tf_op jit(solution)/shard_map/pallas_call | solution.py:80
  65.0 0.6 copy-done
  65.7 0.6 copy-done.6
  66.3 3.0 %shard_map.69 = (f32[8,256]{1,0:T(8,128)}, f32[512,128]{1,0:T(8,128)}) custom-call(s32[34]{0:T(128)} %copy-done.1, bf16[256,128]{1,0:T(8,128)(2,1)} %copy-done.5, bf16[256,128]{1,0:T(8,128)(2,1)} %copy-done.6, f32[256,128]{1,0:T(8,128)} %copy-done, f32[256,1000]{1,0:T(8,128)} %get-tuple-element.26.own_c, f32[256,1000]{1,0:T(8,128)} %get-tuple-element.27.sib_c), custom_call_target="tpu_custom_call" | custom-call | tf_op jit(solution)/shard_map/pallas_call | solution.py:129
  69.3 0.8 slice_reduce_fusion.1
  70.2 0.1 reduce_sum.47
  70.4 0.7 slice.83
  71.1 0.1 reduce_sum.46
  71.2 8.5 %all-to-all-start.1 = ((f32[128,4,128]{2,1,0:T(4,128)}), f32[128,4,128]{2,1,0:T(4,128)S(1)}, u32[]{:S(2)}, u32[]{:S(2)}) async-start(f32[128,4,128]{2,1,0:T(4,128)} %bitcast.20), calls=%async_computation.1 | async-start | bytes 524288 | tf_op jit(solution)/shard_map/all_to_all | solution.py:237
  79.7 0.8 fusion
  80.8 0.7 multiply_divide_fusion
  81.5 10.4 %all-to-all-done.1 = f32[128,4,128]{2,1,0:T(4,128)S(1)} async-done(((f32[128,4,128]{2,1,0:T(4,128)}), f32[128,4,128]{2,1,0:T(4,128)S(1)}, u32[]{:S(2)}, u32[]{:S(2)}) %all-to-all-start.1) | async-done | bytes 262176 | tf_op jit(solution)/shard_map/all_to_all | solution.py:237
  91.9 0.1 reduce_sum.45
  92.1 0.6 copy-done.2
  92.8 7.2 %shard_map.70 = (bf16[64,2304]{1,0:T(8,128)(2,1)S(1)}, bf16[64,2304]{1,0:T(8,128)(2,1)S(1)}, bf16[64,2304]{1,0:T(8,128)(2,1)S(1)}, bf16[64,2304]{1,0:T(8,128)(2,1)S(1)}) custom-call(s32[34]{0:T(128)S(1)} %copy-done.2, f32[8,256]{1,0:T(8,128)S(1)} %stack.46.rows_ref, f32[256,1000]{1,0:T(8,128)} %get-tuple-element.26.own_c, ...), custom_call_target="tpu_custom_call" | custom-call | flops 2359296000 | bytes 10395648 | tf_op jit(solution)/shard_map/pallas_call | solution.py:176
  100.0 0.8 collective-permute-start.14
  100.8 2.0 %collective-permute-start.15 = (bf16[64,2304]{1,0:T(8,128)(2,1)S(1)}, bf16[64,2304]{1,0:T(8,128)(2,1)S(1)}, u32[]{:S(2)}, u32[]{:S(2)}) collective-permute-start(bf16[64,2304]{1,0:T(8,128)(2,1)S(1)} %get-tuple-element.32), channel_id=1, source_target_pairs={{0,128},{64,192},{128,0},{192,64},{1,129},{65,193},{129,1},{193,65... | collective-permute-start | bytes 884744 | tf_op jit(solution)/shard_map/ppermute | solution.py:18
  102.8 0.3 collective-permute-start.16
  103.1 7.3 %shard_map.71 = (bf16[64,2304]{1,0:T(8,128)(2,1)S(1)}, bf16[64,2304]{1,0:T(8,128)(2,1)S(1)}, bf16[64,2304]{1,0:T(8,128)(2,1)S(1)}, bf16[64,2304]{1,0:T(8,128)(2,1)S(1)}) custom-call(s32[18]{0:T(128)S(1)} %pad_add_fusion.1.where_ref, f32[8,256]{1,0:T(8,128)S(1)} %stack.46.rows_ref, f32[256,1000]{1,0:T(8,128)} %get-tuple-element.26.own_c, ...), custom_call_target="tpu_custom_call" | custom-call | flops 2359296000 | bytes 10395648 | tf_op jit(solution)/shard_map/pallas_call | solution.py:176
  110.5 0.1 reduce_sum.49
  110.6 0.6 slice.96
  111.2 1.4 collective-permute-start.20
  112.5 1.0 collective-permute-start.21
  113.5 1.6 %collective-permute-start.22 = (bf16[64,2304]{1,0:T(8,128)(2,1)S(1)}, bf16[64,2304]{1,0:T(8,128)(2,1)S(1)}, u32[]{:S(2)}, u32[]{:S(2)}) collective-permute-start(bf16[64,2304]{1,0:T(8,128)(2,1)S(1)} %get-tuple-element.41), channel_id=1, source_target_pairs={{0,8},{8,16},{16,24},{24,0},{1,9},{9,17},{17,25},{25,1},{2,10},{10... | collective-permute-start | bytes 884744 | tf_op jit(solution)/shard_map/ppermute | solution.py:18
  115.2 0.1 add_convert_fusion.1
  115.3 0.8 collective-permute-start.17
  116.2 2.2 %collective-permute-start.18 = (bf16[16,2304]{1,0:T(8,128)(2,1)S(1)}, bf16[16,2304]{1,0:T(8,128)(2,1)S(1)}, u32[]{:S(2)}, u32[]{:S(2)}) collective-permute-start(bf16[16,2304]{1,0:T(8,128)(2,1)S(1)} %get-tuple-element.48), channel_id=1, source_target_pairs={{0,16},{8,24},{16,0},{24,8},{1,17},{9,25},{17,1},{25,9},{2,18},{10... | collective-permute-start | bytes 221192 | tf_op jit(solution)/shard_map/ppermute | solution.py:18
  118.4 2.2 %collective-permute-done.20 = bf16[64,2304]{1,0:T(8,128)(2,1)S(1)} collective-permute-done((bf16[64,2304]{1,0:T(8,128)(2,1)S(1)}, bf16[64,2304]{1,0:T(8,128)(2,1)S(1)}, u32[]{:S(2)}, u32[]{:S(2)}) %collective-permute-start.20) | collective-permute-done | bytes 294944 | tf_op jit(solution)/shard_map/ppermute | solution.py:18
  120.6 0.6 collective-permute-start.19
  121.2 2.7 %collective-permute-done.21 = bf16[64,2304]{1,0:T(8,128)(2,1)S(1)} collective-permute-done((bf16[64,2304]{1,0:T(8,128)(2,1)S(1)}, bf16[64,2304]{1,0:T(8,128)(2,1)S(1)}, u32[]{:S(2)}, u32[]{:S(2)}) %collective-permute-start.21) | collective-permute-done | bytes 294944 | tf_op jit(solution)/shard_map/ppermute | solution.py:18
  123.9 1.4 collective-permute-done.22
  125.3 0.2 add_convert_fusion
  125.5 2.8 %collective-permute-start.23 = (bf16[16,2304]{1,0:T(8,128)(2,1)S(1)}, bf16[16,2304]{1,0:T(8,128)(2,1)S(1)}, u32[]{:S(2)}, u32[]{:S(2)}) collective-permute-start(bf16[16,2304]{1,0:T(8,128)(2,1)S(1)} %get-tuple-element.49), channel_id=1, source_target_pairs={{0,192},{64,0},{128,64},{192,128},{1,193},{65,1},{129,65},{193,129... | collective-permute-start | bytes 221192 | tf_op jit(solution)/shard_map/ppermute | solution.py:18
  128.2 0.4 collective-permute-start.24
  128.7 1.2 collective-permute-start.25
  130.0 0.3 collective-permute-done.23
  130.2 3.9 %collective-permute-done.24 = bf16[16,2304]{1,0:T(8,128)(2,1)S(1)} collective-permute-done((bf16[16,2304]{1,0:T(8,128)(2,1)S(1)}, bf16[16,2304]{1,0:T(8,128)(2,1)S(1)}, u32[]{:S(2)}, u32[]{:S(2)}) %collective-permute-start.24) | collective-permute-done | bytes 73760 | tf_op jit(solution)/shard_map/ppermute | solution.py:18
  134.2 0.7 collective-permute-done.25
  135.0 0.7 reshape.109
  135.7 3.4 %all-to-all-start.2 = ((bf16[8,2,4608]{2,1,0:T(2,128)(2,1)}), bf16[8,2,4608]{2,1,0:T(2,128)(2,1)S(1)}, u32[]{:S(2)}, u32[]{:S(2)}) async-start(bf16[8,2,4608]{2,1,0:T(2,128)(2,1)} %reshape.109), calls=%async_computation.2 | async-start | bytes 294912 | tf_op jit(solution)/shard_map/all_to_all | solution.py:265
  139.1 0.7 broadcast_select_fusion
  139.8 1.1 collective-permute-done.26
  140.9 0.5 add_divide_fusion
  141.4 6.8 %all-to-all-done.2 = bf16[8,2,4608]{2,1,0:T(2,128)(2,1)S(1)} async-done(((bf16[8,2,4608]{2,1,0:T(2,128)(2,1)}), bf16[8,2,4608]{2,1,0:T(2,128)(2,1)S(1)}, u32[]{:S(2)}, u32[]{:S(2)}) %all-to-all-start.2) | async-done | bytes 147488 | tf_op jit(solution)/shard_map/all_to_all | solution.py:265
  148.2 0.7 convert_reduce_fusion
  (72 shorter events, 1.9 us)
Async XLA Ops:
  0.6 21.2 %collective-permute-start = (bf16[1000,4608]{1,0:T(8,128)(2,1)}, bf16[1000,4608]{1,0:T(8,128)(2,1)}, u32[]{:S(2)}, u32[]{:S(2)}) collective-permute-start(bf16[1000,4608]{1,0:T(8,128)(2,1)} %own_ref.3), channel_id=1, source_target_pairs={{0,32},{32,0},{1,33},{33,1},{2,34},{34,2},{3,35},{35,3},{4,36},{36... | collective-permute-start | bytes 27648008 | tf_op jit(solution)/shard_map/ppermute | solution.py:209
  3.2 18.6 %all-to-all-start = ((bf16[8,2,4736]{2,1,0:T(2,128)(2,1)}), bf16[8,2,4736]{2,1,0:T(2,128)(2,1)S(1)}, u32[]{:S(2)}, u32[]{:S(2)}) async-start(bf16[8,2,4736]{2,1,0:T(2,128)(2,1)} %pad_maximum_fusion.2), calls=%async_computation | async-start | bytes 303104 | tf_op jit(solution)/shard_map/all_to_all | solution.py:215
  21.9 7.9 %collective-permute-start.1 = (bf16[16,2432]{1,0:T(8,128)(2,1)S(1)}, bf16[16,2432]{1,0:T(8,128)(2,1)S(1)}, u32[]{:S(2)}, u32[]{:S(2)}) collective-permute-start(bf16[16,2432]{1,0:T(8,128)(2,1)S(1)} %slice.75), channel_id=1, source_target_pairs={{0,8},{8,16},{16,24},{24,0},{1,9},{9,17},{17,25},{25,1},{2,10},{10... | collective-permute-start | bytes 233480 | tf_op jit(solution)/shard_map/ppermute | solution.py:18
  23.6 8.5 %collective-permute-start.2 = (bf16[16,2432]{1,0:T(8,128)(2,1)S(1)}, bf16[16,2432]{1,0:T(8,128)(2,1)S(1)}, u32[]{:S(2)}, u32[]{:S(2)}) collective-permute-start(bf16[16,2432]{1,0:T(8,128)(2,1)S(1)} %slice.75), channel_id=1, source_target_pairs={{0,16},{8,24},{16,0},{24,8},{1,17},{9,25},{17,1},{25,9},{2,18},{10... | collective-permute-start | bytes 233480 | tf_op jit(solution)/shard_map/ppermute | solution.py:18
  24.5 7.6 %collective-permute-start.3 = (bf16[16,2432]{1,0:T(8,128)(2,1)S(1)}, bf16[16,2432]{1,0:T(8,128)(2,1)S(1)}, u32[]{:S(2)}, u32[]{:S(2)}) collective-permute-start(bf16[16,2432]{1,0:T(8,128)(2,1)S(1)} %slice.75), channel_id=1, source_target_pairs={{0,24},{8,0},{16,8},{24,16},{1,25},{9,1},{17,9},{25,17},{2,26},{10... | collective-permute-start | bytes 233480 | tf_op jit(solution)/shard_map/ppermute | solution.py:18
  27.0 7.8 %collective-permute-start.10 = (bf16[16,2304]{1,0:T(8,128)(2,1)S(1)}, bf16[16,2304]{1,0:T(8,128)(2,1)S(1)}, u32[]{:S(2)}, u32[]{:S(2)}) collective-permute-start(bf16[16,2304]{1,0:T(8,128)(2,1)S(1)} %slice.80), channel_id=1, source_target_pairs={{0,192},{64,0},{128,64},{192,128},{1,193},{65,1},{129,65},{193,129... | collective-permute-start | bytes 221192 | tf_op jit(solution)/shard_map/ppermute | solution.py:18
  29.8 7.2 %collective-permute-start.8 = (bf16[16,2304]{1,0:T(8,128)(2,1)S(1)}, bf16[16,2304]{1,0:T(8,128)(2,1)S(1)}, u32[]{:S(2)}, u32[]{:S(2)}) collective-permute-start(bf16[16,2304]{1,0:T(8,128)(2,1)S(1)} %slice.80), channel_id=1, source_target_pairs={{0,64},{64,128},{128,192},{192,0},{1,65},{65,129},{129,193},{193,1... | collective-permute-start | bytes 221192 | tf_op jit(solution)/shard_map/ppermute | solution.py:18
  29.8 7.2 %collective-permute-start.9 = (bf16[16,2304]{1,0:T(8,128)(2,1)S(1)}, bf16[16,2304]{1,0:T(8,128)(2,1)S(1)}, u32[]{:S(2)}, u32[]{:S(2)}) collective-permute-start(bf16[16,2304]{1,0:T(8,128)(2,1)S(1)} %slice.80), channel_id=1, source_target_pairs={{0,128},{64,192},{128,0},{192,64},{1,129},{65,193},{129,1},{193,65... | collective-permute-start | bytes 221192 | tf_op jit(solution)/shard_map/ppermute | solution.py:18
  32.1 17.6 %collective-permute-start.4 = (bf16[64,2432]{1,0:T(8,128)(2,1)S(1)}, bf16[64,2432]{1,0:T(8,128)(2,1)S(1)}, u32[]{:S(2)}, u32[]{:S(2)}) collective-permute-start(bf16[64,2432]{1,0:T(8,128)(2,1)S(1)} %pad_maximum_fusion.refs_0_), channel_id=1, source_target_pairs={{0,64},{64,128},{128,192},{192,0},{1,65},{65,129},{129,193},{193,1... | collective-permute-start | bytes 933896 | tf_op jit(solution)/shard_map/ppermute | solution.py:18
  34.0 13.8 %collective-permute-start.5 = (bf16[64,2432]{1,0:T(8,128)(2,1)S(1)}, bf16[64,2432]{1,0:T(8,128)(2,1)S(1)}, u32[]{:S(2)}, u32[]{:S(2)}) collective-permute-start(bf16[64,2432]{1,0:T(8,128)(2,1)S(1)} %pad_maximum_fusion.refs_0_), channel_id=1, source_target_pairs={{0,128},{64,192},{128,0},{192,64},{1,129},{65,193},{129,1},{193,65... | collective-permute-start | bytes 933896 | tf_op jit(solution)/shard_map/ppermute | solution.py:18
  34.8 14.9 %collective-permute-start.6 = (bf16[64,2432]{1,0:T(8,128)(2,1)S(1)}, bf16[64,2432]{1,0:T(8,128)(2,1)S(1)}, u32[]{:S(2)}, u32[]{:S(2)}) collective-permute-start(bf16[64,2432]{1,0:T(8,128)(2,1)S(1)} %pad_maximum_fusion.refs_0_), channel_id=1, source_target_pairs={{0,192},{64,0},{128,64},{192,128},{1,193},{65,1},{129,65},{193,129... | collective-permute-start | bytes 933896 | tf_op jit(solution)/shard_map/ppermute | solution.py:18
  37.0 13.1 %collective-permute-start.11 = (bf16[64,2304]{1,0:T(8,128)(2,1)S(1)}, bf16[64,2304]{1,0:T(8,128)(2,1)S(1)}, u32[]{:S(2)}, u32[]{:S(2)}) collective-permute-start(bf16[64,2304]{1,0:T(8,128)(2,1)S(1)} %pad_maximum_fusion.1.refs_4_), channel_id=1, source_target_pairs={{0,8},{8,16},{16,24},{24,0},{1,9},{9,17},{17,25},{25,1},{2,10},{10... | collective-permute-start | bytes 884744 | tf_op jit(solution)/shard_map/ppermute | solution.py:18
  37.1 13.0 %collective-permute-start.12 = (bf16[64,2304]{1,0:T(8,128)(2,1)S(1)}, bf16[64,2304]{1,0:T(8,128)(2,1)S(1)}, u32[]{:S(2)}, u32[]{:S(2)}) collective-permute-start(bf16[64,2304]{1,0:T(8,128)(2,1)S(1)} %pad_maximum_fusion.1.refs_4_), channel_id=1, source_target_pairs={{0,16},{8,24},{16,0},{24,8},{1,17},{9,25},{17,1},{25,9},{2,18},{10... | collective-permute-start | bytes 884744 | tf_op jit(solution)/shard_map/ppermute | solution.py:18
  47.9 6.7 %copy-start.3 = (bf16[64,2432]{1,0:T(8,128)(2,1)}, bf16[64,2432]{1,0:T(8,128)(2,1)S(1)}, u32[]{:S(2)}) copy-start(bf16[64,2432]{1,0:T(8,128)(2,1)S(1)} %collective-permute-done.5.refs_2_) | copy-start | bytes 933892
  47.9 6.7 %collective-permute-start.13 = (bf16[64,2304]{1,0:T(8,128)(2,1)S(1)}, bf16[64,2304]{1,0:T(8,128)(2,1)S(1)}, u32[]{:S(2)}, u32[]{:S(2)}) collective-permute-start(bf16[64,2304]{1,0:T(8,128)(2,1)S(1)} %pad_maximum_fusion.1.refs_4_), channel_id=1, source_target_pairs={{0,24},{8,0},{16,8},{24,16},{1,25},{9,1},{17,9},{25,17},{2,26},{10... | collective-permute-start | bytes 884744 | tf_op jit(solution)/shard_map/ppermute | solution.py:18
  49.7 15.3 %copy-start.1 = (s32[34]{0:T(128)}, s32[34]{0:T(128)S(1)}, u32[]{:S(2)}) copy-start(s32[34]{0:T(128)S(1)} %pad_add_fusion.where_ref) | copy-start | bytes 412
  49.8 4.8 %copy-start.4 = (bf16[64,2432]{1,0:T(8,128)(2,1)}, bf16[64,2432]{1,0:T(8,128)(2,1)S(1)}, u32[]{:S(2)}) copy-start(bf16[64,2432]{1,0:T(8,128)(2,1)S(1)} %collective-permute-done.6.refs_3_) | copy-start | bytes 933892
  49.8 15.2 %copy-start.5 = (bf16[256,128]{1,0:T(8,128)(2,1)}, bf16[256,128]{1,0:T(8,128)(2,1)S(1)}, u32[]{:S(2)}) copy-start(bf16[256,128]{1,0:T(8,128)(2,1)S(1)} %pad_maximum_fusion.4.own_ref) | copy-start | bytes 196612
  49.8 15.9 %collective-permute-start.7 = (bf16[256,128]{1,0:T(8,128)(2,1)S(1)}, bf16[256,128]{1,0:T(8,128)(2,1)S(1)}, u32[]{:S(2)}, u32[]{:S(2)}) collective-permute-start(bf16[256,128]{1,0:T(8,128)(2,1)S(1)} %pad_maximum_fusion.4.own_ref), channel_id=1, source_target_pairs={{0,32},{32,0},{1,33},{33,1},{2,34},{34,2},{3,35},{35,3},{4,36},{36... | collective-permute-start | bytes 196616 | tf_op jit(solution)/shard_map/ppermute | solution.py:224
  65.0 0.6 copy-start
  65.7 0.6 copy-start.6
  71.2 20.7 %all-to-all-start.1 = ((f32[128,4,128]{2,1,0:T(4,128)}), f32[128,4,128]{2,1,0:T(4,128)S(1)}, u32[]{:S(2)}, u32[]{:S(2)}) async-start(f32[128,4,128]{2,1,0:T(4,128)} %bitcast.20), calls=%async_computation.1 | async-start | bytes 524288 | tf_op jit(solution)/shard_map/all_to_all | solution.py:237
  92.1 0.7 copy-start.2
  100.0 13.5 %collective-permute-start.14 = (bf16[64,2304]{1,0:T(8,128)(2,1)S(1)}, bf16[64,2304]{1,0:T(8,128)(2,1)S(1)}, u32[]{:S(2)}, u32[]{:S(2)}) collective-permute-start(bf16[64,2304]{1,0:T(8,128)(2,1)S(1)} %get-tuple-element.31), channel_id=1, source_target_pairs={{0,192},{64,0},{128,64},{192,128},{1,193},{65,1},{129,65},{193,129... | collective-permute-start | bytes 884744 | tf_op jit(solution)/shard_map/ppermute | solution.py:18
  100.8 14.4 %collective-permute-start.15 = (bf16[64,2304]{1,0:T(8,128)(2,1)S(1)}, bf16[64,2304]{1,0:T(8,128)(2,1)S(1)}, u32[]{:S(2)}, u32[]{:S(2)}) collective-permute-start(bf16[64,2304]{1,0:T(8,128)(2,1)S(1)} %get-tuple-element.32), channel_id=1, source_target_pairs={{0,128},{64,192},{128,0},{192,64},{1,129},{65,193},{129,1},{193,65... | collective-permute-start | bytes 884744 | tf_op jit(solution)/shard_map/ppermute | solution.py:18
  102.8 12.4 %collective-permute-start.16 = (bf16[64,2304]{1,0:T(8,128)(2,1)S(1)}, bf16[64,2304]{1,0:T(8,128)(2,1)S(1)}, u32[]{:S(2)}, u32[]{:S(2)}) collective-permute-start(bf16[64,2304]{1,0:T(8,128)(2,1)S(1)} %get-tuple-element.33), channel_id=1, source_target_pairs={{0,64},{64,128},{128,192},{192,0},{1,65},{65,129},{129,193},{193,1... | collective-permute-start | bytes 884744 | tf_op jit(solution)/shard_map/ppermute | solution.py:18
  111.2 9.4 %collective-permute-start.20 = (bf16[64,2304]{1,0:T(8,128)(2,1)S(1)}, bf16[64,2304]{1,0:T(8,128)(2,1)S(1)}, u32[]{:S(2)}, u32[]{:S(2)}) collective-permute-start(bf16[64,2304]{1,0:T(8,128)(2,1)S(1)} %get-tuple-element.39), channel_id=1, source_target_pairs={{0,24},{8,0},{16,8},{24,16},{1,25},{9,1},{17,9},{25,17},{2,26},{10... | collective-permute-start | bytes 884744 | tf_op jit(solution)/shard_map/ppermute | solution.py:18
  112.5 11.3 %collective-permute-start.21 = (bf16[64,2304]{1,0:T(8,128)(2,1)S(1)}, bf16[64,2304]{1,0:T(8,128)(2,1)S(1)}, u32[]{:S(2)}, u32[]{:S(2)}) collective-permute-start(bf16[64,2304]{1,0:T(8,128)(2,1)S(1)} %get-tuple-element.40), channel_id=1, source_target_pairs={{0,16},{8,24},{16,0},{24,8},{1,17},{9,25},{17,1},{25,9},{2,18},{10... | collective-permute-start | bytes 884744 | tf_op jit(solution)/shard_map/ppermute | solution.py:18
  113.5 11.7 %collective-permute-start.22 = (bf16[64,2304]{1,0:T(8,128)(2,1)S(1)}, bf16[64,2304]{1,0:T(8,128)(2,1)S(1)}, u32[]{:S(2)}, u32[]{:S(2)}) collective-permute-start(bf16[64,2304]{1,0:T(8,128)(2,1)S(1)} %get-tuple-element.41), channel_id=1, source_target_pairs={{0,8},{8,16},{16,24},{24,0},{1,9},{9,17},{17,25},{25,1},{2,10},{10... | collective-permute-start | bytes 884744 | tf_op jit(solution)/shard_map/ppermute | solution.py:18
  115.3 13.3 %collective-permute-start.17 = (bf16[16,2304]{1,0:T(8,128)(2,1)S(1)}, bf16[16,2304]{1,0:T(8,128)(2,1)S(1)}, u32[]{:S(2)}, u32[]{:S(2)}) collective-permute-start(bf16[16,2304]{1,0:T(8,128)(2,1)S(1)} %get-tuple-element.46), channel_id=1, source_target_pairs={{0,24},{8,0},{16,8},{24,16},{1,25},{9,1},{17,9},{25,17},{2,26},{10... | collective-permute-start | bytes 221192 | tf_op jit(solution)/shard_map/ppermute | solution.py:18
  116.2 13.7 %collective-permute-start.18 = (bf16[16,2304]{1,0:T(8,128)(2,1)S(1)}, bf16[16,2304]{1,0:T(8,128)(2,1)S(1)}, u32[]{:S(2)}, u32[]{:S(2)}) collective-permute-start(bf16[16,2304]{1,0:T(8,128)(2,1)S(1)} %get-tuple-element.48), channel_id=1, source_target_pairs={{0,16},{8,24},{16,0},{24,8},{1,17},{9,25},{17,1},{25,9},{2,18},{10... | collective-permute-start | bytes 221192 | tf_op jit(solution)/shard_map/ppermute | solution.py:18
  120.6 9.3 %collective-permute-start.19 = (bf16[16,2304]{1,0:T(8,128)(2,1)S(1)}, bf16[16,2304]{1,0:T(8,128)(2,1)S(1)}, u32[]{:S(2)}, u32[]{:S(2)}) collective-permute-start(bf16[16,2304]{1,0:T(8,128)(2,1)S(1)} %get-tuple-element.47), channel_id=1, source_target_pairs={{0,8},{8,16},{16,24},{24,0},{1,9},{9,17},{17,25},{25,1},{2,10},{10... | collective-permute-start | bytes 221192 | tf_op jit(solution)/shard_map/ppermute | solution.py:18
  125.5 4.8 %collective-permute-start.23 = (bf16[16,2304]{1,0:T(8,128)(2,1)S(1)}, bf16[16,2304]{1,0:T(8,128)(2,1)S(1)}, u32[]{:S(2)}, u32[]{:S(2)}) collective-permute-start(bf16[16,2304]{1,0:T(8,128)(2,1)S(1)} %get-tuple-element.49), channel_id=1, source_target_pairs={{0,192},{64,0},{128,64},{192,128},{1,193},{65,1},{129,65},{193,129... | collective-permute-start | bytes 221192 | tf_op jit(solution)/shard_map/ppermute | solution.py:18
  128.2 5.9 %collective-permute-start.24 = (bf16[16,2304]{1,0:T(8,128)(2,1)S(1)}, bf16[16,2304]{1,0:T(8,128)(2,1)S(1)}, u32[]{:S(2)}, u32[]{:S(2)}) collective-permute-start(bf16[16,2304]{1,0:T(8,128)(2,1)S(1)} %get-tuple-element.51), channel_id=1, source_target_pairs={{0,128},{64,192},{128,0},{192,64},{1,129},{65,193},{129,1},{193,65... | collective-permute-start | bytes 221192 | tf_op jit(solution)/shard_map/ppermute | solution.py:18
  128.7 6.2 %collective-permute-start.25 = (bf16[16,2304]{1,0:T(8,128)(2,1)S(1)}, bf16[16,2304]{1,0:T(8,128)(2,1)S(1)}, u32[]{:S(2)}, u32[]{:S(2)}) collective-permute-start(bf16[16,2304]{1,0:T(8,128)(2,1)S(1)} %get-tuple-element.50), channel_id=1, source_target_pairs={{0,64},{64,128},{128,192},{192,0},{1,65},{65,129},{129,193},{193,1... | collective-permute-start | bytes 221192 | tf_op jit(solution)/shard_map/ppermute | solution.py:18
  135.7 12.6 %all-to-all-start.2 = ((bf16[8,2,4608]{2,1,0:T(2,128)(2,1)}), bf16[8,2,4608]{2,1,0:T(2,128)(2,1)S(1)}, u32[]{:S(2)}, u32[]{:S(2)}) async-start(bf16[8,2,4608]{2,1,0:T(2,128)(2,1)} %reshape.109), calls=%async_computation.2 | async-start | bytes 294912 | tf_op jit(solution)/shard_map/all_to_all | solution.py:265
  139.8 1.1 collective-permute-start.26
